TPU v7x, 32 devices: a whole 2x2x4 slice. The times are simulated.
32 devices in a mesh: batch: 2 (over y), res: 16 (over z, x, core), head: 1.
Axes of the slice: x: 2, y: 2, z: 4, core: 2. Of those that a mesh axis runs over, the one named last changes fastest.
Arguments:
- single: bfloat16 [768, 384], P(('batch', 'res')), parts along dimension 0, may hold values from -50 to 50
- pair: bfloat16 [768, 384, 128], P(('batch', 'res'), 'head'), parts along dimension 0, may hold values from -6 to 6
- rotations: float32 [3, 3, 768], P(None, None, 'batch'), parts along dimension 2, may hold values from -1 to 1, as said below
- translations: float32 [3, 768], P(None, 'batch'), parts along dimension 1, may hold values from -4 to 4
- residue_chain_index: int32 [384], replicated, may hold values from 0 to 3, never falling along the last dimension, each value on 1 to 192 neighbouring positions
- residue_move_mask: int32 [768], P('batch'), parts along dimension 0, may hold values 0 or 1
- timestep: int32 [1], replicated, may hold values from 0 to 6
- single_projection_weight: bfloat16 [384, 16, 132], P(None, 'head'), may hold values from -1 to 1, as said below
- head_bias_weight: bfloat16 [128, 16], replicated, may hold values from -0.5 to 0.5
- head_distance_weight: float32 [16], P('head'), may hold values from 0.1 to 1
- chain_logit_offset: float32 [16], P('head'), may hold values from -2 to 2
- local_output_weight: bfloat16 [16, 64, 384], P('head'), may hold values from -0.109375 to 0.109375
- pair_output_weight: bfloat16 [16, 128, 384], replicated, may hold values from -0.109375 to 0.109375
- single_norm_gain: float32 [384], replicated, may hold values from 0.5 to 1.5
- frame_velocity_weight: bfloat16 [384, 6], replicated, may hold values from -0.3125 to 0.3125
- left_pair_weight: bfloat16 [384, 128], replicated, may hold values from -0.3125 to 0.3125
- right_pair_weight: bfloat16 [384, 128], replicated, may hold values from -0.3125 to 0.3125
- pair_norm_gain: float32 [128], replicated, may hold values from 0.5 to 1.5
- transition_hidden_weight: bfloat16 [128, 256], replicated, may hold values from -0.5 to 0.5
- transition_middle_weight: bfloat16 [256, 256], replicated, may hold values from -0.375 to 0.375
- transition_back_weight: bfloat16 [256, 128], replicated, may hold values from -0.375 to 0.375
Outputs:
- single_out: bfloat16 [768, 384], P(('batch', 'res')), parts along dimension 0
- rot_out: float32 [3, 3, 768], P(None, None, ('batch', 'res')), parts along dimension 2
- trans_out: float32 [3, 768], P(None, ('batch', 'res')), parts along dimension 1
- pair_out: bfloat16 [768, 384, 128], P(('batch', 'res'), 'head'), parts along dimension 0
There are 2 independent parts, one for each index of `batch`. A program takes and returns all parts, laid end to end along the dimension named above; an argument that names none is the same for every part. Nothing has to cross between parts.
Inputs may be any that keep to these rules, and one draw needn't show every extreme that they name: Each residue's 3 x 3 block rotations[:, :, i] is a rotation matrix. `single_projection_weight`: mean zero entries of deviation about 1 / sqrt(384).
All inputs are finite; a program needn't handle non-finite values.
Results may differ from a plain program's by a relative error of at most 0.0044.
The roundings to bfloat16 on the way count: a program that leaves them out, or rounds other values in their place, can miss the bound.
Values may be sent and summed in bfloat16 or wider, within the bound.
No kernel may reach another device: no remote copies, remote signals or barrier semaphores. Data moves between devices by JAX's collectives and lax.ppermute only.
A program may use at most 64 MiB of HBM per device.

v0:
```python
import math

import jax
import jax.numpy as jnp
from jax import lax
from jax.sharding import PartitionSpec as P

HEAD_FEATURES = 16
PQ = 8
PV = 12
STEPS = 8


LOGIT_FACTOR = math.sqrt(1.0 / 3.0)
HIGHEST = lax.Precision.HIGHEST


def rounded(values):
    return lax.optimization_barrier(values.astype(jnp.bfloat16))


def layer_norm(values, gain):
    centre = jnp.mean(values, axis=-1, keepdims=True)
    variance = jnp.mean(jnp.square(values - centre), axis=-1, keepdims=True)
    return (values - centre) * lax.rsqrt(variance + 1e-05) * gain


def to_global(local, rot_cols, trans_cols, npoints):
    rows_here = local.shape[0]
    heads_here = local.shape[1]
    points = local.reshape(rows_here, heads_here, npoints, 3)
    turned = jnp.sum(rot_cols[:, None, None, :, :] * points[:, :, :, None, :], axis=-1)
    return turned + trans_cols[:, None, None, :]


def key_features(projected, rot_cols, trans_cols):
    rows_here = projected.shape[0]
    heads_here = projected.shape[1]
    offset = 3 * HEAD_FEATURES
    key_points = to_global(
        projected[:, :, offset + 3 * PQ : offset + 6 * PQ], rot_cols, trans_cols, PQ
    )
    value_points = to_global(projected[:, :, offset + 6 * PQ :], rot_cols, trans_cols, PV)
    packed_projection = jnp.concatenate(
        [
            projected[:, :, HEAD_FEATURES : 3 * HEAD_FEATURES],
            key_points.reshape(rows_here, heads_here, 3 * PQ),
            value_points.reshape(rows_here, heads_here, 3 * PV),
        ],
        axis=-1,
    )
    return rounded(
        packed_projection.reshape(rows_here, heads_here * (2 * HEAD_FEATURES + 3 * PQ + 3 * PV))
    )


def hat_matrix(vectors):
    comp_x = vectors[:, 0]
    comp_y = vectors[:, 1]
    comp_z = vectors[:, 2]
    zeros_col = jnp.zeros_like(comp_x)
    first_row = jnp.stack([zeros_col, -comp_z, comp_y], -1)
    second_row = jnp.stack([comp_z, zeros_col, -comp_x], -1)
    third_row = jnp.stack([-comp_y, comp_x, zeros_col], -1)
    return jnp.stack([first_row, second_row, third_row], 1)


def frame_step(single_out, frame_velocity_weight, rot_cols, trans_cols, live_rows, step_ratio):
    motion = jnp.dot(single_out, frame_velocity_weight, preferred_element_type=jnp.float32)
    rotvec = step_ratio * jnp.tanh(motion[:, 0:3]) * live_rows[:, None]
    velocity = step_ratio * motion[:, 3:6] * live_rows[:, None]
    angle_sq = jnp.sum(jnp.square(rotvec), -1)
    coef_a = jnp.zeros_like(angle_sq)
    coef_b = jnp.zeros_like(angle_sq)
    coef_c = jnp.zeros_like(angle_sq)
    powers = jnp.ones_like(angle_sq)
    for order in range(8):
        parity = (-1.0) ** order
        coef_a = coef_a + powers * (parity / float(math.factorial(2 * order + 1)))
        coef_b = coef_b + powers * (parity / float(math.factorial(2 * order + 2)))
        coef_c = coef_c + powers * (parity / float(math.factorial(2 * order + 3)))
        powers = powers * angle_sq
    cross_mat = hat_matrix(rotvec)
    cross_sq = jnp.einsum("nab,nbc->nac", cross_mat, cross_mat, precision=HIGHEST)
    identity = jnp.eye(3, dtype=jnp.float32)[None]
    turn = identity + coef_a[:, None, None] * cross_mat + coef_b[:, None, None] * cross_sq
    jacobian = identity + coef_b[:, None, None] * cross_mat + coef_c[:, None, None] * cross_sq
    new_rot = jnp.einsum("nab,nbc->nac", rot_cols, turn, precision=HIGHEST)
    moved = jnp.einsum("nab,nb->na", jacobian, velocity, precision=HIGHEST)
    new_trans = trans_cols + jnp.einsum("nab,nb->na", rot_cols, moved, precision=HIGHEST)
    return (jnp.transpose(new_rot, (1, 2, 0)), jnp.transpose(new_trans))


def local_logit_rows(
    query_values,
    query_flattened,
    packed_projection,
    pair_head_bias,
    within_chain,
    distance_weight,
    chain_offset,
    key_present,
):
    key_scalar = packed_projection[:, :, 0:HEAD_FEATURES]
    key_flat = packed_projection[:, :, 2 * HEAD_FEATURES : 2 * HEAD_FEATURES + 3 * PQ].astype(
        jnp.float32
    )
    scalar_logit_term = jnp.einsum(
        "rhc,nhc->rhn", query_values, key_scalar, preferred_element_type=jnp.float32
    )
    cross_term = jnp.einsum("rhp,nhp->rhn", query_flattened, key_flat, precision=HIGHEST)
    key_square = jnp.transpose(jnp.sum(jnp.square(key_flat), -1))
    point_distance = (
        jnp.sum(jnp.square(query_flattened), -1)[:, :, None] + key_square[None] - 2.0 * cross_term
    )
    point_term_weight = math.sqrt(2.0 / (9.0 * PQ))
    logit_matrix = LOGIT_FACTOR * (
        scalar_logit_term / math.sqrt(HEAD_FEATURES)
        + pair_head_bias
        + chain_offset[None, :, None] * within_chain[:, None, :]
        - (0.5 * point_term_weight * distance_weight)[None, :, None] * point_distance
    )
    return jnp.where(key_present[None, None, :], logit_matrix, -1000000000.0)


def local_points(scalar_out, point_global, rot_own, trans_own, local_output_weight):
    rows_dev = scalar_out.shape[0]
    heads_here = scalar_out.shape[1]
    point_global = point_global.reshape(rows_dev, heads_here, PV, 3)
    centred = point_global - trans_own[:, None, None, :]
    point_local = jnp.sum(rot_own[:, None, None, :, :] * centred[:, :, :, :, None], axis=-2)
    point_norm = jnp.sqrt(jnp.sum(jnp.square(point_local), -1) + 1.0)
    features = jnp.concatenate(
        [scalar_out, point_local.reshape(rows_dev, heads_here, 3 * PV), point_norm], -1
    )
    return jnp.einsum(
        "rhf,hfd->rd", features, local_output_weight.astype(jnp.float32), precision=HIGHEST
    )


def shards(
    single,
    pair,
    rotations,
    translations,
    residue_chain_index,
    residue_move_mask,
    timestep,
    single_projection_weight,
    head_bias_weight,
    head_distance_weight,
    chain_logit_offset,
    local_output_weight,
    pair_output_weight,
    single_norm_gain,
    frame_velocity_weight,
    left_pair_weight,
    right_pair_weight,
    pair_norm_gain,
    transition_hidden_weight,
    transition_middle_weight,
    transition_back_weight,
):
    rows_dev = single.shape[0]
    col_count = pair.shape[1]
    total = rotations.shape[2]
    heads_here = single_projection_weight.shape[1]
    row_start = lax.axis_index("res") * rows_dev
    col_start = lax.axis_index("head") * col_count
    rot_all = jnp.transpose(rotations, (2, 0, 1))
    trans_all = jnp.transpose(translations)
    rot_own = lax.dynamic_slice_in_dim(rot_all, row_start, rows_dev, 0)
    trans_own = lax.dynamic_slice_in_dim(trans_all, row_start, rows_dev, 0)
    own_chain = lax.dynamic_slice_in_dim(residue_chain_index, row_start, rows_dev, 0)
    offset = 3 * HEAD_FEATURES
    feat_count = 2 * HEAD_FEATURES + 3 * PQ + 3 * PV
    every_single = lax.all_gather(single, "res", axis=0, tiled=True)
    every_proj = jnp.einsum(
        "nd,dhf->nhf", every_single, single_projection_weight, preferred_element_type=jnp.float32
    )
    projected = lax.dynamic_slice_in_dim(every_proj, row_start, rows_dev, 0)
    packed_projection = key_features(every_proj, rot_all, trans_all)
    packed_projection = packed_projection.reshape(total, heads_here, feat_count)
    query_values = projected[:, :, 0:HEAD_FEATURES].astype(jnp.bfloat16)
    query_flattened = to_global(
        projected[:, :, offset : offset + 3 * PQ], rot_own, trans_own, PQ
    ).reshape(rows_dev, heads_here, 3 * PQ)
    bias_local = jnp.einsum(
        "rjc,ch->rhj", pair, head_bias_weight, preferred_element_type=jnp.float32
    ).astype(jnp.bfloat16)
    pair_head_bias = lax.all_to_all(
        bias_local, "head", split_axis=1, concat_axis=2, tiled=True
    ).astype(jnp.float32)
    within_chain = (own_chain[:, None] == residue_chain_index[None, :]).astype(jnp.float32)
    logit_matrix = local_logit_rows(
        query_values,
        query_flattened,
        packed_projection,
        pair_head_bias,
        within_chain,
        head_distance_weight,
        chain_logit_offset,
        residue_move_mask > 0,
    )
    peak = jnp.max(logit_matrix, axis=-1, keepdims=True)
    exponent = jnp.exp(logit_matrix - peak)
    attention = rounded(exponent / jnp.sum(exponent, axis=-1, keepdims=True))
    scalar_out = jnp.einsum(
        "rhn,nhc->rhc",
        attention,
        packed_projection[:, :, HEAD_FEATURES : 2 * HEAD_FEATURES],
        preferred_element_type=jnp.float32,
    )
    point_global = jnp.einsum(
        "rhn,nhp->rhp",
        attention.astype(jnp.float32),
        packed_projection[:, :, 2 * HEAD_FEATURES + 3 * PQ :].astype(jnp.float32),
        precision=HIGHEST,
    )
    update_local = local_points(scalar_out, point_global, rot_own, trans_own, local_output_weight)
    attention_cols = lax.all_to_all(attention, "head", split_axis=2, concat_axis=1, tiled=True)
    pair_attended = jnp.einsum(
        "rhj,rjc->rhc", attention_cols, pair, preferred_element_type=jnp.float32
    )
    update_pair = jnp.einsum(
        "rhc,hcd->rd", pair_attended, pair_output_weight.astype(jnp.float32), precision=HIGHEST
    )
    update = lax.psum(update_local + update_pair, "head")
    single_out = layer_norm(single.astype(jnp.float32) + update, single_norm_gain).astype(
        jnp.bfloat16
    )
    live_all = (residue_move_mask > 0).astype(jnp.float32)
    live_own = lax.dynamic_slice_in_dim(live_all, row_start, rows_dev, 0)
    live_cols = lax.dynamic_slice_in_dim(live_all, col_start, col_count, 0)
    step_ratio = 1.0 / (STEPS - timestep[0]).astype(jnp.float32)
    rot_out, trans_out = frame_step(
        single_out, frame_velocity_weight, rot_own, trans_own, live_own, step_ratio
    )
    left_proj = jnp.dot(single_out, left_pair_weight, preferred_element_type=jnp.float32).astype(
        jnp.bfloat16
    )
    every_new = lax.all_gather(single_out, "res", axis=0, tiled=True)
    col_new = lax.dynamic_slice_in_dim(every_new, col_start, col_count, 0)
    right_proj = jnp.dot(col_new, right_pair_weight, preferred_element_type=jnp.float32).astype(
        jnp.bfloat16
    )
    right_wide = rounded(right_proj).astype(jnp.float32)
    block_rows = math.gcd(rows_dev, 8)
    block_count = rows_dev // block_rows

    def transition(args):
        pair_rows, left_rows, live_rows = args
        summed = (
            pair_rows.astype(jnp.float32)
            + left_rows.astype(jnp.float32)[:, None, :]
            + right_wide[None]
        )
        normed = layer_norm(summed, pair_norm_gain).astype(jnp.bfloat16)
        hidden_one = jax.nn.relu(
            jnp.einsum(
                "rjc,ck->rjk", normed, transition_hidden_weight, preferred_element_type=jnp.float32
            )
        ).astype(jnp.bfloat16)
        hidden_two = jax.nn.relu(
            jnp.einsum(
                "rjc,ck->rjk",
                hidden_one,
                transition_middle_weight,
                preferred_element_type=jnp.float32,
            )
        ).astype(jnp.bfloat16)
        branch = jnp.einsum(
            "rjk,kc->rjc", hidden_two, transition_back_weight, preferred_element_type=jnp.float32
        )
        pair_live = (live_rows[:, None] * live_cols[None, :])[:, :, None]
        return (pair_rows.astype(jnp.float32) + pair_live * branch).astype(jnp.bfloat16)

    pair_out = lax.map(
        transition,
        (
            pair.reshape(block_count, block_rows, col_count, -1),
            left_proj.reshape(block_count, block_rows, -1),
            live_own.reshape(block_count, block_rows),
        ),
    ).reshape(pair.shape)
    return (single_out, rot_out, trans_out, pair_out)


def solution(mesh):
    placed = (
        P(("batch", "res"), None),
        P(("batch", "res"), "head", None),
        P(None, None, "batch"),
        P(None, "batch"),
        P(),
        P("batch"),
        P(),
        P(None, "head", None),
        P(),
        P("head"),
        P("head"),
        P("head", None, None),
        P(),
        P(),
        P(),
        P(),
        P(),
        P(),
        P(),
        P(),
        P(),
    )
    return jax.shard_map(
        shards,
        mesh=mesh,
        in_specs=placed,
        out_specs=(
            P(("batch", "res"), None),
            P(None, None, ("batch", "res")),
            P(None, ("batch", "res")),
            P(("batch", "res"), "head", None),
        ),
        check_vma=False,
    )
```

profile of v0, /device:TPU:0, one launch (start us, length us, event | category | flops | bytes accessed | tf_op | source)
XLA Modules:
  0.0 108.3 jit_solution(17804247734807519207)
XLA Ops:
  0.7 24.2 %all_gather.6 = bf16[384,384]{1,0:T(8,128)(2,1)S(1)} all-gather(bf16[24,384]{1,0:T(8,128)(2,1)} %param.23), channel_id=1, replica_groups=mesh['batch'=2,'res'=16,'head'=1] {'res'}, dimensions={0}, use_global_device_ids=true | all-gather | bytes 313344 | tf_op jit(solution)/shard_map/all_gather | solution.py:177
  24.9 3.0 %fusion.37 = f32[384,16,132]{0,2,1:T(8,128)} fusion(bf16[384,16,132]{0,1,2:T(8,128)(2,1)S(1)} %copy-done, bf16[384,384]{1,0:T(8,128)(2,1)S(1)} %all_gather.6), kind=kOutput, calls=%fused_computation.37 | convolution fusion | flops 622854144 | bytes 5160960 | tf_op jit(solution)/shard_map/nd,dhf->nhf/dot_general | solution.py:178
  27.9 1.1 %constant_dynamic-slice_fusion.2 = f32[24,16,24]{0,2,1:T(8,128)S(1)} fusion(f32[384,16,132]{0,2,1:T(8,128)} %fusion.37, s32[]{:T(128)S(6)} %select_n.6, s32[]{:T(128)S(6)} %add.349), kind=kLoop, calls=%fused_computation.117 | loop fusion | bytes 73736 | tf_op jit(solution)/shard_map/slice | solution.py:186
  29.5 0.7 bitcast_add_fusion.2
  31.9 1.0 fusion.53
  34.0 1.2 %slice.80 = bf16[384,16,32]{0,2,1:T(8,128)(2,1)S(1)} slice(f32[384,16,132]{0,2,1:T(8,128)} %fusion.37), slice={[0:384], [0:16], [16:48]} | slice | bytes 786432 | tf_op jit(solution)/shard_map/slice | solution.py:46
  35.8 1.1 %convert_element_type.93 = bf16[384,1472]{0,1:T(8,128)(2,1)} reshape(bf16[384,16,92]{0,2,1:T(8,128)(2,1)S(1)} %copy.128) | data formatting | bytes 2260992 | tf_op jit(solution)/shard_map/convert_element_type | solution.py:19
  36.9 1.4 %reshape.221 = bf16[384,16,92]{0,2,1:T(8,128)(2,1)S(1)} reshape(bf16[384,1472]{0,1:T(8,128)(2,1)} %convert_element_type.93) | data formatting | bytes 2260992 | tf_op jit(solution)/shard_map/reshape | solution.py:183
  38.5 1.4 %fusion.49 = f32[24,16,384]{2,0,1:T(8,128)} fusion(f32[16,384]{1,0:T(8,128)S(1)} %bitcast.175, f32[24,16]{0,1:T(8,128)S(1)} %copy-done.11, f32[16]{0:T(128)S(1)} %broadcast_multiply_fusion.3, bf16[384,16,92]{0,2,1:T(8,128)(2,1)S(1)} %reshape.221, f32[24,16,24]{0,1,2:T(8,128)S(1)} %copy-done.2), kind=kOutput, calls=%fused_computation.51 | convolution fusion | flops 43057152 | bytes 1114624 | tf_op jit(solution)/shard_map/rhp,nhp->rhn/dot_general | solution.py:111
  40.0 3.1 %fusion.72 = bf16[16,24,384]{2,0,1:T(8,128)(2,1)} fusion(bf16[24,384,128]{2,1,0:T(8,128)(2,1)} %param.24, bf16[128,16]{0,1:T(8,128)(2,1)S(1)} %copy-done.15), kind=kOutput, calls=%fused_computation.102 | convolution fusion | flops 37748736 | bytes 2658304 | tf_op jit(solution)/shard_map/rjc,ch->rhj/dot_general | solution.py:188
  43.1 2.5 %fusion.79 = (f32[24,16]{0,1:T(8,128)S(1)}, f32[24,16,384]{2,0,1:T(8,128)}) fusion(f32[24,16,384]{2,0,1:T(8,128)S(1)} %copy-done.3, bf16[16,24,384]{2,0,1:T(8,128)(2,1)} %fusion.72, f32[24,384]{1,0:T(8,128)S(1)} %compare_convert_fusion, f32[16]{0:T(128)S(1)} %copy-done.23, pred[384]{0:T(512)(128)(4,1)S(1)} %get-tuple-element.107, ...), kind=kOutput, calls=%fused_computation.131 | convolution fusion | flops 6193535 | bytes 1776132 | tf_op jit(solution)/shard_map/sub | solution.py:206
  45.6 1.2 %divide_convert_fusion = bf16[24,16,384]{2,0,1:T(8,128)(2,1)S(1)} fusion(f32[24,16,384]{2,0,1:T(8,128)} %get-tuple-element.122, f32[24,16]{0,1:T(8,128)S(1)} %get-tuple-element.121), kind=kLoop, calls=%fused_computation.70 | loop fusion | flops 294912 | bytes 886272 | tf_op jit(solution)/shard_map/convert_element_type | solution.py:19
  48.3 1.7 %convolution_bitcast_fusion.4 = f32[24,384]{1,0:T(8,128)S(1)} fusion(bf16[16,64,384]{2,1,0:T(8,128)(2,1)} %param.34, f32[24,16,12]{2,0,1:T(8,128)S(1)} %copy.140, f32[24,16,36]{2,0,1:T(8,128)S(1)} %copy.139, f32[24,16,16]{2,0,1:T(8,128)S(1)} %copy.138), kind=kOutput, calls=%fused_computation.60 | convolution fusion | flops 113295360 | bytes 921600 | tf_op jit(solution)/shard_map/rhf,hfd->rd/dot_general | solution.py:136
  50.0 2.3 %fusion.57 = f32[24,16,128]{2,1,0:T(8,128)S(1)} fusion(bf16[24,384,128]{2,1,0:T(8,128)(2,1)} %param.24, bf16[24,16,384]{2,0,1:T(8,128)(2,1)S(1)} %divide_convert_fusion), kind=kOutput, calls=%fused_computation.75 | convolution fusion | flops 37748736 | bytes 2850816 | tf_op jit(solution)/shard_map/rhj,rjc->rhc/dot_general | solution.py:222
  52.4 0.9 fusion.80
  53.6 18.4 %all_gather.7 = bf16[384,384]{1,0:T(8,128)(2,1)S(1)} all-gather(bf16[24,384]{1,0:T(8,128)(2,1)S(1)} %multiply_convert_fusion), channel_id=1, replica_groups=mesh['batch'=2,'res'=16,'head'=1] {'res'}, dimensions={0}, use_global_device_ids=true | all-gather | bytes 313344 | tf_op jit(solution)/shard_map/all_gather | solution.py:242
  72.7 30.8 %while.10 = (s32[]{:T(128)}, bf16[3,8,384,128]{3,2,1,0:T(8,128)(2,1)}, bf16[3,8,384,128]{3,2,1,0:T(8,128)(2,1)}, f32[3,8]{1,0:T(4,128)S(1)}, f32[384]{0:T(512)S(...) while((s32[]{:T(128)}, ...), condition=%wide.region_15.16_spmd, body=%wide.region_12.15_spmd.sunk | while | flops 816716800 | bytes 8086757 | solution.py:278
  72.7 1.6 %fusion.117 = f32[8,384]{1,0:T(8,128)S(1)} fusion(f32[384,128]{1,0:T(8,128)S(1)} %get-tuple-element.222, f32[8,128]{1,0:T(8,128)S(1)} %bitcast_convert_fusion.2, bf16[3,8,384,128]{3,2,1,0:T(8,128)(2,1)} %get-tuple-element.218, s32[]{:T(128)} %get-tuple-element.204), kind=kLoop, calls=%fused_computation.6.clone.1 | loop fusion | flops 1569792 | bytes 999428 | tf_op jit(solution)/shard_map/while/body/eval_jaxpr/reduce_sum | solution.py:23
  74.3 2.0 %fusion.118 = f32[8,384]{1,0:T(8,128)S(1)} fusion(f32[8,384]{1,0:T(8,128)S(1)} %broadcast_multiply_fusion.6, f32[384,128]{1,0:T(8,128)S(1)} %get-tuple-element.222, f32[8,128]{1,0:T(8,128)S(1)} %bitcast_convert_fusion.2, bf16[3,8,384,128]{3,2,1,0:T(8,128)(2,1)} %get-tuple-element.218, s32[]{:T(128)} %get-tuple-element.204), kind=kLoop, calls=%fused_computation.9.clone.1 | loop fusion | flops 2356224 | bytes 1011716 | tf_op jit(solution)/shard_map/while/body/eval_jaxpr/reduce_sum | solution.py:24
  76.4 3.4 %maximum_convert_fusion.3 = bf16[8,384,256]{2,1,0:T(8,128)(2,1)} fusion(f32[128]{0:T(128)S(1)} %get-tuple-element.223, f32[8,384]{1,0:T(8,128)S(1)} %add_rsqrt_fusion.3, f32[8,384]{1,0:T(8,128)S(1)} %broadcast_multiply_fusion.6, f32[384,128]{1,0:T(8,128)S(1)} %get-tuple-element.222, f32[8,128]{1,0:T(8,128)S(1)} %bitcast_convert_fusion.2, ...), kind=kOutput, calls=%fused_computation.clone.1 | convolution fusion | flops 609878016 | bytes 2782208 | tf_op jit(solution)/shard_map/while/body/eval_jaxpr/rjc,ck->rjk/dot_general | solution.py:265
  79.9 3.1 %fusion.120 = bf16[3,8,384,128]{3,2,1,0:T(8,128)(2,1)} fusion(bf16[3,8,384,128]{3,2,1,0:T(8,128)(2,1)} %get-tuple-element.205, s32[]{:T(128)} %get-tuple-element.204, bf16[8,384,256]{2,1,0:T(8,128)(2,1)} %maximum_convert_fusion.3, f32[8,384]{1,0:T(8,128)S(1)} %broadcast_multiply_fusion.7, bf16[3,8,384,128]{3,2,1,0:T(8,128)(2,1)} %get-tuple-element.218, ...), kind=kOutput, calls=%fused_computation.15.clone.1 | convolution fusion | flops 202899456 | bytes 3224064 | tf_op jit(solution)/shard_map/while/body/eval_jaxpr/rjk,kc->rjc/dot_general | solution.py:272
  83.0 1.6 %fusion.117 = f32[8,384]{1,0:T(8,128)S(1)} fusion(f32[384,128]{1,0:T(8,128)S(1)} %get-tuple-element.222, f32[8,128]{1,0:T(8,128)S(1)} %bitcast_convert_fusion.2, bf16[3,8,384,128]{3,2,1,0:T(8,128)(2,1)} %get-tuple-element.218, s32[]{:T(128)} %get-tuple-element.204), kind=kLoop, calls=%fused_computation.6.clone.1 | loop fusion | flops 1569792 | bytes 999428 | tf_op jit(solution)/shard_map/while/body/eval_jaxpr/reduce_sum | solution.py:23
  84.6 2.0 %fusion.118 = f32[8,384]{1,0:T(8,128)S(1)} fusion(f32[8,384]{1,0:T(8,128)S(1)} %broadcast_multiply_fusion.6, f32[384,128]{1,0:T(8,128)S(1)} %get-tuple-element.222, f32[8,128]{1,0:T(8,128)S(1)} %bitcast_convert_fusion.2, bf16[3,8,384,128]{3,2,1,0:T(8,128)(2,1)} %get-tuple-element.218, s32[]{:T(128)} %get-tuple-element.204), kind=kLoop, calls=%fused_computation.9.clone.1 | loop fusion | flops 2356224 | bytes 1011716 | tf_op jit(solution)/shard_map/while/body/eval_jaxpr/reduce_sum | solution.py:24
  86.7 3.4 %maximum_convert_fusion.3 = bf16[8,384,256]{2,1,0:T(8,128)(2,1)} fusion(f32[128]{0:T(128)S(1)} %get-tuple-element.223, f32[8,384]{1,0:T(8,128)S(1)} %add_rsqrt_fusion.3, f32[8,384]{1,0:T(8,128)S(1)} %broadcast_multiply_fusion.6, f32[384,128]{1,0:T(8,128)S(1)} %get-tuple-element.222, f32[8,128]{1,0:T(8,128)S(1)} %bitcast_convert_fusion.2, ...), kind=kOutput, calls=%fused_computation.clone.1 | convolution fusion | flops 609878016 | bytes 2782208 | tf_op jit(solution)/shard_map/while/body/eval_jaxpr/rjc,ck->rjk/dot_general | solution.py:265
  90.2 3.1 %fusion.120 = bf16[3,8,384,128]{3,2,1,0:T(8,128)(2,1)} fusion(bf16[3,8,384,128]{3,2,1,0:T(8,128)(2,1)} %get-tuple-element.205, s32[]{:T(128)} %get-tuple-element.204, bf16[8,384,256]{2,1,0:T(8,128)(2,1)} %maximum_convert_fusion.3, f32[8,384]{1,0:T(8,128)S(1)} %broadcast_multiply_fusion.7, bf16[3,8,384,128]{3,2,1,0:T(8,128)(2,1)} %get-tuple-element.218, ...), kind=kOutput, calls=%fused_computation.15.clone.1 | convolution fusion | flops 202899456 | bytes 3224064 | tf_op jit(solution)/shard_map/while/body/eval_jaxpr/rjk,kc->rjc/dot_general | solution.py:272
  93.2 1.6 %fusion.117 = f32[8,384]{1,0:T(8,128)S(1)} fusion(f32[384,128]{1,0:T(8,128)S(1)} %get-tuple-element.222, f32[8,128]{1,0:T(8,128)S(1)} %bitcast_convert_fusion.2, bf16[3,8,384,128]{3,2,1,0:T(8,128)(2,1)} %get-tuple-element.218, s32[]{:T(128)} %get-tuple-element.204), kind=kLoop, calls=%fused_computation.6.clone.1 | loop fusion | flops 1569792 | bytes 999428 | tf_op jit(solution)/shard_map/while/body/eval_jaxpr/reduce_sum | solution.py:23
  94.9 2.0 %fusion.118 = f32[8,384]{1,0:T(8,128)S(1)} fusion(f32[8,384]{1,0:T(8,128)S(1)} %broadcast_multiply_fusion.6, f32[384,128]{1,0:T(8,128)S(1)} %get-tuple-element.222, f32[8,128]{1,0:T(8,128)S(1)} %bitcast_convert_fusion.2, bf16[3,8,384,128]{3,2,1,0:T(8,128)(2,1)} %get-tuple-element.218, s32[]{:T(128)} %get-tuple-element.204), kind=kLoop, calls=%fused_computation.9.clone.1 | loop fusion | flops 2356224 | bytes 1011716 | tf_op jit(solution)/shard_map/while/body/eval_jaxpr/reduce_sum | solution.py:24
  96.9 3.4 %maximum_convert_fusion.3 = bf16[8,384,256]{2,1,0:T(8,128)(2,1)} fusion(f32[128]{0:T(128)S(1)} %get-tuple-element.223, f32[8,384]{1,0:T(8,128)S(1)} %add_rsqrt_fusion.3, f32[8,384]{1,0:T(8,128)S(1)} %broadcast_multiply_fusion.6, f32[384,128]{1,0:T(8,128)S(1)} %get-tuple-element.222, f32[8,128]{1,0:T(8,128)S(1)} %bitcast_convert_fusion.2, ...), kind=kOutput, calls=%fused_computation.clone.1 | convolution fusion | flops 609878016 | bytes 2782208 | tf_op jit(solution)/shard_map/while/body/eval_jaxpr/rjc,ck->rjk/dot_general | solution.py:265
  100.4 3.1 %fusion.120 = bf16[3,8,384,128]{3,2,1,0:T(8,128)(2,1)} fusion(bf16[3,8,384,128]{3,2,1,0:T(8,128)(2,1)} %get-tuple-element.205, s32[]{:T(128)} %get-tuple-element.204, bf16[8,384,256]{2,1,0:T(8,128)(2,1)} %maximum_convert_fusion.3, f32[8,384]{1,0:T(8,128)S(1)} %broadcast_multiply_fusion.7, bf16[3,8,384,128]{3,2,1,0:T(8,128)(2,1)} %get-tuple-element.218, ...), kind=kOutput, calls=%fused_computation.15.clone.1 | convolution fusion | flops 202899456 | bytes 3224064 | tf_op jit(solution)/shard_map/while/body/eval_jaxpr/rjk,kc->rjc/dot_general | solution.py:272
  105.1 0.8 constant_dynamic-slice_fusion.1
  106.4 0.7 bitcast_add_fusion.3
  107.6 0.7 copy.148
  (136 shorter events, 8.4 us)
Async XLA Ops:
  0.6 24.3 %copy-start = (bf16[384,16,132]{0,1,2:T(8,128)(2,1)S(1)}, bf16[384,16,132]{0,1,2:T(8,128)(2,1)}, u32[]{:S(2)}) copy-start(bf16[384,16,132]{0,1,2:T(8,128)(2,1)} %param.30) | copy-start | bytes 4866052
  24.9 4.3 %copy-start.5 = (f32[3,3,384]{2,1,0:T(4,128)S(1)}, f32[3,3,384]{2,1,0:T(4,128)}, u32[]{:S(2)}) copy-start(f32[3,3,384]{2,1,0:T(4,128)} %param.25) | copy-start | bytes 41476
  27.9 1.5 %copy-start.10 = (f32[3,384]{1,0:T(4,128)S(1)}, f32[3,384]{1,0:T(4,128)}, u32[]{:S(2)}) copy-start(f32[3,384]{1,0:T(4,128)} %param.26) | copy-start | bytes 13828
  29.4 1.5 %slice-start = ((f32[384,16,132]{0,2,1:T(8,128)}), f32[384,16,36]{0,2,1:T(8,128)S(1)}, s32[]{:S(2)}) async-start(f32[384,16,132]{0,2,1:T(8,128)} %fusion.37), calls=%async_computation | async-start | bytes 1966080 | tf_op jit(solution)/shard_map/slice | solution.py:43
  29.5 1.5 %copy-start.12 = (f32[24,3]{0,1:T(4,128)}, f32[24,3]{0,1:T(4,128)S(1)}, u32[]{:S(2)}) copy-start(f32[24,3]{0,1:T(4,128)S(1)} %dynamic-slice_bitcast_fusion) | copy-start | bytes 868
  31.3 1.7 %slice-start.1 = ((f32[384,16,132]{0,2,1:T(8,128)}), f32[384,16,24]{0,2,1:T(8,128)S(1)}, s32[]{:S(2)}) async-start(f32[384,16,132]{0,2,1:T(8,128)} %fusion.37), calls=%async_computation.1 | async-start | bytes 1179648 | tf_op jit(solution)/shard_map/slice | solution.py:41
  32.9 0.7 copy-start.6
  36.9 1.6 %copy-start.22 = (f32[16]{0:T(128)S(1)}, f32[16]{0:T(128)}, u32[]{:S(2)}) copy-start(f32[16]{0:T(128)} %param.32) | copy-start | bytes 196
  36.9 1.6 %copy-start.2 = (f32[24,16,24]{0,1,2:T(8,128)S(1)}, f32[24,16,24]{0,1,2:T(8,128)}, u32[]{:S(2)}) copy-start(f32[24,16,24]{0,1,2:T(8,128)} %bitcast_add_fusion.2) | copy-start | bytes 110596
  36.9 1.6 %copy-start.11 = (f32[24,16]{0,1:T(8,128)S(1)}, f32[24,16]{0,1:T(8,128)}, u32[]{:S(2)}) copy-start(f32[24,16]{0,1:T(8,128)} %multiply_reduce_fusion.6) | copy-start | bytes 4612
  36.9 3.0 %copy-start.16 = (s32[384]{0:T(512)S(1)}, s32[384]{0:T(512)}, u32[]{:S(2)}) copy-start(s32[384]{0:T(512)} %param.27) | copy-start | bytes 4612
  36.9 3.1 %copy-start.18 = (s32[384]{0:T(512)S(1)}, s32[384]{0:T(512)}, u32[]{:S(2)}) copy-start(s32[384]{0:T(512)} %param.28) | copy-start | bytes 4612
  36.9 3.1 %copy-start.15 = (bf16[128,16]{0,1:T(8,128)(2,1)S(1)}, bf16[128,16]{0,1:T(8,128)(2,1)}, u32[]{:S(2)}) copy-start(bf16[128,16]{0,1:T(8,128)(2,1)} %param.31) | copy-start | bytes 12292
  39.8 3.3 %copy-start.3 = (f32[24,16,384]{2,0,1:T(8,128)S(1)}, f32[24,16,384]{2,0,1:T(8,128)}, u32[]{:S(2)}) copy-start(f32[24,16,384]{2,0,1:T(8,128)} %fusion.49) | copy-start | bytes 1769476
  39.8 3.3 %copy-start.23 = (f32[16]{0:T(128)S(1)}, f32[16]{0:T(128)}, u32[]{:S(2)}) copy-start(f32[16]{0:T(128)} %param.33) | copy-start | bytes 196
  45.6 2.1 %copy-start.13 = (f32[24,3]{0,1:T(4,128)S(1)}, f32[24,3]{0,1:T(4,128)}, u32[]{:S(2)}) copy-start(f32[24,3]{0,1:T(4,128)} %copy-done.12) | copy-start | bytes 868
  50.0 2.3 %copy-start.1 = (bf16[16,128,384]{2,1,0:T(8,128)(2,1)S(1)}, bf16[16,128,384]{2,1,0:T(8,128)(2,1)}, u32[]{:S(2)}) copy-start(bf16[16,128,384]{2,1,0:T(8,128)(2,1)} %param.35) | copy-start | bytes 4718596
  50.0 2.3 %copy-start.9 = (bf16[24,384]{1,0:T(8,128)(2,1)S(1)}, bf16[24,384]{1,0:T(8,128)(2,1)}, u32[]{:S(2)}) copy-start(bf16[24,384]{1,0:T(8,128)(2,1)} %param.23) | copy-start | bytes 55300
  52.3 1.2 %copy-start.17 = (f32[384]{0:T(512)S(1)}, f32[384]{0:T(512)}, u32[]{:S(2)}) copy-start(f32[384]{0:T(512)} %param.36) | copy-start | bytes 4612
  52.4 19.7 %copy-start.8 = (bf16[384,128]{1,0:T(8,128)(2,1)S(1)}, bf16[384,128]{1,0:T(8,128)(2,1)}, u32[]{:S(2)}) copy-start(bf16[384,128]{1,0:T(8,128)(2,1)} %param.39) | copy-start | bytes 294916
  52.4 19.9 %copy-start.7 = (bf16[384,128]{1,0:T(8,128)(2,1)S(1)}, bf16[384,128]{1,0:T(8,128)(2,1)}, u32[]{:S(2)}) copy-start(bf16[384,128]{1,0:T(8,128)(2,1)} %param.38) | copy-start | bytes 294916
  52.4 20.2 %copy-start.19 = (bf16[256,256]{1,0:T(8,128)(2,1)S(1)}, bf16[256,256]{1,0:T(8,128)(2,1)}, u32[]{:S(2)}) copy-start(bf16[256,256]{1,0:T(8,128)(2,1)} %param.42) | copy-start | bytes 393220
  52.4 20.2 %copy-start.20 = (bf16[128,256]{1,0:T(8,128)(2,1)S(1)}, bf16[128,256]{1,0:T(8,128)(2,1)}, u32[]{:S(2)}) copy-start(bf16[128,256]{1,0:T(8,128)(2,1)} %param.41) | copy-start | bytes 196612
  52.4 20.2 %copy-start.21 = (bf16[256,128]{1,0:T(8,128)(2,1)S(1)}, bf16[256,128]{1,0:T(8,128)(2,1)}, u32[]{:S(2)}) copy-start(bf16[256,128]{1,0:T(8,128)(2,1)} %param.43) | copy-start | bytes 196612
  52.4 20.2 %copy-start.24 = (f32[128]{0:T(128)S(1)}, f32[128]{0:T(128)}, u32[]{:S(2)}) copy-start(f32[128]{0:T(128)} %param.40) | copy-start | bytes 1540
  53.6 49.9 %copy-start.4 = (bf16[24,384]{1,0:T(8,128)(2,1)}, bf16[24,384]{1,0:T(8,128)(2,1)S(1)}, u32[]{:S(2)}) copy-start(bf16[24,384]{1,0:T(8,128)(2,1)S(1)} %multiply_convert_fusion) | copy-start | bytes 55300
  72.7 30.9 %copy-start.14 = (bf16[384,6]{0,1:T(8,128)(2,1)S(1)}, bf16[384,6]{0,1:T(8,128)(2,1)}, u32[]{:S(2)}) copy-start(bf16[384,6]{0,1:T(8,128)(2,1)} %param.37) | copy-start | bytes 13828
where the time goes:
time: 109 us; the launch traced here: 108 us
  blocking collectives  42.7 us (39%)
  matrix products  36.3 us (33%)
  other arithmetic  16.9 us (16%)
  local copies, waits for them, and re-layouts  10.4 us (10%)
  between operations  1.91 us (2%)
    all_gather x1, blocking collectives, shards(): every_single = lax.all_gather(single, 'res', axis=0, tiled=True)  24.2 us
    all_gather x1, blocking collectives, shards(): every_new = lax.all_gather(single_out, 'res', axis=0, tiled=True)  18.4 us
    dot_general x3, matrix products, transition(): jnp.einsum('rjc,ck->rjk', hidden_one, transition_middle_weight, preferred...  10.3 us
    dot_general x3, matrix products, transition(): jnp.einsum('rjk,kc->rjc', hidden_two, transition_back_weight, preferred_e...  9.21 us
    reduce_sum x4, other arithmetic, layer_norm(): variance = jnp.mean(jnp.square(values - centre), axis=-1, keepdims=True)  6.3 us
    reduce_sum x3, other arithmetic, layer_norm(): centre = jnp.mean(values, axis=-1, keepdims=True)  4.84 us
    dot_general x1, matrix products, shards(): jnp.einsum('rjc,ch->rhj', pair, head_bias_weight, preferred_element_type=...  3.12 us
    dot_general x1, matrix products, shards(): jnp.einsum('nd,dhf->nhf', every_single, single_projection_weight, preferr...  3.03 us

commit v1 on v0

--- a/solution.py
+++ b/solution.py
@@ -1,8 +1,11 @@
+import functools
 import math
 
 import jax
 import jax.numpy as jnp
 from jax import lax
+from jax.experimental import pallas as pl
+from jax.experimental.pallas import tpu as pltpu
 from jax.sharding import PartitionSpec as P
 
 HEAD_FEATURES = 16
@@ -135,6 +138,159 @@
     )
     return jnp.einsum(
         "rhf,hfd->rd", features, local_output_weight.astype(jnp.float32), precision=HIGHEST
+    )
+
+
+def exchange(block, count, step):
+    return lax.ppermute(block, "res", [(k, k ^ step) for k in range(count)])
+
+
+def gather_blocks(block, count):
+    if count < 16 or count & (count - 1):
+        whole = lax.all_gather(block, "res", axis=0)
+        return None, whole
+    held, offsets = block[None], [0]
+    quarter = count // 4
+    step = quarter // 2
+    while step > 1:
+        held = jnp.concatenate([held, exchange(held, count, step)], 0)
+        offsets = offsets + [o ^ step for o in offsets]
+        step //= 2
+    parts = [held] + [exchange(held, count, k * quarter) for k in (3, 2, 1)]
+    held = jnp.concatenate(parts, 0)
+    offsets = [o ^ (k * quarter) for k in (0, 3, 2, 1) for o in offsets]
+    other = exchange(held, count, 1)
+    return offsets, (held, other)
+
+
+def sorted_blocks(offsets, blocks):
+    if offsets is None:
+        return blocks
+    held, other = blocks
+    entries = [held[e] for e in range(len(offsets))] + [other[e] for e in range(len(offsets))]
+    every = dict(zip(offsets + [o ^ 1 for o in offsets], entries))
+    both = jnp.stack([every[o] for o in range(len(every))])
+    index = lax.axis_index("res")
+    bit = 1
+    while bit < len(every):
+        halves = both.reshape((-1, 2, bit) + held.shape[1:])
+        both = jnp.where((index & bit) > 0, halves[:, ::-1], halves).reshape(both.shape)
+        bit *= 2
+    return both
+
+
+def transition_kernel(
+    rows_block,
+    rows_dev,
+    offsets,
+    live_ref,
+    pair_ref,
+    left_ref,
+    live_row_ref,
+    gain_ref,
+    hidden_ref,
+    middle_ref,
+    back_ref,
+    *rest,
+):
+    block_refs, (out_ref, right_ref, live_cols_ref, centring_ref) = rest[:-4], rest[-4:]
+    step = pl.program_id(0)
+    cols, feats = pair_ref.shape[1:]
+    me = lax.axis_index("res")
+    col_start = lax.axis_index("head") * cols
+
+    @pl.when(step == 0)
+    def _():
+        at = 0
+        for ref in block_refs:
+            for e in range(ref.shape[0]):
+                value = ref[e].astype(jnp.float32)
+                value = value - jnp.mean(value, axis=-1, keepdims=True)
+                owner = me ^ offsets[at] if offsets is not None else at
+                at += 1
+                right_ref[pl.ds(pl.multiple_of(owner * rows_dev, 8), rows_dev), :] = value
+        wide = jnp.broadcast_to(live_row_ref[...].astype(jnp.float32), (feats, live_row_ref.shape[1]))
+        live_cols_ref[...] = jnp.where(jnp.transpose(wide) > 0, 1.0, 0.0)
+        across = lax.broadcasted_iota(jnp.int32, (feats, feats), 0)
+        down = lax.broadcasted_iota(jnp.int32, (feats, feats), 1)
+        centring_ref[...] = (jnp.where(across == down, 1.0, 0.0) - 1.0 / feats).astype(jnp.bfloat16)
+
+    columns = pl.ds(pl.multiple_of(col_start, 8), cols)
+    pair = pair_ref[...].reshape(rows_block * cols, feats)
+    centred = jnp.dot(pair, centring_ref[...], preferred_element_type=jnp.float32)
+    left = left_ref[...].astype(jnp.float32)
+    left = left - jnp.mean(left, axis=-1, keepdims=True)
+    centred = centred.reshape(rows_block, cols, feats) + left[:, None, :] + right_ref[columns, :][None]
+    centred = centred.reshape(rows_block * cols, feats)
+    averaging = jnp.full((feats, feats), 1.0 / feats, jnp.bfloat16)
+    variance = jnp.dot(
+        (centred * centred).astype(jnp.bfloat16), averaging, preferred_element_type=jnp.float32
+    )
+    normed = (centred * lax.rsqrt(variance + 1e-05) * gain_ref[...]).astype(jnp.bfloat16)
+    hidden_one = jnp.maximum(
+        jnp.dot(normed, hidden_ref[...], preferred_element_type=jnp.float32).astype(jnp.bfloat16), 0
+    )
+    hidden_two = jnp.maximum(
+        jnp.dot(hidden_one, middle_ref[...], preferred_element_type=jnp.float32).astype(
+            jnp.bfloat16
+        ),
+        0,
+    )
+    branch = jnp.dot(hidden_two, back_ref[...], preferred_element_type=jnp.float32)
+    branch = branch.reshape(rows_block, cols, feats)
+    live_cols = live_cols_ref[columns, :]
+    for r in range(rows_block):
+        live = jnp.where(live_ref[me * rows_dev + step * rows_block + r] > 0, 1.0, 0.0)
+        out_ref[r] = (
+            pair_ref[r].astype(jnp.float32) + live * live_cols * branch[r]
+        ).astype(jnp.bfloat16)
+
+
+def pair_transition(
+    pair, left_proj, move_mask, gain, hidden, middle, back, offsets, blocks
+):
+    rows_dev, cols, feats = pair.shape
+    total = move_mask.shape[0]
+    rows_block = math.gcd(rows_dev, max(1, 1536 // cols))
+    left_wide = left_proj.reshape(rows_dev // rows_block, rows_block, feats)
+    whole = lambda *shape: pl.BlockSpec(shape, lambda i: (0,) * len(shape))
+    kernel = functools.partial(transition_kernel, rows_block, rows_dev, offsets)
+    macs = rows_dev * cols * (2 * feats * feats + 2 * feats * hidden.shape[1] + hidden.shape[1] ** 2)
+    return pl.pallas_call(
+        kernel,
+        grid=(rows_dev // rows_block,),
+        in_specs=[
+            pl.BlockSpec(memory_space=pltpu.SMEM),
+            pl.BlockSpec((rows_block, cols, feats), lambda i: (i, 0, 0)),
+            pl.BlockSpec((None, rows_block, feats), lambda i: (i, 0, 0)),
+            whole(1, total),
+            whole(1, feats),
+            whole(*hidden.shape),
+            whole(*middle.shape),
+            whole(*back.shape),
+        ]
+        + [whole(*b.shape) for b in blocks],
+        out_specs=pl.BlockSpec((rows_block, cols, feats), lambda i: (i, 0, 0)),
+        out_shape=jax.ShapeDtypeStruct(pair.shape, pair.dtype),
+        scratch_shapes=[
+            pltpu.VMEM((total, feats), jnp.float32),
+            pltpu.VMEM((total, feats), jnp.float32),
+            pltpu.VMEM((feats, feats), jnp.bfloat16),
+        ],
+        compiler_params=pltpu.CompilerParams(vmem_limit_bytes=48 * 1024 * 1024),
+        cost_estimate=pl.CostEstimate(
+            flops=2 * macs, bytes_accessed=2 * pair.size * 2, transcendentals=0
+        ),
+    )(
+        move_mask,
+        pair,
+        left_wide,
+        move_mask[None],
+        gain[None],
+        hidden,
+        middle,
+        back,
+        *blocks,
     )
 
 
@@ -166,7 +322,6 @@
     total = rotations.shape[2]
     heads_here = single_projection_weight.shape[1]
     row_start = lax.axis_index("res") * rows_dev
-    col_start = lax.axis_index("head") * col_count
     rot_all = jnp.transpose(rotations, (2, 0, 1))
     trans_all = jnp.transpose(translations)
     rot_own = lax.dynamic_slice_in_dim(rot_all, row_start, rows_dev, 0)
@@ -174,7 +329,8 @@
     own_chain = lax.dynamic_slice_in_dim(residue_chain_index, row_start, rows_dev, 0)
     offset = 3 * HEAD_FEATURES
     feat_count = 2 * HEAD_FEATURES + 3 * PQ + 3 * PV
-    every_single = lax.all_gather(single, "res", axis=0, tiled=True)
+    count = total // rows_dev
+    every_single = sorted_blocks(*gather_blocks(single, count)).reshape(total, -1)
     every_proj = jnp.einsum(
         "nd,dhf->nhf", every_single, single_projection_weight, preferred_element_type=jnp.float32
     )
@@ -231,7 +387,6 @@
     )
     live_all = (residue_move_mask > 0).astype(jnp.float32)
     live_own = lax.dynamic_slice_in_dim(live_all, row_start, rows_dev, 0)
-    live_cols = lax.dynamic_slice_in_dim(live_all, col_start, col_count, 0)
     step_ratio = 1.0 / (STEPS - timestep[0]).astype(jnp.float32)
     rot_out, trans_out = frame_step(
         single_out, frame_velocity_weight, rot_own, trans_own, live_own, step_ratio
@@ -239,50 +394,25 @@
     left_proj = jnp.dot(single_out, left_pair_weight, preferred_element_type=jnp.float32).astype(
         jnp.bfloat16
     )
-    every_new = lax.all_gather(single_out, "res", axis=0, tiled=True)
-    col_new = lax.dynamic_slice_in_dim(every_new, col_start, col_count, 0)
-    right_proj = jnp.dot(col_new, right_pair_weight, preferred_element_type=jnp.float32).astype(
+    right_proj = jnp.dot(single_out, right_pair_weight, preferred_element_type=jnp.float32).astype(
         jnp.bfloat16
     )
-    right_wide = rounded(right_proj).astype(jnp.float32)
-    block_rows = math.gcd(rows_dev, 8)
-    block_count = rows_dev // block_rows
-
-    def transition(args):
-        pair_rows, left_rows, live_rows = args
-        summed = (
-            pair_rows.astype(jnp.float32)
-            + left_rows.astype(jnp.float32)[:, None, :]
-            + right_wide[None]
-        )
-        normed = layer_norm(summed, pair_norm_gain).astype(jnp.bfloat16)
-        hidden_one = jax.nn.relu(
-            jnp.einsum(
-                "rjc,ck->rjk", normed, transition_hidden_weight, preferred_element_type=jnp.float32
-            )
-        ).astype(jnp.bfloat16)
-        hidden_two = jax.nn.relu(
-            jnp.einsum(
-                "rjc,ck->rjk",
-                hidden_one,
-                transition_middle_weight,
-                preferred_element_type=jnp.float32,
-            )
-        ).astype(jnp.bfloat16)
-        branch = jnp.einsum(
-            "rjk,kc->rjc", hidden_two, transition_back_weight, preferred_element_type=jnp.float32
-        )
-        pair_live = (live_rows[:, None] * live_cols[None, :])[:, :, None]
-        return (pair_rows.astype(jnp.float32) + pair_live * branch).astype(jnp.bfloat16)
-
-    pair_out = lax.map(
-        transition,
-        (
-            pair.reshape(block_count, block_rows, col_count, -1),
-            left_proj.reshape(block_count, block_rows, -1),
-            live_own.reshape(block_count, block_rows),
-        ),
-    ).reshape(pair.shape)
+    offsets, blocks = gather_blocks(right_proj, count)
+    if offsets is None:
+        blocks = (blocks,)
+    else:
+        offsets = offsets + [o ^ 1 for o in offsets]
+    pair_out = pair_transition(
+        pair,
+        left_proj,
+        residue_move_mask,
+        pair_norm_gain,
+        transition_hidden_weight,
+        transition_middle_weight,
+        transition_back_weight,
+        offsets,
+        blocks,
+    )
     return (single_out, rot_out, trans_out, pair_out)
 
 

time: 109 us -> 75 us (0.69)
  blocking collectives: 42.7 us -> 0 us
  matrix products: 36.3 us -> 14.7 us
  starting transfers between devices: 0 us -> 12.5 us
  Pallas kernels: 0 us -> 9.49 us
  local copies, waits for them, and re-layouts: 10.4 us -> 19.6 us
  other arithmetic: 16.9 us -> 8.88 us
  waiting for transfers between devices: 0 us -> 6.9 us
    all_gather x2 -> x0, blocking collectives: 42.7 us -> none  [the longest x1 24.2 us: shards(): every_single = lax.all_gather(single, 'res', axis=0, tiled=True)]
    dot_general x7 -> x1, matrix products: 19.7 us -> 0.14 us  [shards(): jnp.dot(single_out, right_pair_weight, preferred_element_type=jnp.float32)]
    ppermute x0 -> x10, starting transfers between devices: none -> 12.5 us  [exchange(): return lax.ppermute(block, 'res', [(k, k ^ step) for k in range(count)])]
    pallas_call x0 -> x1, Pallas kernels: none -> 9.49 us  [pair_transition(): pl.pallas_call(kernel, grid=(rows_dev // rows_block,), in_specs=[pl.Block...]
    ppermute x0 -> x10, waiting for transfers between devices: none -> 6.9 us  [exchange(): return lax.ppermute(block, 'res', [(k, k ^ step) for k in range(count)])]
    reduce_sum x4 -> x1, other arithmetic: 6.3 us -> 0.18 us  [layer_norm(): variance = jnp.mean(jnp.square(values - centre), axis=-1, keepdims=True)]
    unnamed x52 -> x81, local copies, waits for them, and re-layouts: 1.31 us -> 6.96 us
    reduce_sum x3 -> x0, other arithmetic: 4.84 us -> none  [layer_norm(): centre = jnp.mean(values, axis=-1, keepdims=True)]
  transfers between devices with their start and end apart: 0 -> 10, of which waited for: 0 -> 6; matrix products, arithmetic and copies ran while one was open for 0% -> 22% of each run, Pallas kernels for 0% -> 0%
where the time goes in v1:
time: 75 us; the launch traced here: 74.2 us
  local copies, waits for them, and re-layouts  19.6 us (26%)
  matrix products  14.7 us (20%)
  starting transfers between devices  12.5 us (17%)
  Pallas kernels  9.49 us (13%)
  other arithmetic  8.88 us (12%)
  waiting for transfers between devices  6.9 us (9%)
  between operations  2.05 us (3%)
    ppermute x10, starting transfers between devices, exchange(): return lax.ppermute(block, 'res', [(k, k ^ step) for k in range(count)])  12.5 us
    pallas_call x1, Pallas kernels, pair_transition(): pl.pallas_call(kernel, grid=(rows_dev // rows_block,), in_specs=[pl.Block...  9.49 us
    unnamed x81, local copies, waits for them, and re-layouts  6.96 us
    ppermute x10, waiting for transfers between devices, exchange(): return lax.ppermute(block, 'res', [(k, k ^ step) for k in range(count)])  6.9 us
    dot_general x1, matrix products, shards(): jnp.einsum('rjc,ch->rhj', pair, head_bias_weight, preferred_element_type=...  3.14 us
    dot_general x1, matrix products, local_points(): jnp.einsum('rhf,hfd->rd', features, local_output_weight.astype(jnp.float3...  2.04 us
    sub x1, matrix products, shards(): exponent = jnp.exp(logit_matrix - peak)  1.95 us
    dot_general x1, matrix products, shards(): jnp.einsum('rhc,hcd->rd', pair_attended, pair_output_weight.astype(jnp.fl...  1.89 us
  transfers between devices with their start and end apart: 10, of which 6 were waited for; matrix products, arithmetic and copies ran while one was open for 22% of the time, Pallas kernels for 0%

profile of v1, /device:TPU:0, one launch (start us, length us, event | category | flops | bytes accessed | tf_op | source)
XLA Modules:
  0.0 74.2 jit_solution(3063033935289997041)
XLA Ops:
  0.7 3.0 %collective-permute-start = (bf16[1,24,384]{2,1,0:T(8,128)(2,1)}, bf16[1,24,384]{2,1,0:T(8,128)(2,1)S(1)}, u32[]{:S(2)}, u32[]{:S(2)}) collective-permute-start(bf16[1,24,384]{2,1,0:T(8,128)(2,1)} %bitcast.135), channel_id=1, source_target_pairs={{0,2},{1,3},{2,0},{3,1},{4,6},{5,7},{6,4},{7,5},{8,10},{9,11},{10,... | collective-permute-start | bytes 55304 | tf_op jit(solution)/shard_map/ppermute | solution.py:145
  3.7 0.8 %constant_dynamic-update-slice_fusion.4 = (bf16[8,24,384]{2,1,0:T(8,128)(2,1)S(1)}, bf16[16,24,384]{2,1,0:T(8,128)(2,1)S(1)}) fusion(bf16[24,384]{1,0:T(8,128)(2,1)} %param.21), kind=kLoop, calls=%fused_computation.66 | loop fusion | bytes 55296
  4.4 1.2 %broadcast_multiply_fusion.1 = f32[16]{0:T(128)} fusion(f32[16]{0:T(128)} %param.30), kind=kLoop, calls=%fused_computation.121 | loop fusion | flops 16 | bytes 128 | tf_op jit(solution)/shard_map/mul | solution.py:124
  6.4 1.4 %compare_convert_fusion = f32[24,384]{1,0:T(8,128)} fusion(s32[384]{0:T(512)} %param.25, s32[24]{0:T(128)S(1)} %dynamic_slice.18), kind=kLoop, calls=%fused_computation.94 | loop fusion | flops 18432 | bytes 38496 | tf_op jit(solution)/shard_map/convert_element_type | solution.py:350
  7.8 1.2 %fusion.41 = (f32[384]{0:T(512)S(1)}, pred[384]{0:T(512)(128)(4,1)}) fusion(s32[384]{0:T(512)} %live_ref.1), kind=kLoop, calls=%fused_computation.127 | loop fusion | flops 768 | bytes 3456 | tf_op jit(solution)/shard_map/convert_element_type | solution.py:388
  9.0 0.8 %constant_dynamic-slice_fusion = f32[3,3,24]{2,1,0:T(4,128)S(1)} fusion(f32[3,3,384]{2,1,0:T(4,128)} %param.23, s32[]{:T(128)S(6)} %select_n.51), kind=kLoop, calls=%fused_computation.113 | loop fusion | bytes 1732 | tf_op jit(solution)/shard_map/dynamic-slice
  9.8 3.1 %fusion.35 = bf16[16,24,384]{2,0,1:T(8,128)(2,1)} fusion(bf16[24,384,128]{2,1,0:T(8,128)(2,1)} %pair_ref.1, bf16[128,16]{0,1:T(8,128)(2,1)} %param.29), kind=kOutput, calls=%fused_computation.99 | convolution fusion | flops 37748736 | bytes 2658304 | tf_op jit(solution)/shard_map/rjc,ch->rhj/dot_general | solution.py:344
  13.5 3.7 %collective-permute-start.1 = (bf16[2,24,384]{2,1,0:T(8,128)(2,1)S(1)}, bf16[2,24,384]{2,1,0:T(8,128)(2,1)S(1)}, u32[]{:S(2)}, u32[]{:S(2)}) collective-permute-start(bf16[2,24,384]{2,1,0:T(8,128)(2,1)S(1)} %pad_maximum_fusion.1), channel_id=1, source_target_pairs={{0,12},{1,13},{2,14},{3,15},{4,8},{5,9},{6,10},{7,11},{8,4},{9,5},... | collective-permute-start | bytes 110600 | tf_op jit(solution)/shard_map/ppermute | solution.py:145
  17.2 0.8 %collective-permute-start.3 = (bf16[2,24,384]{2,1,0:T(8,128)(2,1)S(1)}, bf16[2,24,384]{2,1,0:T(8,128)(2,1)S(1)}, u32[]{:S(2)}, u32[]{:S(2)}) collective-permute-start(bf16[2,24,384]{2,1,0:T(8,128)(2,1)S(1)} %pad_maximum_fusion.1), channel_id=1, source_target_pairs={{0,4},{1,5},{2,6},{3,7},{4,0},{5,1},{6,2},{7,3},{8,12},{9,13},{10,... | collective-permute-start | bytes 110600 | tf_op jit(solution)/shard_map/ppermute | solution.py:145
  18.0 1.8 %collective-permute-done.1 = bf16[2,24,384]{2,1,0:T(8,128)(2,1)S(1)} collective-permute-done((bf16[2,24,384]{2,1,0:T(8,128)(2,1)S(1)}, bf16[2,24,384]{2,1,0:T(8,128)(2,1)S(1)}, u32[]{:S(2)}, u32[]{:S(2)}) %collective-permute-start.1) | collective-permute-done | bytes 36896 | tf_op jit(solution)/shard_map/ppermute | solution.py:145
  19.7 2.3 %collective-permute-done.2 = bf16[2,24,384]{2,1,0:T(8,128)(2,1)S(1)} collective-permute-done((bf16[2,24,384]{2,1,0:T(8,128)(2,1)S(1)}, bf16[2,24,384]{2,1,0:T(8,128)(2,1)S(1)}, u32[]{:S(2)}, u32[]{:S(2)}) %collective-permute-start.2) | collective-permute-done | bytes 36896 | tf_op jit(solution)/shard_map/ppermute | solution.py:145
  25.0 0.8 %fusion.65 = f32[24,3,3]{0,2,1:T(4,128)S(1)} fusion(f32[3,3,384]{2,1,0:T(4,128)} %param.23, s32[]{:T(128)S(6)} %select_n.51), kind=kLoop, calls=%fused_computation.132 | loop fusion | bytes 1732 | tf_op jit(solution)/shard_map/dynamic_slice | solution.py:327
  26.2 1.4 %fusion.1 = f32[384,16,132]{0,2,1:T(8,128)S(1)} fusion(bf16[384,384,1]{1,0,2:T(8,128)(2,1)S(1)} %bitcast.128, bf16[384,16,132]{0,1,2:T(8,128)(2,1)S(1)} %copy-done), kind=kOutput, calls=%fused_computation.3 | convolution fusion | flops 622854144 | bytes 5160960 | tf_op jit(solution)/shard_map/nd,dhf->nhf/dot_general | solution.py:334
  27.7 1.6 %copy-done.8 = f32[384,16,132]{0,2,1:T(8,128)} copy-done((f32[384,16,132]{0,2,1:T(8,128)}, f32[384,16,132]{0,2,1:T(8,128)S(1)}, u32[]{:S(2)}) %copy-start.8) | copy-done | bytes 3244056
  33.1 1.3 %convert_element_type.61 = bf16[384,1472]{0,1:T(8,128)(2,1)} reshape(bf16[384,16,92]{0,2,1:T(8,128)(2,1)S(1)} %copy.128) | data formatting | bytes 2260992 | tf_op jit(solution)/shard_map/convert_element_type | solution.py:22
  34.5 1.4 %reshape.162 = bf16[384,16,92]{0,2,1:T(8,128)(2,1)S(1)} reshape(bf16[384,1472]{0,1:T(8,128)(2,1)} %convert_element_type.61) | data formatting | bytes 2260992 | tf_op jit(solution)/shard_map/reshape | solution.py:339
  36.0 1.4 %fusion.13 = f32[24,16,384]{2,0,1:T(8,128)} fusion(f32[16,384]{1,0:T(8,128)S(1)} %bitcast.139, f32[24,16]{0,1:T(8,128)S(1)} %copy-done.19, f32[16]{0:T(128)S(1)} %copy-done.25, bf16[384,16,92]{0,2,1:T(8,128)(2,1)S(1)} %reshape.162, f32[24,16,24]{0,1,2:T(8,128)S(1)} %bitcast_add_fusion.2), kind=kOutput, calls=%fused_computation.17 | convolution fusion | flops 43057152 | bytes 1114624 | tf_op jit(solution)/shard_map/rhp,nhp->rhn/dot_general | solution.py:114
  37.4 1.9 %fusion.42 = (f32[24,16]{0,1:T(8,128)S(1)}, f32[24,16,384]{2,0,1:T(8,128)S(1)}) fusion(f32[24,16,384]{2,0,1:T(8,128)} %fusion.13, bf16[16,24,384]{2,0,1:T(8,128)(2,1)} %fusion.35, f32[24,384]{1,0:T(8,128)S(1)} %copy-done.18, f32[16]{0:T(128)S(1)} %copy-done.28, pred[384]{0:T(512)(128)(4,1)S(1)} %copy-done.26, bf16[384,16,92]{0,2,1:T(8,128)(2,1)S(1)} %reshape.162, ...), kind=kOutput, calls=%fused_computation.128 | convolution fusion | flops 6193535 | bytes 1776132 | tf_op jit(solution)/shard_map/sub | solution.py:362
  40.0 1.0 %copy-done.1 = bf16[24,384,128]{2,1,0:T(8,128)(2,1)S(1)} copy-done((bf16[24,384,128]{2,1,0:T(8,128)(2,1)S(1)}, bf16[24,384,128]{2,1,0:T(8,128)(2,1)}, u32[]{:S(2)}) %copy-start.1) | copy-done | bytes 2359320
  41.0 1.2 %fusion.20 = f32[24,16,128]{2,1,0:T(8,128)} fusion(bf16[24,384,128]{2,1,0:T(8,128)(2,1)S(1)} %copy-done.1, bf16[24,16,384]{2,0,1:T(8,128)(2,1)S(1)} %divide_convert_fusion), kind=kOutput, calls=%fused_computation.44 | convolution fusion | flops 37748736 | bytes 2850816 | tf_op jit(solution)/shard_map/rhj,rjc->rhc/dot_general | solution.py:378
  42.2 0.8 %copy.138 = f32[24,16,16]{2,0,1:T(8,128)} copy(f32[24,16,16]{0,2,1:T(8,128)S(1)} %convolution_bitcast_fusion.1) | data formatting | bytes 49152 | tf_op jit(solution)/shard_map/rhn,nhc->rhc/transpose | solution.py:364
  44.1 1.7 %copy.140 = f32[24,16,12]{2,0,1:T(8,128)} copy(f32[24,16,12]{0,1,2:T(8,128)} %add_sqrt_fusion) | data formatting | bytes 36864 | tf_op jit(solution)/shard_map/sqrt | solution.py:135
  45.8 0.9 %copy.139 = f32[24,16,36]{2,0,1:T(8,128)} copy(f32[24,16,36]{0,1,2:T(8,128)S(1)} %bitcast.126) | data formatting | bytes 110592 | tf_op jit(solution)/shard_map/reshape | solution.py:137
  46.7 2.0 %convolution_bitcast_fusion.4 = f32[24,384]{1,0:T(8,128)S(1)} fusion(bf16[16,64,384]{2,1,0:T(8,128)(2,1)} %param.32, f32[24,16,12]{2,0,1:T(8,128)} %copy.140, f32[24,16,36]{2,0,1:T(8,128)} %copy.139, f32[24,16,16]{2,0,1:T(8,128)} %copy.138), kind=kOutput, calls=%fused_computation.25 | convolution fusion | flops 113295360 | bytes 921600 | tf_op jit(solution)/shard_map/rhf,hfd->rd/dot_general | solution.py:139
  48.8 1.9 %fusion.43 = (f32[24]{0:T(128)S(1)}, f32[24,384]{1,0:T(8,128)S(1)}) fusion(f32[24,384]{1,0:T(8,128)S(1)} %convolution_bitcast_fusion.4, bf16[16,128,384]{2,1,0:T(8,128)(2,1)S(1)} %copy-done.9, f32[24,16,128]{2,1,0:T(8,128)} %fusion.20, bf16[24,384]{1,0:T(8,128)(2,1)} %param.21), kind=kOutput, calls=%fused_computation.129 | convolution fusion | flops 226529248 | bytes 1861728 | tf_op jit(solution)/shard_map/rhc,hcd->rd/dot_general | solution.py:381
  53.7 1.1 %collective-permute-done.5 = bf16[1,24,128]{2,1,0:T(8,128)(2,1)S(1)} collective-permute-done((bf16[1,24,128]{2,1,0:T(8,128)(2,1)S(1)}, bf16[1,24,128]{2,1,0:T(8,128)(2,1)S(1)}, u32[]{:S(2)}, u32[]{:S(2)}) %collective-permute-start.5) | collective-permute-done | bytes 6176 | tf_op jit(solution)/shard_map/ppermute | solution.py:145
  54.8 1.4 %collective-permute-start.6 = (bf16[2,24,128]{2,1,0:T(8,128)(2,1)S(1)}, bf16[2,24,128]{2,1,0:T(8,128)(2,1)S(1)}, u32[]{:S(2)}, u32[]{:S(2)}) collective-permute-start(bf16[2,24,128]{2,1,0:T(8,128)(2,1)S(1)} %pad_maximum_fusion.2), channel_id=1, source_target_pairs={{0,12},{1,13},{2,14},{3,15},{4,8},{5,9},{6,10},{7,11},{8,4},{9,5},... | collective-permute-start | bytes 36872 | tf_op jit(solution)/shard_map/ppermute | solution.py:145
  56.9 2.3 %collective-permute-start.8 = (bf16[2,24,128]{2,1,0:T(8,128)(2,1)S(1)}, bf16[2,24,128]{2,1,0:T(8,128)(2,1)S(1)}, u32[]{:S(2)}, u32[]{:S(2)}) collective-permute-start(bf16[2,24,128]{2,1,0:T(8,128)(2,1)S(1)} %pad_maximum_fusion.2), channel_id=1, source_target_pairs={{0,4},{1,5},{2,6},{3,7},{4,0},{5,1},{6,2},{7,3},{8,12},{9,13},{10,... | collective-permute-start | bytes 36872 | tf_op jit(solution)/shard_map/ppermute | solution.py:145
  59.2 1.1 %collective-permute-done.6 = bf16[2,24,128]{2,1,0:T(8,128)(2,1)S(1)} collective-permute-done((bf16[2,24,128]{2,1,0:T(8,128)(2,1)S(1)}, bf16[2,24,128]{2,1,0:T(8,128)(2,1)S(1)}, u32[]{:S(2)}, u32[]{:S(2)}) %collective-permute-start.6) | collective-permute-done | bytes 12320 | tf_op jit(solution)/shard_map/ppermute | solution.py:145
  61.0 1.3 %bitcast_add_fusion.3 = f32[3,24]{1,0:T(4,128)} fusion(f32[24,1,3]{0,2,1:T(4,128)S(1)} %copy.156, f32[3,384]{1,0:T(4,128)} %param.24, s32[]{:T(128)S(6)} %select_n.51), kind=kLoop, calls=%fused_computation.104 | loop fusion | flops 72 | bytes 868 | tf_op jit(solution)/shard_map/add | solution.py:93
  63.0 1.7 %copy-done.2 = bf16[24,384,128]{2,1,0:T(8,128)(2,1)S(1)} copy-done((bf16[24,384,128]{2,1,0:T(8,128)(2,1)S(1)}, bf16[24,384,128]{2,1,0:T(8,128)(2,1)}, u32[]{:S(2)}) %copy-start.2) | copy-done | bytes 2359320
  64.7 9.5 %shard_map.228 = bf16[24,384,128]{2,1,0:T(8,128)(2,1)} custom-call(s32[384]{0:T(512)S(1)} %copy-done.3, bf16[24,384,128]{2,1,0:T(8,128)(2,1)S(1)} %copy-done.2, bf16[6,4,128]{2,1,0:T(4,128)(2,1)S(1)} %bitcast.123, s32[1,384]{1,0:T(1,128)S(1)} %broadcast_in_dim.23.live_row_ref, f32[1,128]{1,0:T(1,128)S(1)} %bitcast.124, bf16[128,256]{1,0:T(8,128)(2,1)S(1)} %copy-done.5, ...), custom_call_target="tpu_custom_call" | custom-call | flops 3019898880 | bytes 4718592 | tf_op jit(solution)/shard_map/pallas_call | solution.py:259
  (163 shorter events, 14.5 us)
Async XLA Ops:
  0.6 25.6 %copy-start = (bf16[384,16,132]{0,1,2:T(8,128)(2,1)S(1)}, bf16[384,16,132]{0,1,2:T(8,128)(2,1)}, u32[]{:S(2)}) copy-start(bf16[384,16,132]{0,1,2:T(8,128)(2,1)} %param.28) | copy-start | bytes 4866052
  0.6 12.8 %copy-start.11 = (bf16[24,384]{1,0:T(8,128)(2,1)S(1)}, bf16[24,384]{1,0:T(8,128)(2,1)}, u32[]{:S(2)}) copy-start(bf16[24,384]{1,0:T(8,128)(2,1)} %param.21) | copy-start | bytes 55300
  0.7 21.6 %copy-start.3 = (s32[384]{0:T(512)S(1)}, s32[384]{0:T(512)}, u32[]{:S(2)}) copy-start(s32[384]{0:T(512)} %live_ref.1) | copy-start | bytes 4612
  0.7 21.5 %copy-start.17 = (f32[3,384]{1,0:T(4,128)S(1)}, f32[3,384]{1,0:T(4,128)}, u32[]{:S(2)}) copy-start(f32[3,384]{1,0:T(4,128)} %param.24) | copy-start | bytes 13828
  0.7 12.8 %collective-permute-start = (bf16[1,24,384]{2,1,0:T(8,128)(2,1)}, bf16[1,24,384]{2,1,0:T(8,128)(2,1)S(1)}, u32[]{:S(2)}, u32[]{:S(2)}) collective-permute-start(bf16[1,24,384]{2,1,0:T(8,128)(2,1)} %bitcast.135), channel_id=1, source_target_pairs={{0,2},{1,3},{2,0},{3,1},{4,6},{5,7},{6,4},{7,5},{8,10},{9,11},{10,... | collective-permute-start | bytes 55304 | tf_op jit(solution)/shard_map/ppermute | solution.py:145
  13.5 6.2 %collective-permute-start.1 = (bf16[2,24,384]{2,1,0:T(8,128)(2,1)S(1)}, bf16[2,24,384]{2,1,0:T(8,128)(2,1)S(1)}, u32[]{:S(2)}, u32[]{:S(2)}) collective-permute-start(bf16[2,24,384]{2,1,0:T(8,128)(2,1)S(1)} %pad_maximum_fusion.1), channel_id=1, source_target_pairs={{0,12},{1,13},{2,14},{3,15},{4,8},{5,9},{6,10},{7,11},{8,4},{9,5},... | collective-permute-start | bytes 110600 | tf_op jit(solution)/shard_map/ppermute | solution.py:145
  17.2 4.9 %collective-permute-start.2 = (bf16[2,24,384]{2,1,0:T(8,128)(2,1)S(1)}, bf16[2,24,384]{2,1,0:T(8,128)(2,1)S(1)}, u32[]{:S(2)}, u32[]{:S(2)}) collective-permute-start(bf16[2,24,384]{2,1,0:T(8,128)(2,1)S(1)} %pad_maximum_fusion.1), channel_id=1, source_target_pairs={{0,8},{1,9},{2,10},{3,11},{4,12},{5,13},{6,14},{7,15},{8,0},{9,1},... | collective-permute-start | bytes 110600 | tf_op jit(solution)/shard_map/ppermute | solution.py:145
  17.2 4.9 %collective-permute-start.3 = (bf16[2,24,384]{2,1,0:T(8,128)(2,1)S(1)}, bf16[2,24,384]{2,1,0:T(8,128)(2,1)S(1)}, u32[]{:S(2)}, u32[]{:S(2)}) collective-permute-start(bf16[2,24,384]{2,1,0:T(8,128)(2,1)S(1)} %pad_maximum_fusion.1), channel_id=1, source_target_pairs={{0,4},{1,5},{2,6},{3,7},{4,0},{5,1},{6,2},{7,3},{8,12},{9,13},{10,... | collective-permute-start | bytes 110600 | tf_op jit(solution)/shard_map/ppermute | solution.py:145
  22.0 3.7 %collective-permute-start.4 = (bf16[8,24,384]{2,1,0:T(8,128)(2,1)S(1)}, bf16[8,24,384]{2,1,0:T(8,128)(2,1)S(1)}, u32[]{:S(2)}, u32[]{:S(2)}) collective-permute-start(bf16[8,24,384]{2,1,0:T(8,128)(2,1)S(1)} %constant_dynamic-update-slice_fusion), channel_id=1, source_target_pairs={{0,1},{1,0},{2,3},{3,2},{4,5},{5,4},{6,7},{7,6},{8,9},{9,8},{10,11... | collective-permute-start | bytes 442376 | tf_op jit(solution)/shard_map/ppermute | solution.py:145
  22.2 7.5 %copy-start.20 = (f32[24,3]{0,1:T(4,128)}, f32[24,3]{0,1:T(4,128)S(1)}, u32[]{:S(2)}) copy-start(f32[24,3]{0,1:T(4,128)S(1)} %dynamic-slice_bitcast_fusion) | copy-start | bytes 868
  27.6 1.7 %copy-start.8 = (f32[384,16,132]{0,2,1:T(8,128)}, f32[384,16,132]{0,2,1:T(8,128)S(1)}, u32[]{:S(2)}) copy-start(f32[384,16,132]{0,2,1:T(8,128)S(1)} %fusion.1) | copy-start | bytes 9732100
  34.4 2.9 %copy-start.18 = (f32[24,384]{1,0:T(8,128)S(1)}, f32[24,384]{1,0:T(8,128)}, u32[]{:S(2)}) copy-start(f32[24,384]{1,0:T(8,128)} %compare_convert_fusion) | copy-start | bytes 110596
  34.4 2.9 %copy-start.26 = (pred[384]{0:T(512)(128)(4,1)S(1)}, pred[384]{0:T(512)(128)(4,1)}, u32[]{:S(2)}) copy-start(pred[384]{0:T(512)(128)(4,1)} %get-tuple-element.27) | copy-start | bytes 1156
  34.5 2.9 %copy-start.28 = (f32[16]{0:T(128)S(1)}, f32[16]{0:T(128)}, u32[]{:S(2)}) copy-start(f32[16]{0:T(128)} %param.31) | copy-start | bytes 196
  41.0 2.2 %copy-start.21 = (f32[24,3]{0,1:T(4,128)S(1)}, f32[24,3]{0,1:T(4,128)}, u32[]{:S(2)}) copy-start(f32[24,3]{0,1:T(4,128)} %copy-done.20) | copy-start | bytes 868
  43.3 5.5 %copy-start.9 = (bf16[16,128,384]{2,1,0:T(8,128)(2,1)S(1)}, bf16[16,128,384]{2,1,0:T(8,128)(2,1)}, u32[]{:S(2)}) copy-start(bf16[16,128,384]{2,1,0:T(8,128)(2,1)} %param.33) | copy-start | bytes 4718596
  46.7 4.2 %copy-start.24 = (f32[384]{0:T(512)S(1)}, f32[384]{0:T(512)}, u32[]{:S(2)}) copy-start(f32[384]{0:T(512)} %param.34) | copy-start | bytes 4612
  46.7 4.3 %copy-start.14 = (bf16[384,128]{1,0:T(8,128)(2,1)S(1)}, bf16[384,128]{1,0:T(8,128)(2,1)}, u32[]{:S(2)}) copy-start(bf16[384,128]{1,0:T(8,128)(2,1)} %param.37) | copy-start | bytes 294916
  46.7 5.0 %copy-start.15 = (bf16[384,128]{1,0:T(8,128)(2,1)S(1)}, bf16[384,128]{1,0:T(8,128)(2,1)}, u32[]{:S(2)}) copy-start(bf16[384,128]{1,0:T(8,128)(2,1)} %param.36) | copy-start | bytes 294916
  46.7 5.2 %copy-start.23 = (bf16[384,6]{0,1:T(8,128)(2,1)S(1)}, bf16[384,6]{0,1:T(8,128)(2,1)}, u32[]{:S(2)}) copy-start(bf16[384,6]{0,1:T(8,128)(2,1)} %param.35) | copy-start | bytes 13828
  46.7 5.3 %copy-start.27 = (f32[24]{0:T(128)S(1)}, f32[24]{0:T(128)}, u32[]{:S(2)}) copy-start(f32[24]{0:T(128)} %dynamic_slice.22) | copy-start | bytes 292
  48.8 3.8 %copy-start.22 = (f32[3,3]{1,0:T(4,128)S(1)}, f32[3,3]{1,0:T(4,128)}, u32[]{:S(2)}) copy-start(f32[3,3]{1,0:T(4,128)} %fusion.37) | copy-start | bytes 112
  48.8 14.2 %copy-start.4 = (bf16[256,256]{1,0:T(8,128)(2,1)S(1)}, bf16[256,256]{1,0:T(8,128)(2,1)}, u32[]{:S(2)}) copy-start(bf16[256,256]{1,0:T(8,128)(2,1)} %middle_ref.1) | copy-start | bytes 393220
  48.8 14.2 %copy-start.5 = (bf16[128,256]{1,0:T(8,128)(2,1)S(1)}, bf16[128,256]{1,0:T(8,128)(2,1)}, u32[]{:S(2)}) copy-start(bf16[128,256]{1,0:T(8,128)(2,1)} %hidden_ref.1) | copy-start | bytes 196612
  48.8 14.2 %copy-start.6 = (bf16[256,128]{1,0:T(8,128)(2,1)S(1)}, bf16[256,128]{1,0:T(8,128)(2,1)}, u32[]{:S(2)}) copy-start(bf16[256,128]{1,0:T(8,128)(2,1)} %back_ref.1) | copy-start | bytes 196612
  48.8 14.2 %copy-start.7 = (f32[128]{0:T(128)S(1)}, f32[128]{0:T(128)}, u32[]{:S(2)}) copy-start(f32[128]{0:T(128)} %param.38) | copy-start | bytes 1540
  51.0 23.2 %copy-start.10 = (bf16[24,384]{1,0:T(8,128)(2,1)}, bf16[24,384]{1,0:T(8,128)(2,1)S(1)}, u32[]{:S(2)}) copy-start(bf16[24,384]{1,0:T(8,128)(2,1)S(1)} %multiply_convert_fusion) | copy-start | bytes 55300
  51.2 3.6 %collective-permute-start.5 = (bf16[1,24,128]{2,1,0:T(8,128)(2,1)S(1)}, bf16[1,24,128]{2,1,0:T(8,128)(2,1)S(1)}, u32[]{:S(2)}, u32[]{:S(2)}) collective-permute-start(bf16[1,24,128]{2,1,0:T(8,128)(2,1)S(1)} %get-tuple-element.48), channel_id=1, source_target_pairs={{0,2},{1,3},{2,0},{3,1},{4,6},{5,7},{6,4},{7,5},{8,10},{9,11},{10,... | collective-permute-start | bytes 18440 | tf_op jit(solution)/shard_map/ppermute | solution.py:145
  54.8 5.5 %collective-permute-start.6 = (bf16[2,24,128]{2,1,0:T(8,128)(2,1)S(1)}, bf16[2,24,128]{2,1,0:T(8,128)(2,1)S(1)}, u32[]{:S(2)}, u32[]{:S(2)}) collective-permute-start(bf16[2,24,128]{2,1,0:T(8,128)(2,1)S(1)} %pad_maximum_fusion.2), channel_id=1, source_target_pairs={{0,12},{1,13},{2,14},{3,15},{4,8},{5,9},{6,10},{7,11},{8,4},{9,5},... | collective-permute-start | bytes 36872 | tf_op jit(solution)/shard_map/ppermute | solution.py:145
  56.2 4.6 %collective-permute-start.7 = (bf16[2,24,128]{2,1,0:T(8,128)(2,1)S(1)}, bf16[2,24,128]{2,1,0:T(8,128)(2,1)S(1)}, u32[]{:S(2)}, u32[]{:S(2)}) collective-permute-start(bf16[2,24,128]{2,1,0:T(8,128)(2,1)S(1)} %pad_maximum_fusion.2), channel_id=1, source_target_pairs={{0,8},{1,9},{2,10},{3,11},{4,12},{5,13},{6,14},{7,15},{8,0},{9,1},... | collective-permute-start | bytes 36872 | tf_op jit(solution)/shard_map/ppermute | solution.py:145
  56.9 4.1 %collective-permute-start.8 = (bf16[2,24,128]{2,1,0:T(8,128)(2,1)S(1)}, bf16[2,24,128]{2,1,0:T(8,128)(2,1)S(1)}, u32[]{:S(2)}, u32[]{:S(2)}) collective-permute-start(bf16[2,24,128]{2,1,0:T(8,128)(2,1)S(1)} %pad_maximum_fusion.2), channel_id=1, source_target_pairs={{0,4},{1,5},{2,6},{3,7},{4,0},{5,1},{6,2},{7,3},{8,12},{9,13},{10,... | collective-permute-start | bytes 36872 | tf_op jit(solution)/shard_map/ppermute | solution.py:145
  61.0 2.0 %collective-permute-start.9 = (bf16[8,24,128]{2,1,0:T(8,128)(2,1)S(1)}, bf16[8,24,128]{2,1,0:T(8,128)(2,1)S(1)}, u32[]{:S(2)}, u32[]{:S(2)}) collective-permute-start(bf16[8,24,128]{2,1,0:T(8,128)(2,1)S(1)} %constant_dynamic-update-slice_fusion.21.rest_0_), channel_id=1, source_target_pairs={{0,1},{1,0},{2,3},{3,2},{4,5},{5,4},{6,7},{7,6},{8,9},{9,8},{10,11... | collective-permute-start | bytes 147464 | tf_op jit(solution)/shard_map/ppermute | solution.py:145
  (9 other events, 12.0 us)

commit v2 on v1

--- a/solution.py
+++ b/solution.py
@@ -294,6 +294,476 @@
     )
 
 
+def dot(left, right):
+    return jnp.dot(left, right, preferred_element_type=jnp.float32)
+
+
+def dot_rows(left, right, precision=None):
+    return lax.dot_general(
+        left, right, (((1,), (1,)), ((), ())), preferred_element_type=jnp.float32, precision=precision
+    )
+
+
+def head_mask(heads, lanes):
+    head = lax.broadcasted_iota(jnp.int32, (heads, lanes), 0)
+    lane = lax.broadcasted_iota(jnp.int32, (heads, lanes), 1)
+    return lax.rem(lane, heads) == head
+
+
+def as_column(row):
+    size = row.shape[1]
+    return jnp.sum(jnp.where(head_mask(size, size), row, 0.0), axis=1, keepdims=True)
+
+
+def halves(values):
+    high = values.astype(jnp.bfloat16)
+    return high, (values - high.astype(jnp.float32)).astype(jnp.bfloat16)
+
+
+def point_rows(weight_ref, offset, npoints, coord):
+    return jnp.concatenate([weight_ref[offset + 3 * p + coord] for p in range(npoints)], 0)
+
+
+def turn(parts, rot, shift):
+    return [
+        rot[c][0] * parts[0] + rot[c][1] * parts[1] + rot[c][2] * parts[2] + shift[c]
+        for c in range(3)
+    ]
+
+
+def query_kernel(
+    chain_ref,
+    pair_ref,
+    single_ref,
+    weight_ref,
+    bias_ref,
+    rot_ref,
+    trans_ref,
+    chain_row_ref,
+    distance_ref,
+    offset_ref,
+    query_ref,
+    base_ref,
+    frame_ref,
+    table_ref,
+):
+    rows, total, _ = pair_ref.shape
+    heads = weight_ref.shape[1]
+    me = lax.axis_index("res")
+    table_ref[...] = jnp.zeros_like(table_ref)
+    for c in range(3):
+        for d in range(3):
+            table_ref[pl.ds(3 * c + d, 1), :] = rot_ref[c, pl.ds(d, 1), :]
+        table_ref[pl.ds(9 + c, 1), :] = trans_ref[pl.ds(c, 1), :]
+    row = lax.broadcasted_iota(jnp.int32, (rows, total), 0)
+    column = lax.broadcasted_iota(jnp.int32, (rows, total), 1)
+    chosen = jnp.where(column == row + me * rows, 1.0, 0.0)
+    frame = dot_rows(chosen, table_ref[...], HIGHEST)
+    frame_ref[...] = frame
+    rot = [[frame[:, 3 * c + d : 3 * c + d + 1] for d in range(3)] for c in range(3)]
+    shift = [frame[:, 9 + c : 10 + c] for c in range(3)]
+
+    weight = 0.5 * math.sqrt(2.0 / (9.0 * PQ)) * as_column(distance_ref[...])
+    chain_offset = as_column(offset_ref[...])
+    single = single_ref[...]
+    scalar_rows = weight_ref[pl.ds(0, HEAD_FEATURES)].reshape(HEAD_FEATURES * heads, -1)
+    scalar = dot_rows(single, scalar_rows).astype(jnp.bfloat16).astype(jnp.float32)
+    scalar = scalar * (1.0 / math.sqrt(HEAD_FEATURES))
+    lanes = scalar.shape[1]
+    spread = jnp.where(head_mask(heads, lanes)[None], scalar[:, None, :], 0.0)
+    query_ref[:, pl.ds(0, lanes)] = spread.reshape(rows * heads, lanes).astype(jnp.bfloat16)
+    points = [
+        dot_rows(single, point_rows(weight_ref, 3 * HEAD_FEATURES, PQ, c)) for c in range(3)
+    ]
+    points = turn(points, rot, shift)
+    width = PQ * heads
+    square = jnp.zeros((rows, heads, width), jnp.float32)
+    for c in range(3):
+        spread = jnp.where(head_mask(heads, width)[None], points[c][:, None, :], 0.0)
+        square = square + spread * spread
+        rest = spread * (2.0 * weight)[None]
+        for term in range(3):
+            part = rest.astype(jnp.bfloat16)
+            rest = rest - part.astype(jnp.float32)
+            at = lanes + (3 * term + c) * width
+            query_ref[:, pl.ds(at, width)] = part.reshape(rows * heads, width)
+    square = jnp.sum(square, axis=-1, keepdims=True)
+    for r in range(rows):
+        bias = dot_rows(bias_ref[...], pair_ref[r]).astype(jnp.bfloat16).astype(jnp.float32)
+        within = jnp.where(chain_row_ref[...] == chain_ref[me * rows + r], 1.0, 0.0)
+        base_ref[r] = LOGIT_FACTOR * (bias + chain_offset * within - weight * square[r])
+
+
+def attention_kernel(
+    offsets,
+    held_ref,
+    other_ref,
+    weight_ref,
+    query_ref,
+    base_ref,
+    frame_ref,
+    rot_ref,
+    trans_ref,
+    present_ref,
+    distance_ref,
+    pair_ref,
+    single_ref,
+    local_ref,
+    pair_weight_ref,
+    gain_ref,
+    left_ref,
+    right_ref,
+    out_ref,
+    left_out_ref,
+    right_out_ref,
+    every_ref,
+    pair_sum_ref,
+):
+    rows, total, feats = pair_ref.shape
+    heads = weight_ref.shape[1]
+    me = lax.axis_index("res")
+    for ref, step in ((held_ref, 0), (other_ref, 1)):
+        for e, o in enumerate(offsets):
+            owner = me ^ (o ^ step)
+            every_ref[pl.ds(pl.multiple_of(owner * rows, 8), rows), :] = ref[e].astype(jnp.float32)
+    every = every_ref[...].astype(jnp.bfloat16)
+    rot = [[rot_ref[c, pl.ds(d, 1), :] for d in range(3)] for c in range(3)]
+    shift = [trans_ref[pl.ds(c, 1), :] for c in range(3)]
+
+    key_at, value_at = HEAD_FEATURES, 2 * HEAD_FEATURES
+    key_rows = weight_ref[pl.ds(key_at, HEAD_FEATURES)].reshape(HEAD_FEATURES * heads, -1)
+    keys = dot_rows(key_rows, every).astype(jnp.bfloat16)
+    offset = 3 * HEAD_FEATURES + 3 * PQ
+    points = [dot_rows(point_rows(weight_ref, offset, PQ, c), every) for c in range(3)]
+    points = [p.astype(jnp.bfloat16) for p in turn(points, rot, shift)]
+    square = sum(jnp.square(p.astype(jnp.float32)) for p in points)
+    square = jnp.sum(square.reshape(PQ, heads, total), axis=0)
+    keys = jnp.concatenate([keys] + 3 * points, 0)
+    weight = 0.5 * LOGIT_FACTOR * math.sqrt(2.0 / (9.0 * PQ)) * as_column(distance_ref[...])
+    logits = dot(query_ref[...], keys).reshape(rows, heads, total)
+    logits = LOGIT_FACTOR * logits + base_ref[...] - (weight * square)[None]
+    present = present_ref[...] > 0
+    logits = jnp.where(present[None], logits, -1000000000.0)
+    logits = logits.reshape(rows * heads, total)
+    exponent = jnp.exp(logits - jnp.max(logits, axis=-1, keepdims=True))
+    attention = (exponent / jnp.sum(exponent, axis=-1, keepdims=True)).astype(jnp.bfloat16)
+
+    for r in range(rows):
+        pair_sum_ref[pl.ds(r * heads, heads), :] = dot(
+            attention[r * heads : (r + 1) * heads], pair_ref[r]
+        )
+
+    def own_head(values):
+        lanes = values.shape[0]
+        mixed = dot_rows(attention, values).reshape(rows, heads, lanes)
+        return jnp.sum(jnp.where(head_mask(heads, lanes)[None], mixed, 0.0), axis=1)
+
+    value_rows = weight_ref[pl.ds(value_at, HEAD_FEATURES)].reshape(HEAD_FEATURES * heads, -1)
+    scalar_out = own_head(dot_rows(value_rows, every).astype(jnp.bfloat16))
+    offset = 3 * HEAD_FEATURES + 6 * PQ
+    points = [dot_rows(point_rows(weight_ref, offset, PV, c), every) for c in range(3)]
+    points = [own_head(p.astype(jnp.bfloat16)) for p in turn(points, rot, shift)]
+    frame = frame_ref[...]
+    centred = [points[c] - frame[:, 9 + c : 10 + c] for c in range(3)]
+    local = [
+        sum(frame[:, 3 * c + d : 3 * c + d + 1] * centred[c] for c in range(3)) for d in range(3)
+    ]
+    norm = jnp.sqrt(sum(jnp.square(v) for v in local) + 1.0)
+
+    def product(values, rows_of_weight):
+        return dot(jnp.concatenate(halves(values), 0), rows_of_weight)
+
+    first = HEAD_FEATURES * heads
+    update = product(scalar_out, local_ref[pl.ds(0, HEAD_FEATURES)].reshape(first, -1))
+    for c in range(3):
+        update = update + product(local[c], point_rows(local_ref, HEAD_FEATURES, PV, c))
+    norm_rows = local_ref[pl.ds(HEAD_FEATURES + 3 * PV, PV)].reshape(PV * heads, -1)
+    update = update + product(norm, norm_rows)
+    pair_sum = jnp.concatenate(
+        [pair_sum_ref[pl.ds(h, rows, stride=heads), :] for h in range(heads)], 1
+    )
+    update = update + product(pair_sum, pair_weight_ref[...])
+    values = single_ref[...].astype(jnp.float32) + update[:rows] + update[rows:]
+    single_out = layer_norm(values, gain_ref[...]).astype(jnp.bfloat16)
+    out_ref[...] = single_out
+    left_out_ref[...] = dot(single_out, left_ref[...]).astype(jnp.bfloat16)
+    right_out_ref[...] = dot(single_out, right_ref[...]).astype(jnp.bfloat16)
+
+
+def frame_kernel(
+    step_ref,
+    live_ref,
+    single_ref,
+    velocity_ref,
+    rot_ref,
+    trans_ref,
+    rot_out_ref,
+    trans_out_ref,
+    table_ref,
+):
+    rows = single_ref.shape[0]
+    total = rot_ref.shape[2]
+    me = lax.axis_index("res")
+    table_ref[...] = jnp.zeros_like(table_ref)
+    for c in range(3):
+        for d in range(3):
+            table_ref[pl.ds(3 * c + d, 1), :] = rot_ref[c, pl.ds(d, 1), :]
+        table_ref[pl.ds(9 + c, 1), :] = trans_ref[pl.ds(c, 1), :]
+    table_ref[pl.ds(12, 1), :] = jnp.where(live_ref[...] > 0, 1.0, 0.0)
+    row = lax.broadcasted_iota(jnp.int32, (rows, total), 0)
+    column = lax.broadcasted_iota(jnp.int32, (rows, total), 1)
+    chosen = jnp.where(column == row + me * rows, 1.0, 0.0)
+    frame = dot_rows(table_ref[...], chosen, HIGHEST)
+    motion = dot_rows(velocity_ref[...], single_ref[...])
+    live = frame[12:13]
+    ratio = 1.0 / jnp.full((1, rows), STEPS - step_ref[0], jnp.int32).astype(jnp.float32)
+    x, y, z = [ratio * jnp.tanh(motion[c : c + 1]) * live for c in range(3)]
+    velocity = [ratio * motion[3 + c : 4 + c] * live for c in range(3)]
+    angle_sq = x * x + y * y + z * z
+    coefs = [jnp.zeros_like(angle_sq) for _ in range(3)]
+    powers = jnp.ones_like(angle_sq)
+    for order in range(8):
+        parity = (-1.0) ** order
+        coefs = [
+            coef + powers * (parity / float(math.factorial(2 * order + 1 + k)))
+            for k, coef in enumerate(coefs)
+        ]
+        powers = powers * angle_sq
+    zero = jnp.zeros_like(x)
+    cross = [[zero, -z, y], [z, zero, -x], [-y, x, zero]]
+    square = [[sum(cross[a][b] * cross[b][c] for b in range(3)) for c in range(3)] for a in range(3)]
+    one = [[jnp.ones_like(x) if a == b else zero for b in range(3)] for a in range(3)]
+
+    def series(first, second):
+        return [
+            [one[a][b] + first * cross[a][b] + second * square[a][b] for b in range(3)]
+            for a in range(3)
+        ]
+
+    turned, jacobian = series(coefs[0], coefs[1]), series(coefs[1], coefs[2])
+    rot = [[frame[3 * a + b : 3 * a + b + 1] for b in range(3)] for a in range(3)]
+    moved = [sum(jacobian[a][b] * velocity[b] for b in range(3)) for a in range(3)]
+    for a in range(3):
+        for c in range(3):
+            rot_out_ref[a, pl.ds(c, 1), :] = sum(rot[a][b] * turned[b][c] for b in range(3))
+        trans_out_ref[pl.ds(a, 1), :] = frame[9 + a : 10 + a] + sum(
+            rot[a][b] * moved[b] for b in range(3)
+        )
+
+
+def in_vmem(count):
+    return [pl.BlockSpec(memory_space=pltpu.VMEM)] * count
+
+
+def attend(
+    single,
+    pair,
+    rotations,
+    translations,
+    residue_chain_index,
+    residue_move_mask,
+    timestep,
+    single_projection_weight,
+    head_bias_weight,
+    head_distance_weight,
+    chain_logit_offset,
+    local_output_weight,
+    pair_output_weight,
+    single_norm_gain,
+    frame_velocity_weight,
+    left_pair_weight,
+    right_pair_weight,
+):
+    rows, total, feats = pair.shape
+    heads = single_projection_weight.shape[1]
+    width = single.shape[1]
+    offsets, (held, other) = gather_blocks(single, total // rows)
+    weight = jnp.transpose(single_projection_weight, (2, 1, 0))
+    local_weight = jnp.transpose(local_output_weight, (1, 0, 2))
+    distance = head_distance_weight[None]
+    depth = heads * (HEAD_FEATURES + 9 * PQ)
+    query, base, frame = pl.pallas_call(
+        query_kernel,
+        in_specs=[pl.BlockSpec(memory_space=pltpu.SMEM)] + in_vmem(9),
+        out_specs=tuple(in_vmem(3)),
+        out_shape=(
+            jax.ShapeDtypeStruct((rows * heads, depth), jnp.bfloat16),
+            jax.ShapeDtypeStruct((rows, heads, total), jnp.float32),
+            jax.ShapeDtypeStruct((rows, 16), jnp.float32),
+        ),
+        scratch_shapes=[pltpu.VMEM((16, total), jnp.float32)],
+        compiler_params=pltpu.CompilerParams(vmem_limit_bytes=24 * 1024 * 1024),
+        cost_estimate=pl.CostEstimate(flops=10**9, bytes_accessed=6 * 10**6, transcendentals=0),
+    )(
+        residue_chain_index,
+        pair,
+        single,
+        weight,
+        jnp.transpose(head_bias_weight),
+        rotations,
+        translations,
+        residue_chain_index[None],
+        distance,
+        chain_logit_offset[None],
+    )
+    single_out, left_proj, right_proj = pl.pallas_call(
+        functools.partial(attention_kernel, offsets),
+        in_specs=in_vmem(17),
+        out_specs=tuple(in_vmem(3)),
+        out_shape=(
+            jax.ShapeDtypeStruct((rows, width), jnp.bfloat16),
+            jax.ShapeDtypeStruct((rows, feats), jnp.bfloat16),
+            jax.ShapeDtypeStruct((rows, feats), jnp.bfloat16),
+        ),
+        scratch_shapes=[
+            pltpu.VMEM((total, width), jnp.float32),
+            pltpu.VMEM((rows * heads, feats), jnp.float32),
+        ],
+        compiler_params=pltpu.CompilerParams(vmem_limit_bytes=40 * 1024 * 1024),
+        cost_estimate=pl.CostEstimate(flops=2 * 10**9, bytes_accessed=10**7, transcendentals=0),
+    )(
+        held,
+        other,
+        weight,
+        query,
+        base,
+        frame,
+        rotations,
+        translations,
+        residue_move_mask[None],
+        distance,
+        pair,
+        single,
+        local_weight,
+        pair_output_weight.reshape(heads * feats, width),
+        single_norm_gain[None],
+        left_pair_weight,
+        right_pair_weight,
+    )
+    velocity_rows = jnp.pad(jnp.transpose(frame_velocity_weight), ((0, 2), (0, 0)))
+    rot_out, trans_out = pl.pallas_call(
+        frame_kernel,
+        in_specs=[pl.BlockSpec(memory_space=pltpu.SMEM)] + in_vmem(5),
+        out_specs=tuple(in_vmem(2)),
+        out_shape=(
+            jax.ShapeDtypeStruct((3, 3, rows), jnp.float32),
+            jax.ShapeDtypeStruct((3, rows), jnp.float32),
+        ),
+        scratch_shapes=[pltpu.VMEM((16, total), jnp.float32)],
+        cost_estimate=pl.CostEstimate(flops=10**6, bytes_accessed=10**5, transcendentals=0),
+    )(
+        timestep,
+        residue_move_mask[None],
+        single_out,
+        velocity_rows,
+        rotations,
+        translations,
+    )
+    return single_out, rot_out, trans_out, left_proj, right_proj
+
+
+def attend_split(
+    single,
+    pair,
+    rotations,
+    translations,
+    residue_chain_index,
+    residue_move_mask,
+    timestep,
+    single_projection_weight,
+    head_bias_weight,
+    head_distance_weight,
+    chain_logit_offset,
+    local_output_weight,
+    pair_output_weight,
+    single_norm_gain,
+    frame_velocity_weight,
+    left_pair_weight,
+    right_pair_weight,
+):
+    rows_dev = single.shape[0]
+    col_count = pair.shape[1]
+    total = rotations.shape[2]
+    heads_here = single_projection_weight.shape[1]
+    row_start = lax.axis_index("res") * rows_dev
+    rot_all = jnp.transpose(rotations, (2, 0, 1))
+    trans_all = jnp.transpose(translations)
+    rot_own = lax.dynamic_slice_in_dim(rot_all, row_start, rows_dev, 0)
+    trans_own = lax.dynamic_slice_in_dim(trans_all, row_start, rows_dev, 0)
+    own_chain = lax.dynamic_slice_in_dim(residue_chain_index, row_start, rows_dev, 0)
+    offset = 3 * HEAD_FEATURES
+    feat_count = 2 * HEAD_FEATURES + 3 * PQ + 3 * PV
+    count = total // rows_dev
+    every_single = sorted_blocks(*gather_blocks(single, count)).reshape(total, -1)
+    every_proj = jnp.einsum(
+        "nd,dhf->nhf", every_single, single_projection_weight, preferred_element_type=jnp.float32
+    )
+    projected = lax.dynamic_slice_in_dim(every_proj, row_start, rows_dev, 0)
+    packed_projection = key_features(every_proj, rot_all, trans_all)
+    packed_projection = packed_projection.reshape(total, heads_here, feat_count)
+    query_values = projected[:, :, 0:HEAD_FEATURES].astype(jnp.bfloat16)
+    query_flattened = to_global(
+        projected[:, :, offset : offset + 3 * PQ], rot_own, trans_own, PQ
+    ).reshape(rows_dev, heads_here, 3 * PQ)
+    bias_local = jnp.einsum(
+        "rjc,ch->rhj", pair, head_bias_weight, preferred_element_type=jnp.float32
+    ).astype(jnp.bfloat16)
+    pair_head_bias = lax.all_to_all(
+        bias_local, "head", split_axis=1, concat_axis=2, tiled=True
+    ).astype(jnp.float32)
+    within_chain = (own_chain[:, None] == residue_chain_index[None, :]).astype(jnp.float32)
+    logit_matrix = local_logit_rows(
+        query_values,
+        query_flattened,
+        packed_projection,
+        pair_head_bias,
+        within_chain,
+        head_distance_weight,
+        chain_logit_offset,
+        residue_move_mask > 0,
+    )
+    peak = jnp.max(logit_matrix, axis=-1, keepdims=True)
+    exponent = jnp.exp(logit_matrix - peak)
+    attention = rounded(exponent / jnp.sum(exponent, axis=-1, keepdims=True))
+    scalar_out = jnp.einsum(
+        "rhn,nhc->rhc",
+        attention,
+        packed_projection[:, :, HEAD_FEATURES : 2 * HEAD_FEATURES],
+        preferred_element_type=jnp.float32,
+    )
+    point_global = jnp.einsum(
+        "rhn,nhp->rhp",
+        attention.astype(jnp.float32),
+        packed_projection[:, :, 2 * HEAD_FEATURES + 3 * PQ :].astype(jnp.float32),
+        precision=HIGHEST,
+    )
+    update_local = local_points(scalar_out, point_global, rot_own, trans_own, local_output_weight)
+    attention_cols = lax.all_to_all(attention, "head", split_axis=2, concat_axis=1, tiled=True)
+    pair_attended = jnp.einsum(
+        "rhj,rjc->rhc", attention_cols, pair, preferred_element_type=jnp.float32
+    )
+    update_pair = jnp.einsum(
+        "rhc,hcd->rd", pair_attended, pair_output_weight.astype(jnp.float32), precision=HIGHEST
+    )
+    update = lax.psum(update_local + update_pair, "head")
+    single_out = layer_norm(single.astype(jnp.float32) + update, single_norm_gain).astype(
+        jnp.bfloat16
+    )
+    live_all = (residue_move_mask > 0).astype(jnp.float32)
+    live_own = lax.dynamic_slice_in_dim(live_all, row_start, rows_dev, 0)
+    step_ratio = 1.0 / (STEPS - timestep[0]).astype(jnp.float32)
+    rot_out, trans_out = frame_step(
+        single_out, frame_velocity_weight, rot_own, trans_own, live_own, step_ratio
+    )
+    left_proj = jnp.dot(single_out, left_pair_weight, preferred_element_type=jnp.float32).astype(
+        jnp.bfloat16
+    )
+    right_proj = jnp.dot(single_out, right_pair_weight, preferred_element_type=jnp.float32).astype(
+        jnp.bfloat16
+    )
+    return single_out, rot_out, trans_out, left_proj, right_proj
+
+
 def shards(
     single,
     pair,
@@ -318,84 +788,28 @@
     transition_back_weight,
 ):
     rows_dev = single.shape[0]
-    col_count = pair.shape[1]
-    total = rotations.shape[2]
-    heads_here = single_projection_weight.shape[1]
-    row_start = lax.axis_index("res") * rows_dev
-    rot_all = jnp.transpose(rotations, (2, 0, 1))
-    trans_all = jnp.transpose(translations)
-    rot_own = lax.dynamic_slice_in_dim(rot_all, row_start, rows_dev, 0)
-    trans_own = lax.dynamic_slice_in_dim(trans_all, row_start, rows_dev, 0)
-    own_chain = lax.dynamic_slice_in_dim(residue_chain_index, row_start, rows_dev, 0)
-    offset = 3 * HEAD_FEATURES
-    feat_count = 2 * HEAD_FEATURES + 3 * PQ + 3 * PV
-    count = total // rows_dev
-    every_single = sorted_blocks(*gather_blocks(single, count)).reshape(total, -1)
-    every_proj = jnp.einsum(
-        "nd,dhf->nhf", every_single, single_projection_weight, preferred_element_type=jnp.float32
-    )
-    projected = lax.dynamic_slice_in_dim(every_proj, row_start, rows_dev, 0)
-    packed_projection = key_features(every_proj, rot_all, trans_all)
-    packed_projection = packed_projection.reshape(total, heads_here, feat_count)
-    query_values = projected[:, :, 0:HEAD_FEATURES].astype(jnp.bfloat16)
-    query_flattened = to_global(
-        projected[:, :, offset : offset + 3 * PQ], rot_own, trans_own, PQ
-    ).reshape(rows_dev, heads_here, 3 * PQ)
-    bias_local = jnp.einsum(
-        "rjc,ch->rhj", pair, head_bias_weight, preferred_element_type=jnp.float32
-    ).astype(jnp.bfloat16)
-    pair_head_bias = lax.all_to_all(
-        bias_local, "head", split_axis=1, concat_axis=2, tiled=True
-    ).astype(jnp.float32)
-    within_chain = (own_chain[:, None] == residue_chain_index[None, :]).astype(jnp.float32)
-    logit_matrix = local_logit_rows(
-        query_values,
-        query_flattened,
-        packed_projection,
-        pair_head_bias,
-        within_chain,
+    count = rotations.shape[2] // rows_dev
+    whole_heads = lax.axis_size("head") == 1 and count >= 16 and count & (count - 1) == 0
+    single_out, rot_out, trans_out, left_proj, right_proj = (
+        attend if whole_heads else attend_split
+    )(
+        single,
+        pair,
+        rotations,
+        translations,
+        residue_chain_index,
+        residue_move_mask,
+        timestep,
+        single_projection_weight,
+        head_bias_weight,
         head_distance_weight,
         chain_logit_offset,
-        residue_move_mask > 0,
-    )
-    peak = jnp.max(logit_matrix, axis=-1, keepdims=True)
-    exponent = jnp.exp(logit_matrix - peak)
-    attention = rounded(exponent / jnp.sum(exponent, axis=-1, keepdims=True))
-    scalar_out = jnp.einsum(
-        "rhn,nhc->rhc",
-        attention,
-        packed_projection[:, :, HEAD_FEATURES : 2 * HEAD_FEATURES],
-        preferred_element_type=jnp.float32,
-    )
-    point_global = jnp.einsum(
-        "rhn,nhp->rhp",
-        attention.astype(jnp.float32),
-        packed_projection[:, :, 2 * HEAD_FEATURES + 3 * PQ :].astype(jnp.float32),
-        precision=HIGHEST,
-    )
-    update_local = local_points(scalar_out, point_global, rot_own, trans_own, local_output_weight)
-    attention_cols = lax.all_to_all(attention, "head", split_axis=2, concat_axis=1, tiled=True)
-    pair_attended = jnp.einsum(
-        "rhj,rjc->rhc", attention_cols, pair, preferred_element_type=jnp.float32
-    )
-    update_pair = jnp.einsum(
-        "rhc,hcd->rd", pair_attended, pair_output_weight.astype(jnp.float32), precision=HIGHEST
-    )
-    update = lax.psum(update_local + update_pair, "head")
-    single_out = layer_norm(single.astype(jnp.float32) + update, single_norm_gain).astype(
-        jnp.bfloat16
-    )
-    live_all = (residue_move_mask > 0).astype(jnp.float32)
-    live_own = lax.dynamic_slice_in_dim(live_all, row_start, rows_dev, 0)
-    step_ratio = 1.0 / (STEPS - timestep[0]).astype(jnp.float32)
-    rot_out, trans_out = frame_step(
-        single_out, frame_velocity_weight, rot_own, trans_own, live_own, step_ratio
-    )
-    left_proj = jnp.dot(single_out, left_pair_weight, preferred_element_type=jnp.float32).astype(
-        jnp.bfloat16
-    )
-    right_proj = jnp.dot(single_out, right_pair_weight, preferred_element_type=jnp.float32).astype(
-        jnp.bfloat16
+        local_output_weight,
+        pair_output_weight,
+        single_norm_gain,
+        frame_velocity_weight,
+        left_pair_weight,
+        right_pair_weight,
     )
     offsets, blocks = gather_blocks(right_proj, count)
     if offsets is None:

time: 75 us -> 50.6 us (0.67)
  matrix products: 14.7 us -> 0 us
  local copies, waits for them, and re-layouts: 19.6 us -> 7.02 us
  Pallas kernels: 9.49 us -> 17.8 us
  other arithmetic: 8.88 us -> 0.74 us
  waiting for transfers between devices: 6.9 us -> 9.28 us
  starting transfers between devices: 12.5 us -> 13.7 us
    dot_general x14 -> x0, matrix products: 12.8 us -> none  [the longest x1 3.14 us: shards(): jnp.einsum('rjc,ch->rhj', pair, head_bias_weight, preferred_element_type=...]
    pallas_call x0 -> x3, Pallas kernels: none -> 8.35 us  [the longest x1 4.92 us: attend(): pl.pallas_call(functools.partial(attention_kernel, offsets), in_specs=in_...]
    convert_element_type x5 -> x0, other arithmetic: 3.37 us -> none  [the longest x1 1.36 us: shards(): (own_chain[:, None] == residue_chain_index[None, :]).astype(jnp.float32)]
    ppermute x10, waiting for transfers between devices: 6.9 us -> 9.28 us  [exchange(): return lax.ppermute(block, 'res', [(k, k ^ step) for k in range(count)])]
    reshape x2 -> x0, local copies, waits for them, and re-layouts: 2.24 us -> none  [the longest x1 1.38 us: shards(): packed_projection = packed_projection.reshape(total, heads_here, feat_count)]
    dynamic_slice x4 -> x0, local copies, waits for them, and re-layouts: 2.23 us -> none  [the longest x1 0.79 us: shards(): rot_own = lax.dynamic_slice_in_dim(rot_all, row_start, rows_dev, 0)]
    sub x1 -> x0, matrix products: 1.95 us -> none  [shards(): exponent = jnp.exp(logit_matrix - peak)]
    unnamed x81 -> x53, local copies, waits for them, and re-layouts: 6.96 us -> 5.03 us
  transfers between devices with their start and end apart: 10 -> 10, of which waited for: 6 -> 7; matrix products, arithmetic and copies ran while one was open for 22% -> 9% of each run, Pallas kernels for 0% -> 7%
where the time goes in v2:
time: 50.6 us; the launch traced here: 50.1 us
  Pallas kernels  17.8 us (35%)
  starting transfers between devices  13.7 us (27%)
  waiting for transfers between devices  9.28 us (18%)
  local copies, waits for them, and re-layouts  7.02 us (14%)
  between operations  1.6 us (3%)
  other arithmetic  0.74 us (1%)
    ppermute x10, starting transfers between devices, exchange(): return lax.ppermute(block, 'res', [(k, k ^ step) for k in range(count)])  13.7 us
    pallas_call x1, Pallas kernels, pair_transition(): pl.pallas_call(kernel, grid=(rows_dev // rows_block,), in_specs=[pl.Block...  9.41 us
    ppermute x10, waiting for transfers between devices, exchange(): return lax.ppermute(block, 'res', [(k, k ^ step) for k in range(count)])  9.28 us
    unnamed x53, local copies, waits for them, and re-layouts  5.03 us
    pallas_call x1, Pallas kernels, attend(): pl.pallas_call(functools.partial(attention_kernel, offsets), in_specs=in_...  4.92 us
    pallas_call x1, Pallas kernels, attend(): pl.pallas_call(query_kernel, in_specs=[pl.BlockSpec(memory_space=pltpu.SM...  1.86 us
    pallas_call x1, Pallas kernels, attend(): pl.pallas_call(frame_kernel, in_specs=[pl.BlockSpec(memory_space=pltpu.SM...  1.58 us
  transfers between devices with their start and end apart: 10, of which 7 were waited for; matrix products, arithmetic and copies ran while one was open for 9% of the time, Pallas kernels for 7%

profile of v2, /device:TPU:0, one launch (start us, length us, event | category | flops | bytes accessed | tf_op | source)
XLA Modules:
  0.0 50.1 jit_solution(6334871229331290063)
XLA Ops:
  0.7 0.0 copy-start.5
  0.7 0.0 copy-start.8
  0.7 3.0 %collective-permute-start = (bf16[1,24,384]{2,1,0:T(8,128)(2,1)}, bf16[1,24,384]{2,1,0:T(8,128)(2,1)S(1)}, u32[]{:S(2)}, u32[]{:S(2)}) collective-permute-start(bf16[1,24,384]{2,1,0:T(8,128)(2,1)} %bitcast.19), channel_id=1, source_target_pairs={{0,2},{1,3},{2,0},{3,1},{4,6},{5,7},{6,4},{7,5},{8,10},{9,11},{10,... | collective-permute-start | bytes 55304 | tf_op jit(solution)/shard_map/ppermute | solution.py:145
  3.7 0.8 %constant_dynamic-update-slice_fusion.4 = bf16[8,24,384]{2,1,0:T(8,128)(2,1)S(1)} fusion(bf16[24,384]{1,0:T(8,128)(2,1)} %single_ref.3), kind=kLoop, calls=%fused_computation.6 | loop fusion | bytes 36864
  4.5 1.2 %collective-permute-done = bf16[1,24,384]{2,1,0:T(8,128)(2,1)S(1)} collective-permute-done((bf16[1,24,384]{2,1,0:T(8,128)(2,1)}, bf16[1,24,384]{2,1,0:T(8,128)(2,1)S(1)}, u32[]{:S(2)}, u32[]{:S(2)}) %collective-permute-start) | collective-permute-done | bytes 18464 | tf_op jit(solution)/shard_map/ppermute | solution.py:145
  5.7 0.7 %pad_maximum_fusion = bf16[2,24,384]{2,1,0:T(8,128)(2,1)S(1)} fusion(bf16[1,24,384]{2,1,0:T(8,128)(2,1)S(1)} %collective-permute-done, bf16[1,24,384]{2,1,0:T(8,128)(2,1)} %bitcast.20), kind=kLoop, calls=%fused_computation.1 | loop fusion | flops 18432 | bytes 73728 | tf_op jit(solution)/shard_map/concatenate | solution.py:156
  6.4 4.1 %collective-permute-start.1 = (bf16[2,24,384]{2,1,0:T(8,128)(2,1)S(1)}, bf16[2,24,384]{2,1,0:T(8,128)(2,1)S(1)}, u32[]{:S(2)}, u32[]{:S(2)}) collective-permute-start(bf16[2,24,384]{2,1,0:T(8,128)(2,1)S(1)} %pad_maximum_fusion), channel_id=1, source_target_pairs={{0,12},{1,13},{2,14},{3,15},{4,8},{5,9},{6,10},{7,11},{8,4},{9,5},... | collective-permute-start | bytes 110600 | tf_op jit(solution)/shard_map/ppermute | solution.py:145
  10.6 0.6 %collective-permute-start.3 = (bf16[2,24,384]{2,1,0:T(8,128)(2,1)S(1)}, bf16[2,24,384]{2,1,0:T(8,128)(2,1)S(1)}, u32[]{:S(2)}, u32[]{:S(2)}) collective-permute-start(bf16[2,24,384]{2,1,0:T(8,128)(2,1)S(1)} %pad_maximum_fusion), channel_id=1, source_target_pairs={{0,4},{1,5},{2,6},{3,7},{4,0},{5,1},{6,2},{7,3},{8,12},{9,13},{10,... | collective-permute-start | bytes 110600 | tf_op jit(solution)/shard_map/ppermute | solution.py:145
  11.2 1.3 %collective-permute-done.1 = bf16[2,24,384]{2,1,0:T(8,128)(2,1)S(1)} collective-permute-done((bf16[2,24,384]{2,1,0:T(8,128)(2,1)S(1)}, bf16[2,24,384]{2,1,0:T(8,128)(2,1)S(1)}, u32[]{:S(2)}, u32[]{:S(2)}) %collective-permute-start.1) | collective-permute-done | bytes 36896 | tf_op jit(solution)/shard_map/ppermute | solution.py:145
  12.5 2.9 %collective-permute-done.2 = bf16[2,24,384]{2,1,0:T(8,128)(2,1)S(1)} collective-permute-done((bf16[2,24,384]{2,1,0:T(8,128)(2,1)S(1)}, bf16[2,24,384]{2,1,0:T(8,128)(2,1)S(1)}, u32[]{:S(2)}, u32[]{:S(2)}) %collective-permute-start.2) | collective-permute-done | bytes 36896 | tf_op jit(solution)/shard_map/ppermute | solution.py:145
  15.4 0.1 collective-permute-start.4
  15.5 0.7 %broadcast_in_dim.27.chain_row_ref = s32[1,384]{1,0:T(1,128)S(1)} reshape(s32[384]{0:T(512)} %chain_ref.1) | data formatting | bytes 3072 | tf_op jit(solution)/shard_map/broadcast_in_dim | solution.py:605
  16.2 0.7 %broadcast_in_dim.30.present_ref.live_ref.live_row_ref = s32[1,384]{1,0:T(1,128)S(1)} reshape(s32[384]{0:T(512)} %live_ref.1) | data formatting | bytes 3072 | tf_op jit(solution)/shard_map/broadcast_in_dim | solution.py:633
  16.9 1.6 %copy.27 = bf16[16,64,384]{2,0,1:T(8,128)(2,1)S(1)} copy(bf16[16,64,384]{2,1,0:T(8,128)(2,1)} %param.32) | data formatting | bytes 1572864 | tf_op args[11]
  18.6 0.0 copy-start
  18.6 1.7 %copy-done = bf16[24,384,128]{2,1,0:T(8,128)(2,1)S(1)} copy-done((bf16[24,384,128]{2,1,0:T(8,128)(2,1)S(1)}, bf16[24,384,128]{2,1,0:T(8,128)(2,1)}, u32[]{:S(2)}) %copy-start) | copy-done | bytes 2359320
  20.3 1.9 %shard_map.228 = (bf16[384,1408]{1,0:T(8,128)(2,1)S(1)}, f32[24,16,384]{2,1,0:T(8,128)S(1)}, f32[24,16]{1,0:T(8,128)S(1)}) custom-call(s32[384]{0:T(512)S(1)} %copy-done.11, bf16[24,384,128]{2,1,0:T(8,128)(2,1)S(1)} %copy-done, bf16[24,384]{1,0:T(8,128)(2,1)S(1)} %copy-done.4, bf16[132,16,384]{2,1,0:T(8,128)(2,1)S(1)} %bitcast.15, ...), custom_call_target="tpu_custom_call" | custom-call | flops 1000000000 | bytes 6000000 | tf_op jit(solution)/shard_map/pallas_call | solution.py:585
  22.2 0.2 copy-done.3
  22.4 0.0 copy-start.17
  22.5 4.9 %shard_map.229 = (bf16[24,384]{1,0:T(8,128)(2,1)}, bf16[24,128]{1,0:T(8,128)(2,1)S(1)}, bf16[24,128]{1,0:T(8,128)(2,1)S(1)}) custom-call(bf16[8,24,384]{2,1,0:T(8,128)(2,1)S(1)} %constant_dynamic-update-slice_fusion.held_ref, bf16[8,24,384]{2,1,0:T(8,128)(2,1)S(1)} %collective-permute-done.4.other_ref, bf16[132,16,384]{2,1,0:T(8,128)(2,1)S(1)} %bitcast.16, ...), custom_call_target="tpu_custom_call" | custom-call | flops 2000000000 | bytes 10000000 | tf_op jit(solution)/shard_map/pallas_call | solution.py:609
  27.4 1.5 %collective-permute-start.5 = (bf16[1,24,128]{2,1,0:T(8,128)(2,1)S(1)}, bf16[1,24,128]{2,1,0:T(8,128)(2,1)S(1)}, u32[]{:S(2)}, u32[]{:S(2)}) collective-permute-start(bf16[1,24,128]{2,1,0:T(8,128)(2,1)S(1)} %bitcast.21), channel_id=1, source_target_pairs={{0,2},{1,3},{2,0},{3,1},{4,6},{5,7},{6,4},{7,5},{8,10},{9,11},{10,... | collective-permute-start | bytes 18440 | tf_op jit(solution)/shard_map/ppermute | solution.py:145
  28.9 2.1 %collective-permute-done.5 = bf16[1,24,128]{2,1,0:T(8,128)(2,1)S(1)} collective-permute-done((bf16[1,24,128]{2,1,0:T(8,128)(2,1)S(1)}, bf16[1,24,128]{2,1,0:T(8,128)(2,1)S(1)}, u32[]{:S(2)}, u32[]{:S(2)}) %collective-permute-start.5) | collective-permute-done | bytes 6176 | tf_op jit(solution)/shard_map/ppermute | solution.py:145
  31.0 1.4 %collective-permute-start.6 = (bf16[2,24,128]{2,1,0:T(8,128)(2,1)S(1)}, bf16[2,24,128]{2,1,0:T(8,128)(2,1)S(1)}, u32[]{:S(2)}, u32[]{:S(2)}) collective-permute-start(bf16[2,24,128]{2,1,0:T(8,128)(2,1)S(1)} %pad_maximum_fusion.1), channel_id=1, source_target_pairs={{0,12},{1,13},{2,14},{3,15},{4,8},{5,9},{6,10},{7,11},{8,4},{9,5},... | collective-permute-start | bytes 36872 | tf_op jit(solution)/shard_map/ppermute | solution.py:145
  32.5 0.6 %collective-permute-start.7 = (bf16[2,24,128]{2,1,0:T(8,128)(2,1)S(1)}, bf16[2,24,128]{2,1,0:T(8,128)(2,1)S(1)}, u32[]{:S(2)}, u32[]{:S(2)}) collective-permute-start(bf16[2,24,128]{2,1,0:T(8,128)(2,1)S(1)} %pad_maximum_fusion.1), channel_id=1, source_target_pairs={{0,8},{1,9},{2,10},{3,11},{4,12},{5,13},{6,14},{7,15},{8,0},{9,1},... | collective-permute-start | bytes 36872 | tf_op jit(solution)/shard_map/ppermute | solution.py:145
  33.1 2.3 %collective-permute-start.8 = (bf16[2,24,128]{2,1,0:T(8,128)(2,1)S(1)}, bf16[2,24,128]{2,1,0:T(8,128)(2,1)S(1)}, u32[]{:S(2)}, u32[]{:S(2)}) collective-permute-start(bf16[2,24,128]{2,1,0:T(8,128)(2,1)S(1)} %pad_maximum_fusion.1), channel_id=1, source_target_pairs={{0,4},{1,5},{2,6},{3,7},{4,0},{5,1},{6,2},{7,3},{8,12},{9,13},{10,... | collective-permute-start | bytes 36872 | tf_op jit(solution)/shard_map/ppermute | solution.py:145
  35.4 1.1 %collective-permute-done.6 = bf16[2,24,128]{2,1,0:T(8,128)(2,1)S(1)} collective-permute-done((bf16[2,24,128]{2,1,0:T(8,128)(2,1)S(1)}, bf16[2,24,128]{2,1,0:T(8,128)(2,1)S(1)}, u32[]{:S(2)}, u32[]{:S(2)}) %collective-permute-start.6) | collective-permute-done | bytes 12320 | tf_op jit(solution)/shard_map/ppermute | solution.py:145
  36.5 0.5 %collective-permute-done.7 = bf16[2,24,128]{2,1,0:T(8,128)(2,1)S(1)} collective-permute-done((bf16[2,24,128]{2,1,0:T(8,128)(2,1)S(1)}, bf16[2,24,128]{2,1,0:T(8,128)(2,1)S(1)}, u32[]{:S(2)}, u32[]{:S(2)}) %collective-permute-start.7) | collective-permute-done | bytes 12320 | tf_op jit(solution)/shard_map/ppermute | solution.py:145
  37.1 0.1 collective-permute-done.8
  37.9 0.6 %pad.4.velocity_ref = bf16[8,384]{1,0:T(8,128)(2,1)} pad(bf16[6,384]{1,0:T(8,128)(2,1)S(1)} %bitcast.29, bf16[]{:T(256)} %constant.2.clone.1), padding=0_2x0_0 | pad | bytes 10754 | tf_op jit(solution)/shard_map/jit(_pad)/pad | solution.py:643
  38.5 1.6 %shard_map.230 = (f32[3,3,24]{2,1,0:T(4,128)}, f32[3,24]{1,0:T(4,128)}) custom-call(s32[1]{0:T(128)S(6)} %copy.36.step_ref, s32[1,384]{1,0:T(1,128)} %copy-done.9, bf16[24,384]{1,0:T(8,128)(2,1)} %get-tuple-element.8.single_ref, bf16[8,384]{1,0:T(8,128)(2,1)} %pad.4.velocity_ref, f32[3,3,384]{2,1,0:T(4,128)} %rot_ref.5, f32[3,384]{1,0:T(4,128)} %trans_ref.5), custom_call_target="tpu_custom_call" | custom-call | flops 1000000 | bytes 100000 | tf_op jit(solution)/shard_map/pallas_call | solution.py:644
  40.1 0.6 %copy-done.10 = s32[1,384]{1,0:T(1,128)S(1)} copy-done((s32[1,384]{1,0:T(1,128)S(1)}, s32[1,384]{1,0:T(1,128)}, u32[]{:S(2)}) %copy-start.10) | copy-done | bytes 1560
  40.7 9.4 %shard_map.231 = bf16[24,384,128]{2,1,0:T(8,128)(2,1)} custom-call(s32[384]{0:T(512)S(1)} %copy-done.13, bf16[24,384,128]{2,1,0:T(8,128)(2,1)S(1)} %copy-done.1, bf16[6,4,128]{2,1,0:T(4,128)(2,1)S(1)} %bitcast.27, s32[1,384]{1,0:T(1,128)S(1)} %copy-done.10, f32[1,128]{1,0:T(1,128)S(1)} %bitcast.28, bf16[128,256]{1,0:T(8,128)(2,1)S(1)} %copy-done.17, ...), custom_call_target="tpu_custom_call" | custom-call | flops 3019898880 | bytes 4718592 | tf_op jit(solution)/shard_map/pallas_call | solution.py:259
  (53 shorter events, 0.2 us)
Async XLA Ops:
  0.6 17.9 %copy-start.4 = (bf16[24,384]{1,0:T(8,128)(2,1)S(1)}, bf16[24,384]{1,0:T(8,128)(2,1)}, u32[]{:S(2)}) copy-start(bf16[24,384]{1,0:T(8,128)(2,1)} %single_ref.3) | copy-start | bytes 55300
  0.6 17.9 %copy-start.11 = (s32[384]{0:T(512)S(1)}, s32[384]{0:T(512)}, u32[]{:S(2)}) copy-start(s32[384]{0:T(512)} %chain_ref.1) | copy-start | bytes 4612
  0.7 17.9 %copy-start.21 = (f32[384]{0:T(512)S(1)}, f32[384]{0:T(512)}, u32[]{:S(2)}) copy-start(f32[384]{0:T(512)} %param.34) | copy-start | bytes 4612
  0.7 17.9 %copy-start.2 = (bf16[384,16,132]{0,1,2:T(8,128)(2,1)S(1)}, bf16[384,16,132]{0,1,2:T(8,128)(2,1)}, u32[]{:S(2)}) copy-start(bf16[384,16,132]{0,1,2:T(8,128)(2,1)} %param.28) | copy-start | bytes 4866052
  0.7 17.9 %copy-start.14 = (f32[16]{0:T(128)S(1)}, f32[16]{0:T(128)}, u32[]{:S(2)}) copy-start(f32[16]{0:T(128)} %param.30) | copy-start | bytes 196
  0.7 17.9 %copy-start.12 = (bf16[128,16]{0,1:T(8,128)(2,1)S(1)}, bf16[128,16]{0,1:T(8,128)(2,1)}, u32[]{:S(2)}) copy-start(bf16[128,16]{0,1:T(8,128)(2,1)} %param.29) | copy-start | bytes 12292
  0.7 17.9 %copy-start.15 = (f32[16]{0:T(128)S(1)}, f32[16]{0:T(128)}, u32[]{:S(2)}) copy-start(f32[16]{0:T(128)} %param.31) | copy-start | bytes 196
  0.7 17.9 %copy-start.5 = (f32[3,3,384]{2,1,0:T(4,128)S(1)}, f32[3,3,384]{2,1,0:T(4,128)}, u32[]{:S(2)}) copy-start(f32[3,3,384]{2,1,0:T(4,128)} %rot_ref.5) | copy-start | bytes 41476
  0.7 17.9 %copy-start.8 = (f32[3,384]{1,0:T(4,128)S(1)}, f32[3,384]{1,0:T(4,128)}, u32[]{:S(2)}) copy-start(f32[3,384]{1,0:T(4,128)} %trans_ref.5) | copy-start | bytes 13828
  0.7 5.0 %collective-permute-start = (bf16[1,24,384]{2,1,0:T(8,128)(2,1)}, bf16[1,24,384]{2,1,0:T(8,128)(2,1)S(1)}, u32[]{:S(2)}, u32[]{:S(2)}) collective-permute-start(bf16[1,24,384]{2,1,0:T(8,128)(2,1)} %bitcast.19), channel_id=1, source_target_pairs={{0,2},{1,3},{2,0},{3,1},{4,6},{5,7},{6,4},{7,5},{8,10},{9,11},{10,... | collective-permute-start | bytes 55304 | tf_op jit(solution)/shard_map/ppermute | solution.py:145
  6.4 6.1 %collective-permute-start.1 = (bf16[2,24,384]{2,1,0:T(8,128)(2,1)S(1)}, bf16[2,24,384]{2,1,0:T(8,128)(2,1)S(1)}, u32[]{:S(2)}, u32[]{:S(2)}) collective-permute-start(bf16[2,24,384]{2,1,0:T(8,128)(2,1)S(1)} %pad_maximum_fusion), channel_id=1, source_target_pairs={{0,12},{1,13},{2,14},{3,15},{4,8},{5,9},{6,10},{7,11},{8,4},{9,5},... | collective-permute-start | bytes 110600 | tf_op jit(solution)/shard_map/ppermute | solution.py:145
  10.5 4.9 %collective-permute-start.2 = (bf16[2,24,384]{2,1,0:T(8,128)(2,1)S(1)}, bf16[2,24,384]{2,1,0:T(8,128)(2,1)S(1)}, u32[]{:S(2)}, u32[]{:S(2)}) collective-permute-start(bf16[2,24,384]{2,1,0:T(8,128)(2,1)S(1)} %pad_maximum_fusion), channel_id=1, source_target_pairs={{0,8},{1,9},{2,10},{3,11},{4,12},{5,13},{6,14},{7,15},{8,0},{9,1},... | collective-permute-start | bytes 110600 | tf_op jit(solution)/shard_map/ppermute | solution.py:145
  10.6 4.9 %collective-permute-start.3 = (bf16[2,24,384]{2,1,0:T(8,128)(2,1)S(1)}, bf16[2,24,384]{2,1,0:T(8,128)(2,1)S(1)}, u32[]{:S(2)}, u32[]{:S(2)}) collective-permute-start(bf16[2,24,384]{2,1,0:T(8,128)(2,1)S(1)} %pad_maximum_fusion), channel_id=1, source_target_pairs={{0,4},{1,5},{2,6},{3,7},{4,0},{5,1},{6,2},{7,3},{8,12},{9,13},{10,... | collective-permute-start | bytes 110600 | tf_op jit(solution)/shard_map/ppermute | solution.py:145
  15.4 6.7 %collective-permute-start.4 = (bf16[8,24,384]{2,1,0:T(8,128)(2,1)S(1)}, bf16[8,24,384]{2,1,0:T(8,128)(2,1)S(1)}, u32[]{:S(2)}, u32[]{:S(2)}) collective-permute-start(bf16[8,24,384]{2,1,0:T(8,128)(2,1)S(1)} %constant_dynamic-update-slice_fusion.held_ref), channel_id=1, source_target_pairs={{0,1},{1,0},{2,3},{3,2},{4,5},{5,4},{6,7},{7,6},{8,9},{9,8},{10,11... | collective-permute-start | bytes 442376 | tf_op jit(solution)/shard_map/ppermute | solution.py:145
  16.9 5.3 %copy-start.9 = (s32[1,384]{1,0:T(1,128)}, s32[1,384]{1,0:T(1,128)S(1)}, u32[]{:S(2)}) copy-start(s32[1,384]{1,0:T(1,128)S(1)} %broadcast_in_dim.30.present_ref.live_ref.live_row_ref) | copy-start | bytes 4612
  16.9 5.3 %copy-start.7 = (bf16[384,128]{1,0:T(8,128)(2,1)S(1)}, bf16[384,128]{1,0:T(8,128)(2,1)}, u32[]{:S(2)}) copy-start(bf16[384,128]{1,0:T(8,128)(2,1)} %right_ref.1) | copy-start | bytes 294916
  18.6 1.7 %copy-start = (bf16[24,384,128]{2,1,0:T(8,128)(2,1)S(1)}, bf16[24,384,128]{2,1,0:T(8,128)(2,1)}, u32[]{:S(2)}) copy-start(bf16[24,384,128]{2,1,0:T(8,128)(2,1)} %pair_ref.5) | copy-start | bytes 7077892
  20.3 1.9 %copy-start.1 = (bf16[24,384,128]{2,1,0:T(8,128)(2,1)S(1)}, bf16[24,384,128]{2,1,0:T(8,128)(2,1)}, u32[]{:S(2)}) copy-start(bf16[24,384,128]{2,1,0:T(8,128)(2,1)} %pair_ref.5) | copy-start | bytes 7077892
  20.3 2.1 %copy-start.3 = (bf16[16,128,384]{2,1,0:T(8,128)(2,1)S(1)}, bf16[16,128,384]{2,1,0:T(8,128)(2,1)}, u32[]{:S(2)}) copy-start(bf16[16,128,384]{2,1,0:T(8,128)(2,1)} %param.33) | copy-start | bytes 4718596
  20.3 2.1 %copy-start.6 = (bf16[384,128]{1,0:T(8,128)(2,1)S(1)}, bf16[384,128]{1,0:T(8,128)(2,1)}, u32[]{:S(2)}) copy-start(bf16[384,128]{1,0:T(8,128)(2,1)} %left_ref.1) | copy-start | bytes 294916
  22.4 15.4 %copy-start.20 = (bf16[384,6]{0,1:T(8,128)(2,1)S(1)}, bf16[384,6]{0,1:T(8,128)(2,1)}, u32[]{:S(2)}) copy-start(bf16[384,6]{0,1:T(8,128)(2,1)} %param.35) | copy-start | bytes 13828
  22.4 17.6 %copy-start.13 = (s32[384]{0:T(512)S(1)}, s32[384]{0:T(512)}, u32[]{:S(2)}) copy-start(s32[384]{0:T(512)} %live_ref.1) | copy-start | bytes 4612
  22.4 17.6 %copy-start.16 = (bf16[256,256]{1,0:T(8,128)(2,1)S(1)}, bf16[256,256]{1,0:T(8,128)(2,1)}, u32[]{:S(2)}) copy-start(bf16[256,256]{1,0:T(8,128)(2,1)} %middle_ref.1) | copy-start | bytes 393220
  22.4 17.6 %copy-start.17 = (bf16[128,256]{1,0:T(8,128)(2,1)S(1)}, bf16[128,256]{1,0:T(8,128)(2,1)}, u32[]{:S(2)}) copy-start(bf16[128,256]{1,0:T(8,128)(2,1)} %hidden_ref.1) | copy-start | bytes 196612
  22.4 17.6 %copy-start.18 = (bf16[256,128]{1,0:T(8,128)(2,1)S(1)}, bf16[256,128]{1,0:T(8,128)(2,1)}, u32[]{:S(2)}) copy-start(bf16[256,128]{1,0:T(8,128)(2,1)} %back_ref.1) | copy-start | bytes 196612
  22.4 17.6 %copy-start.19 = (f32[128]{0:T(128)S(1)}, f32[128]{0:T(128)}, u32[]{:S(2)}) copy-start(f32[128]{0:T(128)} %param.38) | copy-start | bytes 1540
  27.4 3.6 %collective-permute-start.5 = (bf16[1,24,128]{2,1,0:T(8,128)(2,1)S(1)}, bf16[1,24,128]{2,1,0:T(8,128)(2,1)S(1)}, u32[]{:S(2)}, u32[]{:S(2)}) collective-permute-start(bf16[1,24,128]{2,1,0:T(8,128)(2,1)S(1)} %bitcast.21), channel_id=1, source_target_pairs={{0,2},{1,3},{2,0},{3,1},{4,6},{5,7},{6,4},{7,5},{8,10},{9,11},{10,... | collective-permute-start | bytes 18440 | tf_op jit(solution)/shard_map/ppermute | solution.py:145
  31.0 5.5 %collective-permute-start.6 = (bf16[2,24,128]{2,1,0:T(8,128)(2,1)S(1)}, bf16[2,24,128]{2,1,0:T(8,128)(2,1)S(1)}, u32[]{:S(2)}, u32[]{:S(2)}) collective-permute-start(bf16[2,24,128]{2,1,0:T(8,128)(2,1)S(1)} %pad_maximum_fusion.1), channel_id=1, source_target_pairs={{0,12},{1,13},{2,14},{3,15},{4,8},{5,9},{6,10},{7,11},{8,4},{9,5},... | collective-permute-start | bytes 36872 | tf_op jit(solution)/shard_map/ppermute | solution.py:145
  32.5 4.6 %collective-permute-start.7 = (bf16[2,24,128]{2,1,0:T(8,128)(2,1)S(1)}, bf16[2,24,128]{2,1,0:T(8,128)(2,1)S(1)}, u32[]{:S(2)}, u32[]{:S(2)}) collective-permute-start(bf16[2,24,128]{2,1,0:T(8,128)(2,1)S(1)} %pad_maximum_fusion.1), channel_id=1, source_target_pairs={{0,8},{1,9},{2,10},{3,11},{4,12},{5,13},{6,14},{7,15},{8,0},{9,1},... | collective-permute-start | bytes 36872 | tf_op jit(solution)/shard_map/ppermute | solution.py:145
  33.1 4.1 %collective-permute-start.8 = (bf16[2,24,128]{2,1,0:T(8,128)(2,1)S(1)}, bf16[2,24,128]{2,1,0:T(8,128)(2,1)S(1)}, u32[]{:S(2)}, u32[]{:S(2)}) collective-permute-start(bf16[2,24,128]{2,1,0:T(8,128)(2,1)S(1)} %pad_maximum_fusion.1), channel_id=1, source_target_pairs={{0,4},{1,5},{2,6},{3,7},{4,0},{5,1},{6,2},{7,3},{8,12},{9,13},{10,... | collective-permute-start | bytes 36872 | tf_op jit(solution)/shard_map/ppermute | solution.py:145
  37.2 2.8 %collective-permute-start.9 = (bf16[8,24,128]{2,1,0:T(8,128)(2,1)S(1)}, bf16[8,24,128]{2,1,0:T(8,128)(2,1)S(1)}, u32[]{:S(2)}, u32[]{:S(2)}) collective-permute-start(bf16[8,24,128]{2,1,0:T(8,128)(2,1)S(1)} %constant_dynamic-update-slice_fusion.5.rest_0_), channel_id=1, source_target_pairs={{0,1},{1,0},{2,3},{3,2},{4,5},{5,4},{6,7},{7,6},{8,9},{9,8},{10,11... | collective-permute-start | bytes 147464 | tf_op jit(solution)/shard_map/ppermute | solution.py:145
  40.1 0.6 %copy-start.10 = (s32[1,384]{1,0:T(1,128)S(1)}, s32[1,384]{1,0:T(1,128)}, u32[]{:S(2)}) copy-start(s32[1,384]{1,0:T(1,128)} %copy-done.9) | copy-start | bytes 4612

commit v3 on v2

--- a/solution.py
+++ b/solution.py
@@ -145,10 +145,7 @@
     return lax.ppermute(block, "res", [(k, k ^ step) for k in range(count)])
 
 
-def gather_blocks(block, count):
-    if count < 16 or count & (count - 1):
-        whole = lax.all_gather(block, "res", axis=0)
-        return None, whole
+def gather_most(block, count, tied=()):
     held, offsets = block[None], [0]
     quarter = count // 4
     step = quarter // 2
@@ -156,11 +153,17 @@
         held = jnp.concatenate([held, exchange(held, count, step)], 0)
         offsets = offsets + [o ^ step for o in offsets]
         step //= 2
+    held, tied = lax.optimization_barrier((held, tied))
     parts = [held] + [exchange(held, count, k * quarter) for k in (3, 2, 1)]
     held = jnp.concatenate(parts, 0)
-    offsets = [o ^ (k * quarter) for k in (0, 3, 2, 1) for o in offsets]
-    other = exchange(held, count, 1)
-    return offsets, (held, other)
+    return [o ^ (k * quarter) for k in (0, 3, 2, 1) for o in offsets], held, tied
+
+
+def gather_blocks(block, count, tied=()):
+    if count < 16 or count & (count - 1):
+        return None, lax.all_gather(block, "res", axis=0), tied
+    offsets, held, tied = gather_most(block, count, tied)
+    return offsets, (held, exchange(held, count, 1)), tied
 
 
 def sorted_blocks(offsets, blocks):
@@ -183,6 +186,7 @@
     rows_block,
     rows_dev,
     offsets,
+    live_at,
     live_ref,
     pair_ref,
     left_ref,
@@ -209,7 +213,8 @@
                 owner = me ^ offsets[at] if offsets is not None else at
                 at += 1
                 right_ref[pl.ds(pl.multiple_of(owner * rows_dev, 8), rows_dev), :] = value
-        wide = jnp.broadcast_to(live_row_ref[...].astype(jnp.float32), (feats, live_row_ref.shape[1]))
+        live_row = live_row_ref[pl.ds(live_at, 1), :].astype(jnp.float32)
+        wide = jnp.broadcast_to(live_row, (feats, live_row.shape[1]))
         live_cols_ref[...] = jnp.where(jnp.transpose(wide) > 0, 1.0, 0.0)
         across = lax.broadcasted_iota(jnp.int32, (feats, feats), 0)
         down = lax.broadcasted_iota(jnp.int32, (feats, feats), 1)
@@ -247,14 +252,14 @@
 
 
 def pair_transition(
-    pair, left_proj, move_mask, gain, hidden, middle, back, offsets, blocks
+    pair, left_proj, move_mask, live_rows, live_at, gain, hidden, middle, back, offsets, blocks
 ):
     rows_dev, cols, feats = pair.shape
     total = move_mask.shape[0]
     rows_block = math.gcd(rows_dev, max(1, 1536 // cols))
     left_wide = left_proj.reshape(rows_dev // rows_block, rows_block, feats)
     whole = lambda *shape: pl.BlockSpec(shape, lambda i: (0,) * len(shape))
-    kernel = functools.partial(transition_kernel, rows_block, rows_dev, offsets)
+    kernel = functools.partial(transition_kernel, rows_block, rows_dev, offsets, live_at)
     macs = rows_dev * cols * (2 * feats * feats + 2 * feats * hidden.shape[1] + hidden.shape[1] ** 2)
     return pl.pallas_call(
         kernel,
@@ -263,7 +268,7 @@
             pl.BlockSpec(memory_space=pltpu.SMEM),
             pl.BlockSpec((rows_block, cols, feats), lambda i: (i, 0, 0)),
             pl.BlockSpec((None, rows_block, feats), lambda i: (i, 0, 0)),
-            whole(1, total),
+            whole(*live_rows.shape),
             whole(1, feats),
             whole(*hidden.shape),
             whole(*middle.shape),
@@ -277,7 +282,7 @@
             pltpu.VMEM((total, feats), jnp.float32),
             pltpu.VMEM((feats, feats), jnp.bfloat16),
         ],
-        compiler_params=pltpu.CompilerParams(vmem_limit_bytes=48 * 1024 * 1024),
+        compiler_params=pltpu.CompilerParams(vmem_limit_bytes=32 * 1024 * 1024),
         cost_estimate=pl.CostEstimate(
             flops=2 * macs, bytes_accessed=2 * pair.size * 2, transcendentals=0
         ),
@@ -285,7 +290,7 @@
         move_mask,
         pair,
         left_wide,
-        move_mask[None],
+        live_rows,
         gain[None],
         hidden,
         middle,
@@ -331,15 +336,20 @@
     ]
 
 
+def bias_kernel(weight_ref, pair_ref, out_ref):
+    for r in range(pair_ref.shape[0]):
+        bias = dot_rows(weight_ref[...], pair_ref[r])
+        out_ref[r] = bias.astype(jnp.bfloat16).astype(jnp.float32)
+
+
 def query_kernel(
     chain_ref,
-    pair_ref,
+    bias_ref,
     single_ref,
     weight_ref,
-    bias_ref,
     rot_ref,
     trans_ref,
-    chain_row_ref,
+    rows_ref,
     distance_ref,
     offset_ref,
     query_ref,
@@ -347,8 +357,7 @@
     frame_ref,
     table_ref,
 ):
-    rows, total, _ = pair_ref.shape
-    heads = weight_ref.shape[1]
+    rows, heads, total = bias_ref.shape
     me = lax.axis_index("res")
     table_ref[...] = jnp.zeros_like(table_ref)
     for c in range(3):
@@ -389,9 +398,8 @@
             query_ref[:, pl.ds(at, width)] = part.reshape(rows * heads, width)
     square = jnp.sum(square, axis=-1, keepdims=True)
     for r in range(rows):
-        bias = dot_rows(bias_ref[...], pair_ref[r]).astype(jnp.bfloat16).astype(jnp.float32)
-        within = jnp.where(chain_row_ref[...] == chain_ref[me * rows + r], 1.0, 0.0)
-        base_ref[r] = LOGIT_FACTOR * (bias + chain_offset * within - weight * square[r])
+        within = jnp.where(rows_ref[pl.ds(0, 1), :] == chain_ref[me * rows + r], 1.0, 0.0)
+        base_ref[r] = LOGIT_FACTOR * (bias_ref[r] + chain_offset * within - weight * square[r])
 
 
 def attention_kernel(
@@ -404,7 +412,7 @@
     frame_ref,
     rot_ref,
     trans_ref,
-    present_ref,
+    rows_ref,
     distance_ref,
     pair_ref,
     single_ref,
@@ -442,7 +450,7 @@
     weight = 0.5 * LOGIT_FACTOR * math.sqrt(2.0 / (9.0 * PQ)) * as_column(distance_ref[...])
     logits = dot(query_ref[...], keys).reshape(rows, heads, total)
     logits = LOGIT_FACTOR * logits + base_ref[...] - (weight * square)[None]
-    present = present_ref[...] > 0
+    present = rows_ref[pl.ds(1, 1), :] > 0
     logits = jnp.where(present[None], logits, -1000000000.0)
     logits = logits.reshape(rows * heads, total)
     exponent = jnp.exp(logits - jnp.max(logits, axis=-1, keepdims=True))
@@ -492,7 +500,7 @@
 
 def frame_kernel(
     step_ref,
-    live_ref,
+    rows_ref,
     single_ref,
     velocity_ref,
     rot_ref,
@@ -509,7 +517,7 @@
         for d in range(3):
             table_ref[pl.ds(3 * c + d, 1), :] = rot_ref[c, pl.ds(d, 1), :]
         table_ref[pl.ds(9 + c, 1), :] = trans_ref[pl.ds(c, 1), :]
-    table_ref[pl.ds(12, 1), :] = jnp.where(live_ref[...] > 0, 1.0, 0.0)
+    table_ref[pl.ds(12, 1), :] = jnp.where(rows_ref[pl.ds(1, 1), :] > 0, 1.0, 0.0)
     row = lax.broadcasted_iota(jnp.int32, (rows, total), 0)
     column = lax.broadcasted_iota(jnp.int32, (rows, total), 1)
     chosen = jnp.where(column == row + me * rows, 1.0, 0.0)
@@ -577,14 +585,26 @@
     rows, total, feats = pair.shape
     heads = single_projection_weight.shape[1]
     width = single.shape[1]
-    offsets, (held, other) = gather_blocks(single, total // rows)
+    table = jnp.stack([residue_chain_index, residue_move_mask])
+    gain = single_norm_gain[None]
+    offsets, held, (table, gain) = gather_most(single, total // rows, (table, gain))
     weight = jnp.transpose(single_projection_weight, (2, 1, 0))
     local_weight = jnp.transpose(local_output_weight, (1, 0, 2))
     distance = head_distance_weight[None]
     depth = heads * (HEAD_FEATURES + 9 * PQ)
+    bias = pl.pallas_call(
+        bias_kernel,
+        in_specs=in_vmem(2),
+        out_specs=pl.BlockSpec(memory_space=pltpu.VMEM),
+        out_shape=jax.ShapeDtypeStruct((rows, heads, total), jnp.float32),
+        compiler_params=pltpu.CompilerParams(vmem_limit_bytes=16 * 1024 * 1024),
+        cost_estimate=pl.CostEstimate(flops=10**9, bytes_accessed=6 * 10**6, transcendentals=0),
+    )(jnp.transpose(head_bias_weight), pair)
+    held, bias, local_weight = lax.optimization_barrier((held, bias, local_weight))
+    other = exchange(held, total // rows, 1)
     query, base, frame = pl.pallas_call(
         query_kernel,
-        in_specs=[pl.BlockSpec(memory_space=pltpu.SMEM)] + in_vmem(9),
+        in_specs=[pl.BlockSpec(memory_space=pltpu.SMEM)] + in_vmem(8),
         out_specs=tuple(in_vmem(3)),
         out_shape=(
             jax.ShapeDtypeStruct((rows * heads, depth), jnp.bfloat16),
@@ -596,13 +616,12 @@
         cost_estimate=pl.CostEstimate(flops=10**9, bytes_accessed=6 * 10**6, transcendentals=0),
     )(
         residue_chain_index,
-        pair,
+        bias,
         single,
         weight,
-        jnp.transpose(head_bias_weight),
         rotations,
         translations,
-        residue_chain_index[None],
+        table,
         distance,
         chain_logit_offset[None],
     )
@@ -630,17 +649,17 @@
         frame,
         rotations,
         translations,
-        residue_move_mask[None],
+        table,
         distance,
         pair,
         single,
         local_weight,
         pair_output_weight.reshape(heads * feats, width),
-        single_norm_gain[None],
+        gain,
         left_pair_weight,
         right_pair_weight,
     )
-    velocity_rows = jnp.pad(jnp.transpose(frame_velocity_weight), ((0, 2), (0, 0)))
+    velocity_rows = jnp.transpose(frame_velocity_weight)
     rot_out, trans_out = pl.pallas_call(
         frame_kernel,
         in_specs=[pl.BlockSpec(memory_space=pltpu.SMEM)] + in_vmem(5),
@@ -650,16 +669,17 @@
             jax.ShapeDtypeStruct((3, rows), jnp.float32),
         ),
         scratch_shapes=[pltpu.VMEM((16, total), jnp.float32)],
+        compiler_params=pltpu.CompilerParams(vmem_limit_bytes=4 * 1024 * 1024),
         cost_estimate=pl.CostEstimate(flops=10**6, bytes_accessed=10**5, transcendentals=0),
     )(
         timestep,
-        residue_move_mask[None],
+        table,
         single_out,
         velocity_rows,
         rotations,
         translations,
     )
-    return single_out, rot_out, trans_out, left_proj, right_proj
+    return single_out, rot_out, trans_out, left_proj, right_proj, table, 1
 
 
 def attend_split(
@@ -694,7 +714,7 @@
     offset = 3 * HEAD_FEATURES
     feat_count = 2 * HEAD_FEATURES + 3 * PQ + 3 * PV
     count = total // rows_dev
-    every_single = sorted_blocks(*gather_blocks(single, count)).reshape(total, -1)
+    every_single = sorted_blocks(*gather_blocks(single, count)[:2]).reshape(total, -1)
     every_proj = jnp.einsum(
         "nd,dhf->nhf", every_single, single_projection_weight, preferred_element_type=jnp.float32
     )
@@ -761,7 +781,8 @@
     right_proj = jnp.dot(single_out, right_pair_weight, preferred_element_type=jnp.float32).astype(
         jnp.bfloat16
     )
-    return single_out, rot_out, trans_out, left_proj, right_proj
+    live_rows = residue_move_mask[None]
+    return single_out, rot_out, trans_out, left_proj, right_proj, live_rows, 0
 
 
 def shards(
@@ -790,7 +811,7 @@
     rows_dev = single.shape[0]
     count = rotations.shape[2] // rows_dev
     whole_heads = lax.axis_size("head") == 1 and count >= 16 and count & (count - 1) == 0
-    single_out, rot_out, trans_out, left_proj, right_proj = (
+    single_out, rot_out, trans_out, left_proj, right_proj, live_rows, live_at = (
         attend if whole_heads else attend_split
     )(
         single,
@@ -811,7 +832,7 @@
         left_pair_weight,
         right_pair_weight,
     )
-    offsets, blocks = gather_blocks(right_proj, count)
+    offsets, blocks, _ = gather_blocks(right_proj, count)
     if offsets is None:
         blocks = (blocks,)
     else:
@@ -820,6 +841,8 @@
         pair,
         left_proj,
         residue_move_mask,
+        live_rows,
+        live_at,
         pair_norm_gain,
         transition_hidden_weight,
         transition_middle_weight,

time: 50.6 us -> 47 us (0.929)
  waiting for transfers between devices: 9.28 us -> 6.18 us
    ppermute x10, waiting for transfers between devices: 9.28 us -> 6.18 us  [exchange(): return lax.ppermute(block, 'res', [(k, k ^ step) for k in range(count)])]
    another operation x0 -> x2, local copies, waits for them, and re-layouts: none -> 1.37 us  [attend(): table = jnp.stack([residue_chain_index, residue_move_mask])]
    pallas_call x0 -> x1, Pallas kernels: none -> 0.91 us  [attend(): pl.pallas_call(bias_kernel, in_specs=in_vmem(2), out_specs=pl.BlockSpec(m...]
    pallas_call x1, Pallas kernels: 1.58 us -> 0.82 us  [attend(): pl.pallas_call(frame_kernel, in_specs=[pl.BlockSpec(memory_space=pltpu.SM...]
    broadcast_in_dim x3 -> x1, local copies, waits for them, and re-layouts: 1.37 us -> 0.69 us  [attend(): gain = single_norm_gain[None]]
    pad x1 -> x0, local copies, waits for them, and re-layouts: 0.6 us -> none  [attend(): jnp.pad(jnp.transpose(frame_velocity_weight), ((0, 2), (0, 0)))]
    pallas_call x1, Pallas kernels: 1.86 us -> 1.28 us  [attend(): pl.pallas_call(query_kernel, in_specs=[pl.BlockSpec(memory_space=pltpu.SM...]
    unnamed x53 -> x43, local copies, waits for them, and re-layouts: 5.03 us -> 4.83 us
  transfers between devices with their start and end apart: 10 -> 10, of which waited for: 7 -> 4; matrix products, arithmetic and copies ran while one was open for 9% -> 5% of each run, Pallas kernels for 7% -> 6%
where the time goes in v3:
time: 47 us; the launch traced here: 46.6 us
  Pallas kernels  17.4 us (37%)
  starting transfers between devices  13.8 us (29%)
  local copies, waits for them, and re-layouts  6.88 us (15%)
  waiting for transfers between devices  6.18 us (13%)
  between operations  1.49 us (3%)
  other arithmetic  0.78 us (2%)
    ppermute x10, starting transfers between devices, exchange(): return lax.ppermute(block, 'res', [(k, k ^ step) for k in range(count)])  13.8 us
    pallas_call x1, Pallas kernels, pair_transition(): pl.pallas_call(kernel, grid=(rows_dev // rows_block,), in_specs=[pl.Block...  9.45 us
    ppermute x10, waiting for transfers between devices, exchange(): return lax.ppermute(block, 'res', [(k, k ^ step) for k in range(count)])  6.18 us
    pallas_call x1, Pallas kernels, attend(): pl.pallas_call(functools.partial(attention_kernel, offsets), in_specs=in_...  4.93 us
    unnamed x43, local copies, waits for them, and re-layouts  4.83 us
    another operation x2, local copies, waits for them, and re-layouts, attend(): table = jnp.stack([residue_chain_index, residue_move_mask])  1.37 us
    pallas_call x1, Pallas kernels, attend(): pl.pallas_call(query_kernel, in_specs=[pl.BlockSpec(memory_space=pltpu.SM...  1.28 us
  transfers between devices with their start and end apart: 10, of which 4 were waited for; matrix products, arithmetic and copies ran while one was open for 5% of the time, Pallas kernels for 6%

profile of v3, /device:TPU:0, one launch (start us, length us, event | category | flops | bytes accessed | tf_op | source)
XLA Modules:
  0.0 46.6 jit_solution(4731115421233946060)
XLA Ops:
  0.6 3.0 %collective-permute-start = (bf16[1,24,384]{2,1,0:T(8,128)(2,1)}, bf16[1,24,384]{2,1,0:T(8,128)(2,1)S(1)}, u32[]{:S(2)}, u32[]{:S(2)}) collective-permute-start(bf16[1,24,384]{2,1,0:T(8,128)(2,1)} %bitcast.17), channel_id=1, source_target_pairs={{0,2},{1,3},{2,0},{3,1},{4,6},{5,7},{6,4},{7,5},{8,10},{9,11},{10,... | collective-permute-start | bytes 55304 | tf_op jit(solution)/shard_map/ppermute | solution.py:145
  3.6 0.7 %stack.10 = s32[1,384]{1,0:T(1,128)S(1)} reshape(s32[384]{0:T(512)} %live_ref.1) | data formatting | bytes 3072 | tf_op jit(solution)/shard_map/stack | solution.py:588
  4.3 0.7 %stack.9 = s32[1,384]{1,0:T(1,128)S(1)} reshape(s32[384]{0:T(512)} %chain_ref.1) | data formatting | bytes 3072 | tf_op jit(solution)/shard_map/stack | solution.py:588
  5.0 0.7 %broadcast_in_dim.19.gain_ref = f32[1,384]{1,0:T(1,128)S(1)} reshape(f32[384]{0:T(512)} %param.34) | data formatting | bytes 3072 | tf_op jit(solution)/shard_map/broadcast_in_dim | solution.py:589
  5.7 0.7 %pad_maximum_fusion.2 = bf16[2,24,384]{2,1,0:T(8,128)(2,1)S(1)} fusion(bf16[1,24,384]{2,1,0:T(8,128)(2,1)S(1)} %collective-permute-done, bf16[1,24,384]{2,1,0:T(8,128)(2,1)} %bitcast.18), kind=kLoop, calls=%fused_computation.3 | loop fusion | flops 18432 | bytes 73728 | tf_op jit(solution)/shard_map/concatenate | solution.py:153
  6.4 4.0 %collective-permute-start.1 = (bf16[2,24,384]{2,1,0:T(8,128)(2,1)S(1)}, bf16[2,24,384]{2,1,0:T(8,128)(2,1)S(1)}, u32[]{:S(2)}, u32[]{:S(2)}) collective-permute-start(bf16[2,24,384]{2,1,0:T(8,128)(2,1)S(1)} %pad_maximum_fusion.2), channel_id=1, source_target_pairs={{0,12},{1,13},{2,14},{3,15},{4,8},{5,9},{6,10},{7,11},{8,4},{9,5},... | collective-permute-start | bytes 110600 | tf_op jit(solution)/shard_map/ppermute | solution.py:145
  10.4 0.6 %collective-permute-start.3 = (bf16[2,24,384]{2,1,0:T(8,128)(2,1)S(1)}, bf16[2,24,384]{2,1,0:T(8,128)(2,1)S(1)}, u32[]{:S(2)}, u32[]{:S(2)}) collective-permute-start(bf16[2,24,384]{2,1,0:T(8,128)(2,1)S(1)} %pad_maximum_fusion.2), channel_id=1, source_target_pairs={{0,4},{1,5},{2,6},{3,7},{4,0},{5,1},{6,2},{7,3},{8,12},{9,13},{10,... | collective-permute-start | bytes 110600 | tf_op jit(solution)/shard_map/ppermute | solution.py:145
  11.1 1.7 %copy-done = bf16[24,384,128]{2,1,0:T(8,128)(2,1)S(1)} copy-done((bf16[24,384,128]{2,1,0:T(8,128)(2,1)S(1)}, bf16[24,384,128]{2,1,0:T(8,128)(2,1)}, u32[]{:S(2)}) %copy-start) | copy-done | bytes 2359320
  12.8 0.7 %copy-done.17 = bf16[128,16]{0,1:T(8,128)(2,1)S(1)} copy-done((bf16[128,16]{0,1:T(8,128)(2,1)S(1)}, bf16[128,16]{0,1:T(8,128)(2,1)}, u32[]{:S(2)}) %copy-start.17) | copy-done | bytes 4120
  13.4 0.9 %shard_map.228.bias_ref = f32[24,16,384]{2,1,0:T(8,128)S(1)} custom-call(bf16[16,128]{1,0:T(8,128)(2,1)S(1)} %bitcast.25, bf16[24,384,128]{2,1,0:T(8,128)(2,1)S(1)} %copy-done), custom_call_target="tpu_custom_call" | custom-call | flops 1000000000 | bytes 6000000 | tf_op jit(solution)/shard_map/pallas_call | solution.py:595
  14.4 0.2 copy-done.20
  14.6 0.0 copy-start.13
  14.6 0.0 copy-start.18
  14.6 0.5 copy.27
  15.1 0.2 collective-permute-done.2
  15.3 0.1 collective-permute-start.4
  15.4 0.6 %copy-done.2 = bf16[384,16,132]{0,1,2:T(8,128)(2,1)S(1)} copy-done((bf16[384,16,132]{0,1,2:T(8,128)(2,1)S(1)}, bf16[384,16,132]{0,1,2:T(8,128)(2,1)}, u32[]{:S(2)}) %copy-start.2) | copy-done | bytes 1622040
  16.0 0.0 copy-start.1
  16.0 1.3 %shard_map.229 = (bf16[384,1408]{1,0:T(8,128)(2,1)S(1)}, f32[24,16,384]{2,1,0:T(8,128)S(1)}, f32[24,16]{1,0:T(8,128)S(1)}) custom-call(s32[384]{0:T(512)S(1)} %copy-done.11, f32[24,16,384]{2,1,0:T(8,128)S(1)} %shard_map.228.bias_ref, bf16[24,384]{1,0:T(8,128)(2,1)S(1)} %copy-done.7, bf16[132,16,384]{2,1,0:T(8,128)(2,1)S(1)} %bitcast.14, ...), custom_call_target="tpu_custom_call" | custom-call | flops 1000000000 | bytes 6000000 | tf_op jit(solution)/shard_map/pallas_call | solution.py:605
  17.4 0.5 copy-done.1
  17.8 4.9 %shard_map.230 = (bf16[24,384]{1,0:T(8,128)(2,1)}, bf16[24,128]{1,0:T(8,128)(2,1)S(1)}, bf16[24,128]{1,0:T(8,128)(2,1)S(1)}) custom-call(bf16[8,24,384]{2,1,0:T(8,128)(2,1)S(1)} %pad_maximum_fusion.held_ref, bf16[8,24,384]{2,1,0:T(8,128)(2,1)S(1)} %collective-permute-done.4.other_ref, bf16[132,16,384]{2,1,0:T(8,128)(2,1)S(1)} %bitcast.15, ...), custom_call_target="tpu_custom_call" | custom-call | flops 2000000000 | bytes 10000000 | tf_op jit(solution)/shard_map/pallas_call | solution.py:628
  22.8 1.6 %collective-permute-start.5 = (bf16[1,24,128]{2,1,0:T(8,128)(2,1)S(1)}, bf16[1,24,128]{2,1,0:T(8,128)(2,1)S(1)}, u32[]{:S(2)}, u32[]{:S(2)}) collective-permute-start(bf16[1,24,128]{2,1,0:T(8,128)(2,1)S(1)} %bitcast.20), channel_id=1, source_target_pairs={{0,2},{1,3},{2,0},{3,1},{4,6},{5,7},{6,4},{7,5},{8,10},{9,11},{10,... | collective-permute-start | bytes 18440 | tf_op jit(solution)/shard_map/ppermute | solution.py:145
  24.4 2.0 %collective-permute-done.5 = bf16[1,24,128]{2,1,0:T(8,128)(2,1)S(1)} collective-permute-done((bf16[1,24,128]{2,1,0:T(8,128)(2,1)S(1)}, bf16[1,24,128]{2,1,0:T(8,128)(2,1)S(1)}, u32[]{:S(2)}, u32[]{:S(2)}) %collective-permute-start.5) | collective-permute-done | bytes 6176 | tf_op jit(solution)/shard_map/ppermute | solution.py:145
  26.4 3.8 %collective-permute-start.6 = (bf16[2,24,128]{2,1,0:T(8,128)(2,1)S(1)}, bf16[2,24,128]{2,1,0:T(8,128)(2,1)S(1)}, u32[]{:S(2)}, u32[]{:S(2)}) collective-permute-start(bf16[2,24,128]{2,1,0:T(8,128)(2,1)S(1)} %pad_maximum_fusion.3), channel_id=1, source_target_pairs={{0,12},{1,13},{2,14},{3,15},{4,8},{5,9},{6,10},{7,11},{8,4},{9,5},... | collective-permute-start | bytes 36872 | tf_op jit(solution)/shard_map/ppermute | solution.py:145
  30.2 0.6 %collective-permute-start.8 = (bf16[2,24,128]{2,1,0:T(8,128)(2,1)S(1)}, bf16[2,24,128]{2,1,0:T(8,128)(2,1)S(1)}, u32[]{:S(2)}, u32[]{:S(2)}) collective-permute-start(bf16[2,24,128]{2,1,0:T(8,128)(2,1)S(1)} %pad_maximum_fusion.3), channel_id=1, source_target_pairs={{0,4},{1,5},{2,6},{3,7},{4,0},{5,1},{6,2},{7,3},{8,12},{9,13},{10,... | collective-permute-start | bytes 36872 | tf_op jit(solution)/shard_map/ppermute | solution.py:145
  30.8 1.1 %collective-permute-done.6 = bf16[2,24,128]{2,1,0:T(8,128)(2,1)S(1)} collective-permute-done((bf16[2,24,128]{2,1,0:T(8,128)(2,1)S(1)}, bf16[2,24,128]{2,1,0:T(8,128)(2,1)S(1)}, u32[]{:S(2)}, u32[]{:S(2)}) %collective-permute-start.6) | collective-permute-done | bytes 12320 | tf_op jit(solution)/shard_map/ppermute | solution.py:145
  31.9 2.9 %collective-permute-done.7 = bf16[2,24,128]{2,1,0:T(8,128)(2,1)S(1)} collective-permute-done((bf16[2,24,128]{2,1,0:T(8,128)(2,1)S(1)}, bf16[2,24,128]{2,1,0:T(8,128)(2,1)S(1)}, u32[]{:S(2)}, u32[]{:S(2)}) %collective-permute-start.7) | collective-permute-done | bytes 12320 | tf_op jit(solution)/shard_map/ppermute | solution.py:145
  34.8 0.1 collective-permute-start.9
  35.5 0.0 copy-start.9
  35.5 0.7 %copy-done.9 = bf16[24,384]{1,0:T(8,128)(2,1)S(1)} copy-done((bf16[24,384]{1,0:T(8,128)(2,1)S(1)}, bf16[24,384]{1,0:T(8,128)(2,1)}, u32[]{:S(2)}) %copy-start.9) | copy-done | bytes 18456
  36.2 0.8 %shard_map.231 = (f32[3,3,24]{2,1,0:T(4,128)}, f32[3,24]{1,0:T(4,128)}) custom-call(s32[1]{0:T(128)S(6)} %copy.28.step_ref, s32[2,384]{1,0:T(2,128)S(1)} %pad_add_fusion.rows_ref.live_row_ref, bf16[24,384]{1,0:T(8,128)(2,1)S(1)} %copy-done.9, bf16[6,384]{1,0:T(8,128)(2,1)S(1)} %bitcast.19, f32[3,3,384]{2,1,0:T(4,128)S(1)} %copy-done.6, f32[3,384]{1,0:T(4,128)S(1)} %copy-done.8), custom_call_target="tpu_custom_call" | custom-call | flops 1000000 | bytes 100000 | tf_op jit(solution)/shard_map/pallas_call | solution.py:663
  37.1 9.4 %shard_map.232 = bf16[24,384,128]{2,1,0:T(8,128)(2,1)} custom-call(s32[384]{0:T(512)S(1)} %copy-done.12, bf16[24,384,128]{2,1,0:T(8,128)(2,1)S(1)} %copy-done.1, bf16[6,4,128]{2,1,0:T(4,128)(2,1)S(1)} %bitcast.24, s32[2,384]{1,0:T(2,128)S(1)} %pad_add_fusion.rows_ref.live_row_ref, f32[1,128]{1,0:T(1,128)S(1)} %bitcast.27, bf16[128,256]{1,0:T(8,128)(2,1)S(1)} %copy-done.15, ...), custom_call_target="tpu_custom_call" | custom-call | flops 3019898880 | bytes 4718592 | tf_op jit(solution)/shard_map/pallas_call | solution.py:264
  (44 shorter events, 0.1 us)
Async XLA Ops:
  0.6 5.1 %collective-permute-start = (bf16[1,24,384]{2,1,0:T(8,128)(2,1)}, bf16[1,24,384]{2,1,0:T(8,128)(2,1)S(1)}, u32[]{:S(2)}, u32[]{:S(2)}) collective-permute-start(bf16[1,24,384]{2,1,0:T(8,128)(2,1)} %bitcast.17), channel_id=1, source_target_pairs={{0,2},{1,3},{2,0},{3,1},{4,6},{5,7},{6,4},{7,5},{8,10},{9,11},{10,... | collective-permute-start | bytes 55304 | tf_op jit(solution)/shard_map/ppermute | solution.py:145
  6.4 8.6 %collective-permute-start.1 = (bf16[2,24,384]{2,1,0:T(8,128)(2,1)S(1)}, bf16[2,24,384]{2,1,0:T(8,128)(2,1)S(1)}, u32[]{:S(2)}, u32[]{:S(2)}) collective-permute-start(bf16[2,24,384]{2,1,0:T(8,128)(2,1)S(1)} %pad_maximum_fusion.2), channel_id=1, source_target_pairs={{0,12},{1,13},{2,14},{3,15},{4,8},{5,9},{6,10},{7,11},{8,4},{9,5},... | collective-permute-start | bytes 110600 | tf_op jit(solution)/shard_map/ppermute | solution.py:145
  10.4 4.9 %collective-permute-start.2 = (bf16[2,24,384]{2,1,0:T(8,128)(2,1)S(1)}, bf16[2,24,384]{2,1,0:T(8,128)(2,1)S(1)}, u32[]{:S(2)}, u32[]{:S(2)}) collective-permute-start(bf16[2,24,384]{2,1,0:T(8,128)(2,1)S(1)} %pad_maximum_fusion.2), channel_id=1, source_target_pairs={{0,8},{1,9},{2,10},{3,11},{4,12},{5,13},{6,14},{7,15},{8,0},{9,1},... | collective-permute-start | bytes 110600 | tf_op jit(solution)/shard_map/ppermute | solution.py:145
  10.4 4.9 %collective-permute-start.3 = (bf16[2,24,384]{2,1,0:T(8,128)(2,1)S(1)}, bf16[2,24,384]{2,1,0:T(8,128)(2,1)S(1)}, u32[]{:S(2)}, u32[]{:S(2)}) collective-permute-start(bf16[2,24,384]{2,1,0:T(8,128)(2,1)S(1)} %pad_maximum_fusion.2), channel_id=1, source_target_pairs={{0,4},{1,5},{2,6},{3,7},{4,0},{5,1},{6,2},{7,3},{8,12},{9,13},{10,... | collective-permute-start | bytes 110600 | tf_op jit(solution)/shard_map/ppermute | solution.py:145
  11.1 1.7 %copy-start = (bf16[24,384,128]{2,1,0:T(8,128)(2,1)S(1)}, bf16[24,384,128]{2,1,0:T(8,128)(2,1)}, u32[]{:S(2)}) copy-start(bf16[24,384,128]{2,1,0:T(8,128)(2,1)} %pair_ref.5) | copy-start | bytes 7077892
  12.8 0.7 %copy-start.17 = (bf16[128,16]{0,1:T(8,128)(2,1)S(1)}, bf16[128,16]{0,1:T(8,128)(2,1)}, u32[]{:S(2)}) copy-start(bf16[128,16]{0,1:T(8,128)(2,1)} %param.29) | copy-start | bytes 12292
  13.4 1.1 %copy-start.20 = (bf16[16,64,384]{2,1,0:T(8,128)(2,1)S(1)}, bf16[16,64,384]{2,1,0:T(8,128)(2,1)}, u32[]{:S(2)}) copy-start(bf16[16,64,384]{2,1,0:T(8,128)(2,1)} %param.32) | copy-start | bytes 2359300
  13.4 2.0 %copy-start.7 = (bf16[24,384]{1,0:T(8,128)(2,1)S(1)}, bf16[24,384]{1,0:T(8,128)(2,1)}, u32[]{:S(2)}) copy-start(bf16[24,384]{1,0:T(8,128)(2,1)} %single_ref.3) | copy-start | bytes 55300
  13.4 3.9 %copy-start.4 = (bf16[384,128]{1,0:T(8,128)(2,1)S(1)}, bf16[384,128]{1,0:T(8,128)(2,1)}, u32[]{:S(2)}) copy-start(bf16[384,128]{1,0:T(8,128)(2,1)} %left_ref.1) | copy-start | bytes 294916
  13.4 3.9 %copy-start.5 = (bf16[384,128]{1,0:T(8,128)(2,1)S(1)}, bf16[384,128]{1,0:T(8,128)(2,1)}, u32[]{:S(2)}) copy-start(bf16[384,128]{1,0:T(8,128)(2,1)} %right_ref.1) | copy-start | bytes 294916
  14.6 1.4 %copy-start.2 = (bf16[384,16,132]{0,1,2:T(8,128)(2,1)S(1)}, bf16[384,16,132]{0,1,2:T(8,128)(2,1)}, u32[]{:S(2)}) copy-start(bf16[384,16,132]{0,1,2:T(8,128)(2,1)} %param.28) | copy-start | bytes 4866052
  14.6 1.4 %copy-start.6 = (f32[3,3,384]{2,1,0:T(4,128)S(1)}, f32[3,3,384]{2,1,0:T(4,128)}, u32[]{:S(2)}) copy-start(f32[3,3,384]{2,1,0:T(4,128)} %rot_ref.5) | copy-start | bytes 41476
  14.6 1.4 %copy-start.8 = (f32[3,384]{1,0:T(4,128)S(1)}, f32[3,384]{1,0:T(4,128)}, u32[]{:S(2)}) copy-start(f32[3,384]{1,0:T(4,128)} %trans_ref.5) | copy-start | bytes 13828
  14.6 1.4 %copy-start.11 = (s32[384]{0:T(512)S(1)}, s32[384]{0:T(512)}, u32[]{:S(2)}) copy-start(s32[384]{0:T(512)} %chain_ref.1) | copy-start | bytes 4612
  14.6 1.4 %copy-start.13 = (f32[16]{0:T(128)S(1)}, f32[16]{0:T(128)}, u32[]{:S(2)}) copy-start(f32[16]{0:T(128)} %param.30) | copy-start | bytes 196
  14.6 1.4 %copy-start.18 = (f32[16]{0:T(128)S(1)}, f32[16]{0:T(128)}, u32[]{:S(2)}) copy-start(f32[16]{0:T(128)} %param.31) | copy-start | bytes 196
  15.3 2.0 %copy-start.3 = (bf16[16,128,384]{2,1,0:T(8,128)(2,1)S(1)}, bf16[16,128,384]{2,1,0:T(8,128)(2,1)}, u32[]{:S(2)}) copy-start(bf16[16,128,384]{2,1,0:T(8,128)(2,1)} %param.33) | copy-start | bytes 4718596
  15.3 2.0 %collective-permute-start.4 = (bf16[8,24,384]{2,1,0:T(8,128)(2,1)S(1)}, bf16[8,24,384]{2,1,0:T(8,128)(2,1)S(1)}, u32[]{:S(2)}, u32[]{:S(2)}) collective-permute-start(bf16[8,24,384]{2,1,0:T(8,128)(2,1)S(1)} %pad_maximum_fusion.held_ref), channel_id=1, source_target_pairs={{0,1},{1,0},{2,3},{3,2},{4,5},{5,4},{6,7},{7,6},{8,9},{9,8},{10,11... | collective-permute-start | bytes 442376 | tf_op jit(solution)/shard_map/ppermute | solution.py:145
  16.0 1.8 %copy-start.1 = (bf16[24,384,128]{2,1,0:T(8,128)(2,1)S(1)}, bf16[24,384,128]{2,1,0:T(8,128)(2,1)}, u32[]{:S(2)}) copy-start(bf16[24,384,128]{2,1,0:T(8,128)(2,1)} %pair_ref.5) | copy-start | bytes 7077892
  17.8 17.7 %copy-start.10 = (bf16[384,6]{0,1:T(8,128)(2,1)S(1)}, bf16[384,6]{0,1:T(8,128)(2,1)}, u32[]{:S(2)}) copy-start(bf16[384,6]{0,1:T(8,128)(2,1)} %param.35) | copy-start | bytes 13828
  17.8 19.3 %copy-start.12 = (s32[384]{0:T(512)S(1)}, s32[384]{0:T(512)}, u32[]{:S(2)}) copy-start(s32[384]{0:T(512)} %live_ref.1) | copy-start | bytes 4612
  17.8 19.3 %copy-start.14 = (bf16[256,256]{1,0:T(8,128)(2,1)S(1)}, bf16[256,256]{1,0:T(8,128)(2,1)}, u32[]{:S(2)}) copy-start(bf16[256,256]{1,0:T(8,128)(2,1)} %middle_ref.1) | copy-start | bytes 393220
  17.8 19.3 %copy-start.15 = (bf16[128,256]{1,0:T(8,128)(2,1)S(1)}, bf16[128,256]{1,0:T(8,128)(2,1)}, u32[]{:S(2)}) copy-start(bf16[128,256]{1,0:T(8,128)(2,1)} %hidden_ref.1) | copy-start | bytes 196612
  17.8 19.3 %copy-start.16 = (bf16[256,128]{1,0:T(8,128)(2,1)S(1)}, bf16[256,128]{1,0:T(8,128)(2,1)}, u32[]{:S(2)}) copy-start(bf16[256,128]{1,0:T(8,128)(2,1)} %back_ref.1) | copy-start | bytes 196612
  17.8 19.3 %copy-start.19 = (f32[128]{0:T(128)S(1)}, f32[128]{0:T(128)}, u32[]{:S(2)}) copy-start(f32[128]{0:T(128)} %param.38) | copy-start | bytes 1540
  22.8 3.6 %collective-permute-start.5 = (bf16[1,24,128]{2,1,0:T(8,128)(2,1)S(1)}, bf16[1,24,128]{2,1,0:T(8,128)(2,1)S(1)}, u32[]{:S(2)}, u32[]{:S(2)}) collective-permute-start(bf16[1,24,128]{2,1,0:T(8,128)(2,1)S(1)} %bitcast.20), channel_id=1, source_target_pairs={{0,2},{1,3},{2,0},{3,1},{4,6},{5,7},{6,4},{7,5},{8,10},{9,11},{10,... | collective-permute-start | bytes 18440 | tf_op jit(solution)/shard_map/ppermute | solution.py:145
  26.4 5.5 %collective-permute-start.6 = (bf16[2,24,128]{2,1,0:T(8,128)(2,1)S(1)}, bf16[2,24,128]{2,1,0:T(8,128)(2,1)S(1)}, u32[]{:S(2)}, u32[]{:S(2)}) collective-permute-start(bf16[2,24,128]{2,1,0:T(8,128)(2,1)S(1)} %pad_maximum_fusion.3), channel_id=1, source_target_pairs={{0,12},{1,13},{2,14},{3,15},{4,8},{5,9},{6,10},{7,11},{8,4},{9,5},... | collective-permute-start | bytes 36872 | tf_op jit(solution)/shard_map/ppermute | solution.py:145
  30.2 4.6 %collective-permute-start.7 = (bf16[2,24,128]{2,1,0:T(8,128)(2,1)S(1)}, bf16[2,24,128]{2,1,0:T(8,128)(2,1)S(1)}, u32[]{:S(2)}, u32[]{:S(2)}) collective-permute-start(bf16[2,24,128]{2,1,0:T(8,128)(2,1)S(1)} %pad_maximum_fusion.3), channel_id=1, source_target_pairs={{0,8},{1,9},{2,10},{3,11},{4,12},{5,13},{6,14},{7,15},{8,0},{9,1},... | collective-permute-start | bytes 36872 | tf_op jit(solution)/shard_map/ppermute | solution.py:145
  30.2 4.6 %collective-permute-start.8 = (bf16[2,24,128]{2,1,0:T(8,128)(2,1)S(1)}, bf16[2,24,128]{2,1,0:T(8,128)(2,1)S(1)}, u32[]{:S(2)}, u32[]{:S(2)}) collective-permute-start(bf16[2,24,128]{2,1,0:T(8,128)(2,1)S(1)} %pad_maximum_fusion.3), channel_id=1, source_target_pairs={{0,4},{1,5},{2,6},{3,7},{4,0},{5,1},{6,2},{7,3},{8,12},{9,13},{10,... | collective-permute-start | bytes 36872 | tf_op jit(solution)/shard_map/ppermute | solution.py:145
  34.8 2.3 %collective-permute-start.9 = (bf16[8,24,128]{2,1,0:T(8,128)(2,1)S(1)}, bf16[8,24,128]{2,1,0:T(8,128)(2,1)S(1)}, u32[]{:S(2)}, u32[]{:S(2)}) collective-permute-start(bf16[8,24,128]{2,1,0:T(8,128)(2,1)S(1)} %pad_maximum_fusion.1.rest_0_), channel_id=1, source_target_pairs={{0,1},{1,0},{2,3},{3,2},{4,5},{5,4},{6,7},{7,6},{8,9},{9,8},{10,11... | collective-permute-start | bytes 147464 | tf_op jit(solution)/shard_map/ppermute | solution.py:145
  35.5 0.7 %copy-start.9 = (bf16[24,384]{1,0:T(8,128)(2,1)S(1)}, bf16[24,384]{1,0:T(8,128)(2,1)}, u32[]{:S(2)}) copy-start(bf16[24,384]{1,0:T(8,128)(2,1)} %get-tuple-element.14.single_ref) | copy-start | bytes 55300

commit v4 on v3

--- a/solution.py
+++ b/solution.py
@@ -184,6 +184,7 @@
 
 def transition_kernel(
     rows_block,
+    rows_part,
     rows_dev,
     offsets,
     live_at,
@@ -221,33 +222,33 @@
         centring_ref[...] = (jnp.where(across == down, 1.0, 0.0) - 1.0 / feats).astype(jnp.bfloat16)
 
     columns = pl.ds(pl.multiple_of(col_start, 8), cols)
-    pair = pair_ref[...].reshape(rows_block * cols, feats)
-    centred = jnp.dot(pair, centring_ref[...], preferred_element_type=jnp.float32)
+    right = right_ref[columns, :][None]
+    live_cols = live_cols_ref[columns, :][None]
     left = left_ref[...].astype(jnp.float32)
     left = left - jnp.mean(left, axis=-1, keepdims=True)
-    centred = centred.reshape(rows_block, cols, feats) + left[:, None, :] + right_ref[columns, :][None]
-    centred = centred.reshape(rows_block * cols, feats)
-    averaging = jnp.full((feats, feats), 1.0 / feats, jnp.bfloat16)
-    variance = jnp.dot(
-        (centred * centred).astype(jnp.bfloat16), averaging, preferred_element_type=jnp.float32
-    )
-    normed = (centred * lax.rsqrt(variance + 1e-05) * gain_ref[...]).astype(jnp.bfloat16)
-    hidden_one = jnp.maximum(
-        jnp.dot(normed, hidden_ref[...], preferred_element_type=jnp.float32).astype(jnp.bfloat16), 0
-    )
-    hidden_two = jnp.maximum(
-        jnp.dot(hidden_one, middle_ref[...], preferred_element_type=jnp.float32).astype(
-            jnp.bfloat16
-        ),
-        0,
-    )
-    branch = jnp.dot(hidden_two, back_ref[...], preferred_element_type=jnp.float32)
-    branch = branch.reshape(rows_block, cols, feats)
-    live_cols = live_cols_ref[columns, :]
-    for r in range(rows_block):
-        live = jnp.where(live_ref[me * rows_dev + step * rows_block + r] > 0, 1.0, 0.0)
-        out_ref[r] = (
-            pair_ref[r].astype(jnp.float32) + live * live_cols * branch[r]
+    for first in range(0, rows_block, rows_part):
+        at = step * rows_block + first
+        pair_rows = pair_ref[pl.ds(at, rows_part)]
+        pair = pair_rows.reshape(rows_part * cols, feats)
+        centred = jnp.dot(pair, centring_ref[...], preferred_element_type=jnp.float32)
+        centred = centred.reshape(rows_part, cols, feats)
+        centred = centred + left[first : first + rows_part][:, None, :] + right
+        variance = jnp.mean(centred * centred, axis=-1, keepdims=True)
+        scale = lax.rsqrt(variance + 1e-05)
+        gains = [
+            gain_ref[...] * jnp.where(live_ref[me * rows_dev + at + r] > 0, 1.0, 0.0)
+            for r in range(rows_part)
+        ]
+        normed = centred * scale * jnp.stack(gains)
+        normed = normed.astype(jnp.bfloat16).reshape(rows_part * cols, feats)
+        hidden_one = jnp.dot(normed, hidden_ref[...], preferred_element_type=jnp.float32)
+        hidden_one = jnp.maximum(hidden_one.astype(jnp.bfloat16), 0)
+        hidden_two = jnp.dot(hidden_one, middle_ref[...], preferred_element_type=jnp.float32)
+        hidden_two = jnp.maximum(hidden_two.astype(jnp.bfloat16), 0)
+        branch = jnp.dot(hidden_two, back_ref[...], preferred_element_type=jnp.float32)
+        branch = branch.reshape(rows_part, cols, feats)
+        out_ref[pl.ds(first, rows_part)] = (
+            pair_rows.astype(jnp.float32) + live_cols * branch
         ).astype(jnp.bfloat16)
 
 
@@ -256,17 +257,20 @@
 ):
     rows_dev, cols, feats = pair.shape
     total = move_mask.shape[0]
-    rows_block = math.gcd(rows_dev, max(1, 1536 // cols))
+    rows_part = math.gcd(rows_dev, max(1, 1536 // cols))
+    rows_block = rows_part * math.gcd(rows_dev // rows_part, 3)
     left_wide = left_proj.reshape(rows_dev // rows_block, rows_block, feats)
     whole = lambda *shape: pl.BlockSpec(shape, lambda i: (0,) * len(shape))
-    kernel = functools.partial(transition_kernel, rows_block, rows_dev, offsets, live_at)
+    kernel = functools.partial(
+        transition_kernel, rows_block, rows_part, rows_dev, offsets, live_at
+    )
     macs = rows_dev * cols * (2 * feats * feats + 2 * feats * hidden.shape[1] + hidden.shape[1] ** 2)
     return pl.pallas_call(
         kernel,
         grid=(rows_dev // rows_block,),
         in_specs=[
             pl.BlockSpec(memory_space=pltpu.SMEM),
-            pl.BlockSpec((rows_block, cols, feats), lambda i: (i, 0, 0)),
+            pl.BlockSpec(memory_space=pltpu.VMEM),
             pl.BlockSpec((None, rows_block, feats), lambda i: (i, 0, 0)),
             whole(*live_rows.shape),
             whole(1, feats),
@@ -422,6 +426,7 @@
     left_ref,
     right_ref,
     out_ref,
+    copy_ref,
     left_out_ref,
     right_out_ref,
     every_ref,
@@ -494,12 +499,12 @@
     values = single_ref[...].astype(jnp.float32) + update[:rows] + update[rows:]
     single_out = layer_norm(values, gain_ref[...]).astype(jnp.bfloat16)
     out_ref[...] = single_out
+    copy_ref[...] = single_out
     left_out_ref[...] = dot(single_out, left_ref[...]).astype(jnp.bfloat16)
     right_out_ref[...] = dot(single_out, right_ref[...]).astype(jnp.bfloat16)
 
 
 def frame_kernel(
-    step_ref,
     rows_ref,
     single_ref,
     velocity_ref,
@@ -524,7 +529,7 @@
     frame = dot_rows(table_ref[...], chosen, HIGHEST)
     motion = dot_rows(velocity_ref[...], single_ref[...])
     live = frame[12:13]
-    ratio = 1.0 / jnp.full((1, rows), STEPS - step_ref[0], jnp.int32).astype(jnp.float32)
+    ratio = 1.0 / (STEPS - rows_ref[pl.ds(2, 1), :].astype(jnp.float32))[:, :rows]
     x, y, z = [ratio * jnp.tanh(motion[c : c + 1]) * live for c in range(3)]
     velocity = [ratio * motion[3 + c : 4 + c] * live for c in range(3)]
     angle_sq = x * x + y * y + z * z
@@ -585,7 +590,8 @@
     rows, total, feats = pair.shape
     heads = single_projection_weight.shape[1]
     width = single.shape[1]
-    table = jnp.stack([residue_chain_index, residue_move_mask])
+    step_row = jnp.broadcast_to(timestep, (total,))
+    table = jnp.stack([residue_chain_index, residue_move_mask, step_row])
     gain = single_norm_gain[None]
     offsets, held, (table, gain) = gather_most(single, total // rows, (table, gain))
     weight = jnp.transpose(single_projection_weight, (2, 1, 0))
@@ -625,11 +631,12 @@
         distance,
         chain_logit_offset[None],
     )
-    single_out, left_proj, right_proj = pl.pallas_call(
+    single_out, single_copy, left_proj, right_proj = pl.pallas_call(
         functools.partial(attention_kernel, offsets),
         in_specs=in_vmem(17),
-        out_specs=tuple(in_vmem(3)),
+        out_specs=tuple(in_vmem(4)),
         out_shape=(
+            jax.ShapeDtypeStruct((rows, width), jnp.bfloat16),
             jax.ShapeDtypeStruct((rows, width), jnp.bfloat16),
             jax.ShapeDtypeStruct((rows, feats), jnp.bfloat16),
             jax.ShapeDtypeStruct((rows, feats), jnp.bfloat16),
@@ -662,7 +669,7 @@
     velocity_rows = jnp.transpose(frame_velocity_weight)
     rot_out, trans_out = pl.pallas_call(
         frame_kernel,
-        in_specs=[pl.BlockSpec(memory_space=pltpu.SMEM)] + in_vmem(5),
+        in_specs=in_vmem(5),
         out_specs=tuple(in_vmem(2)),
         out_shape=(
             jax.ShapeDtypeStruct((3, 3, rows), jnp.float32),
@@ -672,9 +679,8 @@
         compiler_params=pltpu.CompilerParams(vmem_limit_bytes=4 * 1024 * 1024),
         cost_estimate=pl.CostEstimate(flops=10**6, bytes_accessed=10**5, transcendentals=0),
     )(
-        timestep,
         table,
-        single_out,
+        single_copy,
         velocity_rows,
         rotations,
         translations,

time: 47 us -> 44 us (0.936)
  Pallas kernels: 17.4 us -> 15.1 us
  starting transfers between devices: 13.8 us -> 13 us
  waiting for transfers between devices: 6.18 us -> 6.78 us
  local copies, waits for them, and re-layouts: 6.88 us -> 6.39 us
    pallas_call x1, Pallas kernels: 9.45 us -> 7.19 us  [pair_transition(): pl.pallas_call(kernel, grid=(rows_dev // rows_block,), in_specs=[pl.Block...]
    ppermute x10, starting transfers between devices: 13.8 us -> 13 us  [exchange(): return lax.ppermute(block, 'res', [(k, k ^ step) for k in range(count)])]
    ppermute x10, waiting for transfers between devices: 6.18 us -> 6.78 us  [exchange(): return lax.ppermute(block, 'res', [(k, k ^ step) for k in range(count)])]
    unnamed x43 -> x41, local copies, waits for them, and re-layouts: 4.83 us -> 4.26 us
    another operation x2 -> x3, local copies, waits for them, and re-layouts: 1.37 us -> 1.44 us  [attend(): table = jnp.stack([residue_chain_index, residue_move_mask, step_row])]
  transfers between devices with their start and end apart: 10 -> 10, of which waited for: 4 -> 5; matrix products, arithmetic and copies ran while one was open for 5% -> 6% of each run, Pallas kernels for 6% -> 7%
where the time goes in v4:
time: 44 us; the launch traced here: 43.6 us
  Pallas kernels  15.1 us (34%)
  starting transfers between devices  13 us (30%)
  waiting for transfers between devices  6.78 us (15%)
  local copies, waits for them, and re-layouts  6.39 us (15%)
  between operations  1.49 us (3%)
  other arithmetic  0.85 us (2%)
    ppermute x10, starting transfers between devices, exchange(): return lax.ppermute(block, 'res', [(k, k ^ step) for k in range(count)])  13 us
    pallas_call x1, Pallas kernels, pair_transition(): pl.pallas_call(kernel, grid=(rows_dev // rows_block,), in_specs=[pl.Block...  7.19 us
    ppermute x10, waiting for transfers between devices, exchange(): return lax.ppermute(block, 'res', [(k, k ^ step) for k in range(count)])  6.78 us
    pallas_call x1, Pallas kernels, attend(): pl.pallas_call(functools.partial(attention_kernel, offsets), in_specs=in_...  4.88 us
    unnamed x41, local copies, waits for them, and re-layouts  4.26 us
    another operation x3, local copies, waits for them, and re-layouts, attend(): table = jnp.stack([residue_chain_index, residue_move_mask, step_row])  1.44 us
    pallas_call x1, Pallas kernels, attend(): pl.pallas_call(query_kernel, in_specs=[pl.BlockSpec(memory_space=pltpu.SM...  1.28 us
    pallas_call x1, Pallas kernels, attend(): pl.pallas_call(bias_kernel, in_specs=in_vmem(2), out_specs=pl.BlockSpec(m...  0.91 us
  transfers between devices with their start and end apart: 10, of which 5 were waited for; matrix products, arithmetic and copies ran while one was open for 6% of the time, Pallas kernels for 7%

profile of v4, /device:TPU:0, one launch (start us, length us, event | category | flops | bytes accessed | tf_op | source)
XLA Modules:
  0.0 43.6 jit_solution(8630286514496146894)
XLA Ops:
  0.6 3.0 %collective-permute-start = (bf16[1,24,384]{2,1,0:T(8,128)(2,1)}, bf16[1,24,384]{2,1,0:T(8,128)(2,1)S(1)}, u32[]{:S(2)}, u32[]{:S(2)}) collective-permute-start(bf16[1,24,384]{2,1,0:T(8,128)(2,1)} %bitcast.17), channel_id=1, source_target_pairs={{0,2},{1,3},{2,0},{3,1},{4,6},{5,7},{6,4},{7,5},{8,10},{9,11},{10,... | collective-permute-start | bytes 55304 | tf_op jit(solution)/shard_map/ppermute | solution.py:145
  3.6 0.7 %stack.10 = s32[1,384]{1,0:T(1,128)S(1)} reshape(s32[384]{0:T(512)} %live_ref.1) | data formatting | bytes 3072 | tf_op jit(solution)/shard_map/stack | solution.py:594
  4.3 0.7 %stack.9 = s32[1,384]{1,0:T(1,128)S(1)} reshape(s32[384]{0:T(512)} %chain_ref.1) | data formatting | bytes 3072 | tf_op jit(solution)/shard_map/stack | solution.py:594
  5.7 0.1 pad.12.clone
  5.7 0.1 add_add_fusion.rows_ref.live_row_ref
  5.8 0.7 %broadcast_in_dim.19.gain_ref = f32[1,384]{1,0:T(1,128)S(1)} reshape(f32[384]{0:T(512)} %param.34) | data formatting | bytes 3072 | tf_op jit(solution)/shard_map/broadcast_in_dim | solution.py:595
  6.5 0.7 %pad_maximum_fusion.2 = bf16[2,24,384]{2,1,0:T(8,128)(2,1)S(1)} fusion(bf16[1,24,384]{2,1,0:T(8,128)(2,1)S(1)} %collective-permute-done, bf16[1,24,384]{2,1,0:T(8,128)(2,1)} %bitcast.18), kind=kLoop, calls=%fused_computation.3 | loop fusion | flops 18432 | bytes 73728 | tf_op jit(solution)/shard_map/concatenate | solution.py:153
  7.2 3.6 %collective-permute-start.1 = (bf16[2,24,384]{2,1,0:T(8,128)(2,1)S(1)}, bf16[2,24,384]{2,1,0:T(8,128)(2,1)S(1)}, u32[]{:S(2)}, u32[]{:S(2)}) collective-permute-start(bf16[2,24,384]{2,1,0:T(8,128)(2,1)S(1)} %pad_maximum_fusion.2), channel_id=1, source_target_pairs={{0,12},{1,13},{2,14},{3,15},{4,8},{5,9},{6,10},{7,11},{8,4},{9,5},... | collective-permute-start | bytes 110600 | tf_op jit(solution)/shard_map/ppermute | solution.py:145
  10.8 0.8 %collective-permute-start.3 = (bf16[2,24,384]{2,1,0:T(8,128)(2,1)S(1)}, bf16[2,24,384]{2,1,0:T(8,128)(2,1)S(1)}, u32[]{:S(2)}, u32[]{:S(2)}) collective-permute-start(bf16[2,24,384]{2,1,0:T(8,128)(2,1)S(1)} %pad_maximum_fusion.2), channel_id=1, source_target_pairs={{0,4},{1,5},{2,6},{3,7},{4,0},{5,1},{6,2},{7,3},{8,12},{9,13},{10,... | collective-permute-start | bytes 110600 | tf_op jit(solution)/shard_map/ppermute | solution.py:145
  11.6 1.7 %copy-done = bf16[24,384,128]{2,1,0:T(8,128)(2,1)S(1)} copy-done((bf16[24,384,128]{2,1,0:T(8,128)(2,1)S(1)}, bf16[24,384,128]{2,1,0:T(8,128)(2,1)}, u32[]{:S(2)}) %copy-start) | copy-done | bytes 2359320
  13.3 0.7 %copy-done.16 = bf16[128,16]{0,1:T(8,128)(2,1)S(1)} copy-done((bf16[128,16]{0,1:T(8,128)(2,1)S(1)}, bf16[128,16]{0,1:T(8,128)(2,1)}, u32[]{:S(2)}) %copy-start.16) | copy-done | bytes 4120
  14.0 0.9 %shard_map.231.bias_ref = f32[24,16,384]{2,1,0:T(8,128)S(1)} custom-call(bf16[16,128]{1,0:T(8,128)(2,1)S(1)} %bitcast.24, bf16[24,384,128]{2,1,0:T(8,128)(2,1)S(1)} %copy-done), custom_call_target="tpu_custom_call" | custom-call | flops 1000000000 | bytes 6000000 | tf_op jit(solution)/shard_map/pallas_call | solution.py:601
  14.9 0.2 copy-done.19
  15.1 0.0 copy-start.12
  15.1 0.0 copy-start.17
  15.1 0.5 %copy.28 = bf16[16,64,384]{2,0,1:T(8,128)(2,1)S(1)} copy(bf16[16,64,384]{2,1,0:T(8,128)(2,1)S(1)} %copy-done.19) | data formatting | bytes 1572864 | tf_op args[11]
  15.6 0.1 collective-permute-done.2
  15.7 0.1 collective-permute-start.4
  15.8 0.7 %copy-done.2 = bf16[384,16,132]{0,1,2:T(8,128)(2,1)S(1)} copy-done((bf16[384,16,132]{0,1,2:T(8,128)(2,1)S(1)}, bf16[384,16,132]{0,1,2:T(8,128)(2,1)}, u32[]{:S(2)}) %copy-start.2) | copy-done | bytes 1622040
  16.6 1.3 %shard_map.232 = (bf16[384,1408]{1,0:T(8,128)(2,1)S(1)}, f32[24,16,384]{2,1,0:T(8,128)S(1)}, f32[24,16]{1,0:T(8,128)S(1)}) custom-call(s32[384]{0:T(512)S(1)} %copy-done.10, f32[24,16,384]{2,1,0:T(8,128)S(1)} %shard_map.231.bias_ref, bf16[24,384]{1,0:T(8,128)(2,1)S(1)} %copy-done.7, bf16[132,16,384]{2,1,0:T(8,128)(2,1)S(1)} %bitcast.14, ...), custom_call_target="tpu_custom_call" | custom-call | flops 1000000000 | bytes 6000000 | tf_op jit(solution)/shard_map/pallas_call | solution.py:611
  17.9 0.4 %copy-done.1 = bf16[24,384,128]{2,1,0:T(8,128)(2,1)S(1)} copy-done((bf16[24,384,128]{2,1,0:T(8,128)(2,1)S(1)}, bf16[24,384,128]{2,1,0:T(8,128)(2,1)}, u32[]{:S(2)}) %copy-start.1) | copy-done | bytes 2359320
  18.4 4.9 %shard_map.233 = (bf16[24,384]{1,0:T(8,128)(2,1)}, bf16[24,384]{1,0:T(8,128)(2,1)S(1)}, bf16[24,128]{1,0:T(8,128)(2,1)S(1)}, bf16[24,128]{1,0:T(8,128)(2,1)S(1)}) custom-call(bf16[8,24,384]{2,1,0:T(8,128)(2,1)S(1)} %pad_maximum_fusion.held_ref, bf16[8,24,384]{2,1,0:T(8,128)(2,1)S(1)} %collective-permute-done.4.other_ref, bf16[132,16,384]{2,1,0:T(8,128)(2,1)S(1)} %bitcast.15, ...), custom_call_target="tpu_custom_call" | custom-call | flops 2000000000 | bytes 10000000 | tf_op jit(solution)/shard_map/pallas_call | solution.py:634
  23.2 1.1 %collective-permute-start.5 = (bf16[1,24,128]{2,1,0:T(8,128)(2,1)S(1)}, bf16[1,24,128]{2,1,0:T(8,128)(2,1)S(1)}, u32[]{:S(2)}, u32[]{:S(2)}) collective-permute-start(bf16[1,24,128]{2,1,0:T(8,128)(2,1)S(1)} %bitcast.20), channel_id=1, source_target_pairs={{0,2},{1,3},{2,0},{3,1},{4,6},{5,7},{6,4},{7,5},{8,10},{9,11},{10,... | collective-permute-start | bytes 18440 | tf_op jit(solution)/shard_map/ppermute | solution.py:145
  24.4 2.5 %collective-permute-done.5 = bf16[1,24,128]{2,1,0:T(8,128)(2,1)S(1)} collective-permute-done((bf16[1,24,128]{2,1,0:T(8,128)(2,1)S(1)}, bf16[1,24,128]{2,1,0:T(8,128)(2,1)S(1)}, u32[]{:S(2)}, u32[]{:S(2)}) %collective-permute-start.5) | collective-permute-done | bytes 6176 | tf_op jit(solution)/shard_map/ppermute | solution.py:145
  26.9 3.6 %collective-permute-start.6 = (bf16[2,24,128]{2,1,0:T(8,128)(2,1)S(1)}, bf16[2,24,128]{2,1,0:T(8,128)(2,1)S(1)}, u32[]{:S(2)}, u32[]{:S(2)}) collective-permute-start(bf16[2,24,128]{2,1,0:T(8,128)(2,1)S(1)} %pad_maximum_fusion.3), channel_id=1, source_target_pairs={{0,12},{1,13},{2,14},{3,15},{4,8},{5,9},{6,10},{7,11},{8,4},{9,5},... | collective-permute-start | bytes 36872 | tf_op jit(solution)/shard_map/ppermute | solution.py:145
  30.5 0.8 %collective-permute-start.8 = (bf16[2,24,128]{2,1,0:T(8,128)(2,1)S(1)}, bf16[2,24,128]{2,1,0:T(8,128)(2,1)S(1)}, u32[]{:S(2)}, u32[]{:S(2)}) collective-permute-start(bf16[2,24,128]{2,1,0:T(8,128)(2,1)S(1)} %pad_maximum_fusion.3), channel_id=1, source_target_pairs={{0,4},{1,5},{2,6},{3,7},{4,0},{5,1},{6,2},{7,3},{8,12},{9,13},{10,... | collective-permute-start | bytes 36872 | tf_op jit(solution)/shard_map/ppermute | solution.py:145
  31.3 1.2 %collective-permute-done.6 = bf16[2,24,128]{2,1,0:T(8,128)(2,1)S(1)} collective-permute-done((bf16[2,24,128]{2,1,0:T(8,128)(2,1)S(1)}, bf16[2,24,128]{2,1,0:T(8,128)(2,1)S(1)}, u32[]{:S(2)}, u32[]{:S(2)}) %collective-permute-start.6) | collective-permute-done | bytes 12320 | tf_op jit(solution)/shard_map/ppermute | solution.py:145
  32.4 2.6 %collective-permute-done.7 = bf16[2,24,128]{2,1,0:T(8,128)(2,1)S(1)} collective-permute-done((bf16[2,24,128]{2,1,0:T(8,128)(2,1)S(1)}, bf16[2,24,128]{2,1,0:T(8,128)(2,1)S(1)}, u32[]{:S(2)}, u32[]{:S(2)}) %collective-permute-start.7) | collective-permute-done | bytes 12320 | tf_op jit(solution)/shard_map/ppermute | solution.py:145
  35.1 0.1 collective-permute-start.9
  35.2 0.8 %shard_map.234 = (f32[3,3,24]{2,1,0:T(4,128)}, f32[3,24]{1,0:T(4,128)}) custom-call(s32[3,384]{1,0:T(4,128)S(1)} %add_add_fusion.rows_ref.live_row_ref, bf16[24,384]{1,0:T(8,128)(2,1)S(1)} %get-tuple-element.29.single_ref, bf16[6,384]{1,0:T(8,128)(2,1)S(1)} %bitcast.19, f32[3,3,384]{2,1,0:T(4,128)S(1)} %copy-done.6, f32[3,384]{1,0:T(4,128)S(1)} %copy-done.8), custom_call_target="tpu_custom_call" | custom-call | flops 1000000 | bytes 100000 | tf_op jit(solution)/shard_map/pallas_call | solution.py:670
  36.0 0.4 collective-permute-done.9.rest_1_
  36.4 7.2 %shard_map.235 = bf16[24,384,128]{2,1,0:T(8,128)(2,1)} custom-call(s32[384]{0:T(512)S(1)} %copy-done.11, bf16[24,384,128]{2,1,0:T(8,128)(2,1)S(1)} %copy-done.1, bf16[2,12,128]{2,1,0:T(8,128)(2,1)S(1)} %reshape.18.left_ref, s32[3,384]{1,0:T(4,128)S(1)} %add_add_fusion.rows_ref.live_row_ref, f32[1,128]{1,0:T(1,128)S(1)} %bitcast.26, ...), custom_call_target="tpu_custom_call" | custom-call | flops 3019898880 | bytes 4718592 | tf_op jit(solution)/shard_map/pallas_call | solution.py:268
  (44 shorter events, 0.1 us)
Async XLA Ops:
  0.6 5.9 %collective-permute-start = (bf16[1,24,384]{2,1,0:T(8,128)(2,1)}, bf16[1,24,384]{2,1,0:T(8,128)(2,1)S(1)}, u32[]{:S(2)}, u32[]{:S(2)}) collective-permute-start(bf16[1,24,384]{2,1,0:T(8,128)(2,1)} %bitcast.17), channel_id=1, source_target_pairs={{0,2},{1,3},{2,0},{3,1},{4,6},{5,7},{6,4},{7,5},{8,10},{9,11},{10,... | collective-permute-start | bytes 55304 | tf_op jit(solution)/shard_map/ppermute | solution.py:145
  7.2 8.4 %collective-permute-start.1 = (bf16[2,24,384]{2,1,0:T(8,128)(2,1)S(1)}, bf16[2,24,384]{2,1,0:T(8,128)(2,1)S(1)}, u32[]{:S(2)}, u32[]{:S(2)}) collective-permute-start(bf16[2,24,384]{2,1,0:T(8,128)(2,1)S(1)} %pad_maximum_fusion.2), channel_id=1, source_target_pairs={{0,12},{1,13},{2,14},{3,15},{4,8},{5,9},{6,10},{7,11},{8,4},{9,5},... | collective-permute-start | bytes 110600 | tf_op jit(solution)/shard_map/ppermute | solution.py:145
  10.8 4.9 %collective-permute-start.2 = (bf16[2,24,384]{2,1,0:T(8,128)(2,1)S(1)}, bf16[2,24,384]{2,1,0:T(8,128)(2,1)S(1)}, u32[]{:S(2)}, u32[]{:S(2)}) collective-permute-start(bf16[2,24,384]{2,1,0:T(8,128)(2,1)S(1)} %pad_maximum_fusion.2), channel_id=1, source_target_pairs={{0,8},{1,9},{2,10},{3,11},{4,12},{5,13},{6,14},{7,15},{8,0},{9,1},... | collective-permute-start | bytes 110600 | tf_op jit(solution)/shard_map/ppermute | solution.py:145
  10.8 4.9 %collective-permute-start.3 = (bf16[2,24,384]{2,1,0:T(8,128)(2,1)S(1)}, bf16[2,24,384]{2,1,0:T(8,128)(2,1)S(1)}, u32[]{:S(2)}, u32[]{:S(2)}) collective-permute-start(bf16[2,24,384]{2,1,0:T(8,128)(2,1)S(1)} %pad_maximum_fusion.2), channel_id=1, source_target_pairs={{0,4},{1,5},{2,6},{3,7},{4,0},{5,1},{6,2},{7,3},{8,12},{9,13},{10,... | collective-permute-start | bytes 110600 | tf_op jit(solution)/shard_map/ppermute | solution.py:145
  11.6 1.7 %copy-start = (bf16[24,384,128]{2,1,0:T(8,128)(2,1)S(1)}, bf16[24,384,128]{2,1,0:T(8,128)(2,1)}, u32[]{:S(2)}) copy-start(bf16[24,384,128]{2,1,0:T(8,128)(2,1)} %pair_ref.5) | copy-start | bytes 7077892
  13.3 0.7 %copy-start.16 = (bf16[128,16]{0,1:T(8,128)(2,1)S(1)}, bf16[128,16]{0,1:T(8,128)(2,1)}, u32[]{:S(2)}) copy-start(bf16[128,16]{0,1:T(8,128)(2,1)} %param.29) | copy-start | bytes 12292
  14.0 1.1 %copy-start.19 = (bf16[16,64,384]{2,1,0:T(8,128)(2,1)S(1)}, bf16[16,64,384]{2,1,0:T(8,128)(2,1)}, u32[]{:S(2)}) copy-start(bf16[16,64,384]{2,1,0:T(8,128)(2,1)} %param.32) | copy-start | bytes 2359300
  14.0 1.8 %copy-start.7 = (bf16[24,384]{1,0:T(8,128)(2,1)S(1)}, bf16[24,384]{1,0:T(8,128)(2,1)}, u32[]{:S(2)}) copy-start(bf16[24,384]{1,0:T(8,128)(2,1)} %single_ref.3) | copy-start | bytes 55300
  14.0 3.9 %copy-start.4 = (bf16[384,128]{1,0:T(8,128)(2,1)S(1)}, bf16[384,128]{1,0:T(8,128)(2,1)}, u32[]{:S(2)}) copy-start(bf16[384,128]{1,0:T(8,128)(2,1)} %left_ref.1) | copy-start | bytes 294916
  14.0 3.9 %copy-start.5 = (bf16[384,128]{1,0:T(8,128)(2,1)S(1)}, bf16[384,128]{1,0:T(8,128)(2,1)}, u32[]{:S(2)}) copy-start(bf16[384,128]{1,0:T(8,128)(2,1)} %right_ref.1) | copy-start | bytes 294916
  15.1 1.4 %copy-start.2 = (bf16[384,16,132]{0,1,2:T(8,128)(2,1)S(1)}, bf16[384,16,132]{0,1,2:T(8,128)(2,1)}, u32[]{:S(2)}) copy-start(bf16[384,16,132]{0,1,2:T(8,128)(2,1)} %param.28) | copy-start | bytes 4866052
  15.1 1.4 %copy-start.6 = (f32[3,3,384]{2,1,0:T(4,128)S(1)}, f32[3,3,384]{2,1,0:T(4,128)}, u32[]{:S(2)}) copy-start(f32[3,3,384]{2,1,0:T(4,128)} %rot_ref.5) | copy-start | bytes 41476
  15.1 1.4 %copy-start.8 = (f32[3,384]{1,0:T(4,128)S(1)}, f32[3,384]{1,0:T(4,128)}, u32[]{:S(2)}) copy-start(f32[3,384]{1,0:T(4,128)} %trans_ref.5) | copy-start | bytes 13828
  15.1 1.4 %copy-start.10 = (s32[384]{0:T(512)S(1)}, s32[384]{0:T(512)}, u32[]{:S(2)}) copy-start(s32[384]{0:T(512)} %chain_ref.1) | copy-start | bytes 4612
  15.1 1.4 %copy-start.12 = (f32[16]{0:T(128)S(1)}, f32[16]{0:T(128)}, u32[]{:S(2)}) copy-start(f32[16]{0:T(128)} %param.30) | copy-start | bytes 196
  15.1 1.4 %copy-start.17 = (f32[16]{0:T(128)S(1)}, f32[16]{0:T(128)}, u32[]{:S(2)}) copy-start(f32[16]{0:T(128)} %param.31) | copy-start | bytes 196
  15.7 2.2 %copy-start.3 = (bf16[16,128,384]{2,1,0:T(8,128)(2,1)S(1)}, bf16[16,128,384]{2,1,0:T(8,128)(2,1)}, u32[]{:S(2)}) copy-start(bf16[16,128,384]{2,1,0:T(8,128)(2,1)} %param.33) | copy-start | bytes 4718596
  15.7 2.1 %collective-permute-start.4 = (bf16[8,24,384]{2,1,0:T(8,128)(2,1)S(1)}, bf16[8,24,384]{2,1,0:T(8,128)(2,1)S(1)}, u32[]{:S(2)}, u32[]{:S(2)}) collective-permute-start(bf16[8,24,384]{2,1,0:T(8,128)(2,1)S(1)} %pad_maximum_fusion.held_ref), channel_id=1, source_target_pairs={{0,1},{1,0},{2,3},{3,2},{4,5},{5,4},{6,7},{7,6},{8,9},{9,8},{10,11... | collective-permute-start | bytes 442376 | tf_op jit(solution)/shard_map/ppermute | solution.py:145
  16.5 1.8 %copy-start.1 = (bf16[24,384,128]{2,1,0:T(8,128)(2,1)S(1)}, bf16[24,384,128]{2,1,0:T(8,128)(2,1)}, u32[]{:S(2)}) copy-start(bf16[24,384,128]{2,1,0:T(8,128)(2,1)} %pair_ref.5) | copy-start | bytes 7077892
  18.3 16.9 %copy-start.9 = (bf16[384,6]{0,1:T(8,128)(2,1)S(1)}, bf16[384,6]{0,1:T(8,128)(2,1)}, u32[]{:S(2)}) copy-start(bf16[384,6]{0,1:T(8,128)(2,1)} %param.35) | copy-start | bytes 13828
  18.3 18.1 %copy-start.11 = (s32[384]{0:T(512)S(1)}, s32[384]{0:T(512)}, u32[]{:S(2)}) copy-start(s32[384]{0:T(512)} %live_ref.1) | copy-start | bytes 4612
  18.3 18.1 %copy-start.13 = (bf16[256,256]{1,0:T(8,128)(2,1)S(1)}, bf16[256,256]{1,0:T(8,128)(2,1)}, u32[]{:S(2)}) copy-start(bf16[256,256]{1,0:T(8,128)(2,1)} %middle_ref.1) | copy-start | bytes 393220
  18.3 18.1 %copy-start.14 = (bf16[128,256]{1,0:T(8,128)(2,1)S(1)}, bf16[128,256]{1,0:T(8,128)(2,1)}, u32[]{:S(2)}) copy-start(bf16[128,256]{1,0:T(8,128)(2,1)} %hidden_ref.1) | copy-start | bytes 196612
  18.3 18.1 %copy-start.15 = (bf16[256,128]{1,0:T(8,128)(2,1)S(1)}, bf16[256,128]{1,0:T(8,128)(2,1)}, u32[]{:S(2)}) copy-start(bf16[256,128]{1,0:T(8,128)(2,1)} %back_ref.1) | copy-start | bytes 196612
  18.4 18.1 %copy-start.18 = (f32[128]{0:T(128)S(1)}, f32[128]{0:T(128)}, u32[]{:S(2)}) copy-start(f32[128]{0:T(128)} %param.38) | copy-start | bytes 1540
  23.2 3.6 %collective-permute-start.5 = (bf16[1,24,128]{2,1,0:T(8,128)(2,1)S(1)}, bf16[1,24,128]{2,1,0:T(8,128)(2,1)S(1)}, u32[]{:S(2)}, u32[]{:S(2)}) collective-permute-start(bf16[1,24,128]{2,1,0:T(8,128)(2,1)S(1)} %bitcast.20), channel_id=1, source_target_pairs={{0,2},{1,3},{2,0},{3,1},{4,6},{5,7},{6,4},{7,5},{8,10},{9,11},{10,... | collective-permute-start | bytes 18440 | tf_op jit(solution)/shard_map/ppermute | solution.py:145
  26.9 5.6 %collective-permute-start.6 = (bf16[2,24,128]{2,1,0:T(8,128)(2,1)S(1)}, bf16[2,24,128]{2,1,0:T(8,128)(2,1)S(1)}, u32[]{:S(2)}, u32[]{:S(2)}) collective-permute-start(bf16[2,24,128]{2,1,0:T(8,128)(2,1)S(1)} %pad_maximum_fusion.3), channel_id=1, source_target_pairs={{0,12},{1,13},{2,14},{3,15},{4,8},{5,9},{6,10},{7,11},{8,4},{9,5},... | collective-permute-start | bytes 36872 | tf_op jit(solution)/shard_map/ppermute | solution.py:145
  30.5 4.6 %collective-permute-start.7 = (bf16[2,24,128]{2,1,0:T(8,128)(2,1)S(1)}, bf16[2,24,128]{2,1,0:T(8,128)(2,1)S(1)}, u32[]{:S(2)}, u32[]{:S(2)}) collective-permute-start(bf16[2,24,128]{2,1,0:T(8,128)(2,1)S(1)} %pad_maximum_fusion.3), channel_id=1, source_target_pairs={{0,8},{1,9},{2,10},{3,11},{4,12},{5,13},{6,14},{7,15},{8,0},{9,1},... | collective-permute-start | bytes 36872 | tf_op jit(solution)/shard_map/ppermute | solution.py:145
  30.5 4.6 %collective-permute-start.8 = (bf16[2,24,128]{2,1,0:T(8,128)(2,1)S(1)}, bf16[2,24,128]{2,1,0:T(8,128)(2,1)S(1)}, u32[]{:S(2)}, u32[]{:S(2)}) collective-permute-start(bf16[2,24,128]{2,1,0:T(8,128)(2,1)S(1)} %pad_maximum_fusion.3), channel_id=1, source_target_pairs={{0,4},{1,5},{2,6},{3,7},{4,0},{5,1},{6,2},{7,3},{8,12},{9,13},{10,... | collective-permute-start | bytes 36872 | tf_op jit(solution)/shard_map/ppermute | solution.py:145
  35.1 1.3 %collective-permute-start.9 = (bf16[8,24,128]{2,1,0:T(8,128)(2,1)S(1)}, bf16[8,24,128]{2,1,0:T(8,128)(2,1)S(1)}, u32[]{:S(2)}, u32[]{:S(2)}) collective-permute-start(bf16[8,24,128]{2,1,0:T(8,128)(2,1)S(1)} %pad_maximum_fusion.1.rest_0_), channel_id=1, source_target_pairs={{0,1},{1,0},{2,3},{3,2},{4,5},{5,4},{6,7},{7,6},{8,9},{9,8},{10,11... | collective-permute-start | bytes 147464 | tf_op jit(solution)/shard_map/ppermute | solution.py:145

commit v5 on v4

--- a/solution.py
+++ b/solution.py
@@ -203,6 +203,7 @@
     cols, feats = pair_ref.shape[1:]
     me = lax.axis_index("res")
     col_start = lax.axis_index("head") * cols
+    total = right_ref.shape[0]
 
     @pl.when(step == 0)
     def _():
@@ -214,7 +215,7 @@
                 owner = me ^ offsets[at] if offsets is not None else at
                 at += 1
                 right_ref[pl.ds(pl.multiple_of(owner * rows_dev, 8), rows_dev), :] = value
-        live_row = live_row_ref[pl.ds(live_at, 1), :].astype(jnp.float32)
+        live_row = live_row_ref[pl.ds(live_at, 1), pl.ds(0, total)].astype(jnp.float32)
         wide = jnp.broadcast_to(live_row, (feats, live_row.shape[1]))
         live_cols_ref[...] = jnp.where(jnp.transpose(wide) > 0, 1.0, 0.0)
         across = lax.broadcasted_iota(jnp.int32, (feats, feats), 0)
@@ -340,10 +341,13 @@
     ]
 
 
-def bias_kernel(weight_ref, pair_ref, out_ref):
-    for r in range(pair_ref.shape[0]):
+def bias_kernel(weight_ref, pair_ref, out_ref, copy_ref):
+    count = pair_ref.shape[0]
+    first = pl.program_id(0) * count
+    for r in range(count):
         bias = dot_rows(weight_ref[...], pair_ref[r])
-        out_ref[r] = bias.astype(jnp.bfloat16).astype(jnp.float32)
+        out_ref[first + r] = bias.astype(jnp.bfloat16).astype(jnp.float32)
+    copy_ref[pl.ds(first, count)] = pair_ref[...]
 
 
 def query_kernel(
@@ -401,8 +405,9 @@
             at = lanes + (3 * term + c) * width
             query_ref[:, pl.ds(at, width)] = part.reshape(rows * heads, width)
     square = jnp.sum(square, axis=-1, keepdims=True)
+    own_row = rows_ref[pl.ds(0, 1), pl.ds(0, total)]
     for r in range(rows):
-        within = jnp.where(rows_ref[pl.ds(0, 1), :] == chain_ref[me * rows + r], 1.0, 0.0)
+        within = jnp.where(own_row == chain_ref[me * rows + r], 1.0, 0.0)
         base_ref[r] = LOGIT_FACTOR * (bias_ref[r] + chain_offset * within - weight * square[r])
 
 
@@ -443,19 +448,26 @@
     rot = [[rot_ref[c, pl.ds(d, 1), :] for d in range(3)] for c in range(3)]
     shift = [trans_ref[pl.ds(c, 1), :] for c in range(3)]
 
-    key_at, value_at = HEAD_FEATURES, 2 * HEAD_FEATURES
-    key_rows = weight_ref[pl.ds(key_at, HEAD_FEATURES)].reshape(HEAD_FEATURES * heads, -1)
-    keys = dot_rows(key_rows, every).astype(jnp.bfloat16)
+    scalars, key_points = HEAD_FEATURES * heads, PQ * heads
     offset = 3 * HEAD_FEATURES + 3 * PQ
-    points = [dot_rows(point_rows(weight_ref, offset, PQ, c), every) for c in range(3)]
-    points = [p.astype(jnp.bfloat16) for p in turn(points, rot, shift)]
+    weight_rows = [weight_ref[pl.ds(HEAD_FEATURES, 2 * HEAD_FEATURES)].reshape(2 * scalars, -1)]
+    weight_rows += [point_rows(weight_ref, offset, PQ, c) for c in range(3)]
+    offset = offset + 3 * PQ
+    weight_rows += [point_rows(weight_ref, offset, PV, c) for c in range(3)]
+    projected = dot_rows(jnp.concatenate(weight_rows, 0), every)
+    parts, at = [], 0
+    for size in [scalars] * 2 + [key_points] * 3 + [PV * heads] * 3:
+        parts.append(projected[at : at + size])
+        at += size
+    keys = parts[0].astype(jnp.bfloat16)
+    points = [p.astype(jnp.bfloat16) for p in turn(parts[2:5], rot, shift)]
     square = sum(jnp.square(p.astype(jnp.float32)) for p in points)
     square = jnp.sum(square.reshape(PQ, heads, total), axis=0)
     keys = jnp.concatenate([keys] + 3 * points, 0)
     weight = 0.5 * LOGIT_FACTOR * math.sqrt(2.0 / (9.0 * PQ)) * as_column(distance_ref[...])
     logits = dot(query_ref[...], keys).reshape(rows, heads, total)
     logits = LOGIT_FACTOR * logits + base_ref[...] - (weight * square)[None]
-    present = rows_ref[pl.ds(1, 1), :] > 0
+    present = rows_ref[pl.ds(1, 1), pl.ds(0, total)] > 0
     logits = jnp.where(present[None], logits, -1000000000.0)
     logits = logits.reshape(rows * heads, total)
     exponent = jnp.exp(logits - jnp.max(logits, axis=-1, keepdims=True))
@@ -471,11 +483,8 @@
         mixed = dot_rows(attention, values).reshape(rows, heads, lanes)
         return jnp.sum(jnp.where(head_mask(heads, lanes)[None], mixed, 0.0), axis=1)
 
-    value_rows = weight_ref[pl.ds(value_at, HEAD_FEATURES)].reshape(HEAD_FEATURES * heads, -1)
-    scalar_out = own_head(dot_rows(value_rows, every).astype(jnp.bfloat16))
-    offset = 3 * HEAD_FEATURES + 6 * PQ
-    points = [dot_rows(point_rows(weight_ref, offset, PV, c), every) for c in range(3)]
-    points = [own_head(p.astype(jnp.bfloat16)) for p in turn(points, rot, shift)]
+    scalar_out = own_head(parts[1].astype(jnp.bfloat16))
+    points = [own_head(p.astype(jnp.bfloat16)) for p in turn(parts[5:8], rot, shift)]
     frame = frame_ref[...]
     centred = [points[c] - frame[:, 9 + c : 10 + c] for c in range(3)]
     local = [
@@ -497,7 +506,7 @@
     )
     update = update + product(pair_sum, pair_weight_ref[...])
     values = single_ref[...].astype(jnp.float32) + update[:rows] + update[rows:]
-    single_out = layer_norm(values, gain_ref[...]).astype(jnp.bfloat16)
+    single_out = layer_norm(values, gain_ref[...][None]).astype(jnp.bfloat16)
     out_ref[...] = single_out
     copy_ref[...] = single_out
     left_out_ref[...] = dot(single_out, left_ref[...]).astype(jnp.bfloat16)
@@ -522,7 +531,7 @@
         for d in range(3):
             table_ref[pl.ds(3 * c + d, 1), :] = rot_ref[c, pl.ds(d, 1), :]
         table_ref[pl.ds(9 + c, 1), :] = trans_ref[pl.ds(c, 1), :]
-    table_ref[pl.ds(12, 1), :] = jnp.where(rows_ref[pl.ds(1, 1), :] > 0, 1.0, 0.0)
+    table_ref[pl.ds(12, 1), :] = jnp.where(rows_ref[pl.ds(1, 1), pl.ds(0, total)] > 0, 1.0, 0.0)
     row = lax.broadcasted_iota(jnp.int32, (rows, total), 0)
     column = lax.broadcasted_iota(jnp.int32, (rows, total), 1)
     chosen = jnp.where(column == row + me * rows, 1.0, 0.0)
@@ -564,6 +573,20 @@
         )
 
 
+def stacked_rows(*rows):
+    longest = max(row.shape[0] for row in rows)
+    wide = [
+        row if row.shape[0] in (1, longest) else jnp.pad(row, (0, longest - row.shape[0]))
+        for row in rows
+    ]
+    wide = [jnp.broadcast_to(row, (longest,)) for row in wide]
+    at = lax.broadcasted_iota(jnp.int32, (len(rows), longest), 0)
+    table = jnp.broadcast_to(wide[0][None], (len(rows), longest))
+    for k in range(1, len(rows)):
+        table = jnp.where(at == k, wide[k][None], table)
+    return table
+
+
 def in_vmem(count):
     return [pl.BlockSpec(memory_space=pltpu.VMEM)] * count
 
@@ -590,23 +613,29 @@
     rows, total, feats = pair.shape
     heads = single_projection_weight.shape[1]
     width = single.shape[1]
-    step_row = jnp.broadcast_to(timestep, (total,))
-    table = jnp.stack([residue_chain_index, residue_move_mask, step_row])
-    gain = single_norm_gain[None]
-    offsets, held, (table, gain) = gather_most(single, total // rows, (table, gain))
+    table = stacked_rows(residue_chain_index, residue_move_mask, timestep)
+    offsets, held, table = gather_most(single, total // rows, table)
     weight = jnp.transpose(single_projection_weight, (2, 1, 0))
     local_weight = jnp.transpose(local_output_weight, (1, 0, 2))
     distance = head_distance_weight[None]
     depth = heads * (HEAD_FEATURES + 9 * PQ)
-    bias = pl.pallas_call(
+    part = math.gcd(rows, 8)
+    bias, pair = pl.pallas_call(
         bias_kernel,
-        in_specs=in_vmem(2),
-        out_specs=pl.BlockSpec(memory_space=pltpu.VMEM),
-        out_shape=jax.ShapeDtypeStruct((rows, heads, total), jnp.float32),
-        compiler_params=pltpu.CompilerParams(vmem_limit_bytes=16 * 1024 * 1024),
+        grid=(rows // part,),
+        in_specs=[
+            pl.BlockSpec((heads, feats), lambda i: (0, 0)),
+            pl.BlockSpec((part, total, feats), lambda i: (i, 0, 0)),
+        ],
+        out_specs=tuple(in_vmem(2)),
+        out_shape=(
+            jax.ShapeDtypeStruct((rows, heads, total), jnp.float32),
+            jax.ShapeDtypeStruct(pair.shape, pair.dtype),
+        ),
+        compiler_params=pltpu.CompilerParams(vmem_limit_bytes=51200 * 1024),
         cost_estimate=pl.CostEstimate(flops=10**9, bytes_accessed=6 * 10**6, transcendentals=0),
     )(jnp.transpose(head_bias_weight), pair)
-    held, bias, local_weight = lax.optimization_barrier((held, bias, local_weight))
+    held, bias, pair, local_weight = lax.optimization_barrier((held, bias, pair, local_weight))
     other = exchange(held, total // rows, 1)
     query, base, frame = pl.pallas_call(
         query_kernel,
@@ -662,7 +691,7 @@
         single,
         local_weight,
         pair_output_weight.reshape(heads * feats, width),
-        gain,
+        single_norm_gain,
         left_pair_weight,
         right_pair_weight,
     )
@@ -685,7 +714,7 @@
         rotations,
         translations,
     )
-    return single_out, rot_out, trans_out, left_proj, right_proj, table, 1
+    return single_out, rot_out, trans_out, left_proj, right_proj, table, 1, pair
 
 
 def attend_split(
@@ -788,7 +817,7 @@
         jnp.bfloat16
     )
     live_rows = residue_move_mask[None]
-    return single_out, rot_out, trans_out, left_proj, right_proj, live_rows, 0
+    return single_out, rot_out, trans_out, left_proj, right_proj, live_rows, 0, pair
 
 
 def shards(
@@ -817,7 +846,7 @@
     rows_dev = single.shape[0]
     count = rotations.shape[2] // rows_dev
     whole_heads = lax.axis_size("head") == 1 and count >= 16 and count & (count - 1) == 0
-    single_out, rot_out, trans_out, left_proj, right_proj, live_rows, live_at = (
+    single_out, rot_out, trans_out, left_proj, right_proj, live_rows, live_at, pair = (
         attend if whole_heads else attend_split
     )(
         single,

time: 44 us -> 42.6 us (0.968)
  local copies, waits for them, and re-layouts: 6.39 us -> 1.26 us
  Pallas kernels: 15.1 us -> 17.1 us
  starting transfers between devices: 13 us -> 13.9 us
  other arithmetic: 0.85 us -> 1.55 us
    unnamed x41 -> x39, local copies, waits for them, and re-layouts: 4.26 us -> 1.25 us
    pallas_call x1, Pallas kernels: 0.91 us -> 3.29 us  [attend(): pl.pallas_call(bias_kernel, grid=(rows // part,), in_specs=[pl.BlockSpec(...]
    another operation x3 -> x0, local copies, waits for them, and re-layouts: 1.44 us -> none  [attend(): table = jnp.stack([residue_chain_index, residue_move_mask, step_row])]
    ppermute x10, starting transfers between devices: 13 us -> 13.9 us  [exchange(): return lax.ppermute(block, 'res', [(k, k ^ step) for k in range(count)])]
    select_n x0 -> x1, other arithmetic: none -> 0.77 us  [stacked_rows(): table = jnp.where(at == k, wide[k][None], table)]
    broadcast_in_dim x1 -> x0, local copies, waits for them, and re-layouts: 0.68 us -> none  [attend(): gain = single_norm_gain[None]]
  transfers between devices with their start and end apart: 10 -> 10, of which waited for: 5 -> 5; matrix products, arithmetic and copies ran while one was open for 6% -> 3% of each run, Pallas kernels for 7% -> 13%
where the time goes in v5:
time: 42.6 us; the launch traced here: 42.3 us
  Pallas kernels  17.1 us (40%)
  starting transfers between devices  13.9 us (33%)
  waiting for transfers between devices  6.85 us (16%)
  between operations  1.62 us (4%)
  other arithmetic  1.55 us (4%)
  local copies, waits for them, and re-layouts  1.26 us (3%)
    ppermute x10, starting transfers between devices, exchange(): return lax.ppermute(block, 'res', [(k, k ^ step) for k in range(count)])  13.9 us
    pallas_call x1, Pallas kernels, pair_transition(): pl.pallas_call(kernel, grid=(rows_dev // rows_block,), in_specs=[pl.Block...  7.19 us
    ppermute x10, waiting for transfers between devices, exchange(): return lax.ppermute(block, 'res', [(k, k ^ step) for k in range(count)])  6.85 us
    pallas_call x1, Pallas kernels, attend(): pl.pallas_call(functools.partial(attention_kernel, offsets), in_specs=in_...  4.54 us
    pallas_call x1, Pallas kernels, attend(): pl.pallas_call(bias_kernel, grid=(rows // part,), in_specs=[pl.BlockSpec(...  3.29 us
    pallas_call x1, Pallas kernels, attend(): pl.pallas_call(query_kernel, in_specs=[pl.BlockSpec(memory_space=pltpu.SM...  1.28 us
    unnamed x39, local copies, waits for them, and re-layouts  1.25 us
  transfers between devices with their start and end apart: 10, of which 5 were waited for; matrix products, arithmetic and copies ran while one was open for 3% of the time, Pallas kernels for 13%

profile of v5, /device:TPU:0, one launch (start us, length us, event | category | flops | bytes accessed | tf_op | source)
XLA Modules:
  0.0 42.3 jit_solution(4083192404144183842)
XLA Ops:
  0.6 3.0 %collective-permute-start = (bf16[1,24,384]{2,1,0:T(8,128)(2,1)}, bf16[1,24,384]{2,1,0:T(8,128)(2,1)S(1)}, u32[]{:S(2)}, u32[]{:S(2)}) collective-permute-start(bf16[1,24,384]{2,1,0:T(8,128)(2,1)} %bitcast.18), channel_id=1, source_target_pairs={{0,2},{1,3},{2,0},{3,1},{4,6},{5,7},{6,4},{7,5},{8,10},{9,11},{10,... | collective-permute-start | bytes 55304 | tf_op jit(solution)/shard_map/ppermute | solution.py:145
  4.3 0.8 %select_select_fusion.rows_ref.live_row_ref = s32[3,384]{1,0:T(4,128)S(1)} fusion(s32[384]{0:T(512)} %chain_ref.1, s32[384]{0:T(512)} %live_ref.1, s32[]{:T(128)} %bitcast.13, pred[3]{0:T(512)(128)(4,1)S(1)} %get-tuple-element.38, pred[3]{0:T(512)(128)(4,1)S(1)} %get-tuple-element.39), kind=kLoop, calls=%fused_computation.5 | loop fusion | flops 2304 | bytes 7690 | tf_op jit(solution)/shard_map/jit(_where)/select_n | solution.py:586
  5.1 0.5 %collective-permute-done = bf16[1,24,384]{2,1,0:T(8,128)(2,1)S(1)} collective-permute-done((bf16[1,24,384]{2,1,0:T(8,128)(2,1)}, bf16[1,24,384]{2,1,0:T(8,128)(2,1)S(1)}, u32[]{:S(2)}, u32[]{:S(2)}) %collective-permute-start) | collective-permute-done | bytes 18464 | tf_op jit(solution)/shard_map/ppermute | solution.py:145
  5.6 0.7 %pad_maximum_fusion.2 = bf16[2,24,384]{2,1,0:T(8,128)(2,1)S(1)} fusion(bf16[1,24,384]{2,1,0:T(8,128)(2,1)S(1)} %collective-permute-done, bf16[1,24,384]{2,1,0:T(8,128)(2,1)} %bitcast.19), kind=kLoop, calls=%fused_computation.3 | loop fusion | flops 18432 | bytes 73728 | tf_op jit(solution)/shard_map/concatenate | solution.py:153
  6.3 4.1 %collective-permute-start.1 = (bf16[2,24,384]{2,1,0:T(8,128)(2,1)S(1)}, bf16[2,24,384]{2,1,0:T(8,128)(2,1)S(1)}, u32[]{:S(2)}, u32[]{:S(2)}) collective-permute-start(bf16[2,24,384]{2,1,0:T(8,128)(2,1)S(1)} %pad_maximum_fusion.2), channel_id=1, source_target_pairs={{0,12},{1,13},{2,14},{3,15},{4,8},{5,9},{6,10},{7,11},{8,4},{9,5},... | collective-permute-start | bytes 110600 | tf_op jit(solution)/shard_map/ppermute | solution.py:145
  10.4 0.6 %collective-permute-start.3 = (bf16[2,24,384]{2,1,0:T(8,128)(2,1)S(1)}, bf16[2,24,384]{2,1,0:T(8,128)(2,1)S(1)}, u32[]{:S(2)}, u32[]{:S(2)}) collective-permute-start(bf16[2,24,384]{2,1,0:T(8,128)(2,1)S(1)} %pad_maximum_fusion.2), channel_id=1, source_target_pairs={{0,4},{1,5},{2,6},{3,7},{4,0},{5,1},{6,2},{7,3},{8,12},{9,13},{10,... | collective-permute-start | bytes 110600 | tf_op jit(solution)/shard_map/ppermute | solution.py:145
  11.1 0.7 %copy-done.15 = bf16[128,16]{0,1:T(8,128)(2,1)S(1)} copy-done((bf16[128,16]{0,1:T(8,128)(2,1)S(1)}, bf16[128,16]{0,1:T(8,128)(2,1)}, u32[]{:S(2)}) %copy-start.15) | copy-done | bytes 4120
  11.8 0.0 copy-start.6
  11.8 0.0 copy-start.8
  11.8 0.0 copy-start.11
  11.8 0.0 copy-start.16
  11.8 3.3 %shard_map.231 = (f32[24,16,384]{2,1,0:T(8,128)S(1)}, bf16[24,384,128]{2,1,0:T(8,128)(2,1)S(1)}) custom-call(bf16[16,128]{1,0:T(8,128)(2,1)S(1)} %bitcast.25, bf16[24,384,128]{2,1,0:T(8,128)(2,1)} %pair_ref.1), custom_call_target="tpu_custom_call" | custom-call | flops 1000000000 | bytes 6000000 | tf_op jit(solution)/shard_map/pallas_call | solution.py:623
  15.1 0.5 %copy.28 = bf16[16,64,384]{2,0,1:T(8,128)(2,1)S(1)} copy(bf16[16,64,384]{2,1,0:T(8,128)(2,1)S(1)} %copy-done.18) | data formatting | bytes 1572864 | tf_op args[11]
  15.6 0.0 copy-start.1
  15.6 0.0 copy-start.10
  15.7 0.1 collective-permute-start.4
  15.9 1.3 %shard_map.232 = (bf16[384,1408]{1,0:T(8,128)(2,1)S(1)}, f32[24,16,384]{2,1,0:T(8,128)S(1)}, f32[24,16]{1,0:T(8,128)S(1)}) custom-call(s32[384]{0:T(512)S(1)} %copy-done.8, f32[24,16,384]{2,1,0:T(8,128)S(1)} %get-tuple-element.25.bias_ref, bf16[24,384]{1,0:T(8,128)(2,1)S(1)} %copy-done.5, bf16[132,16,384]{2,1,0:T(8,128)(2,1)S(1)} %bitcast.15, ...), custom_call_target="tpu_custom_call" | custom-call | flops 1000000000 | bytes 6000000 | tf_op jit(solution)/shard_map/pallas_call | solution.py:640
  17.2 0.0 collective-permute-done.4.other_ref
  17.2 0.0 copy-start.12
  17.2 0.0 copy-start.13
  17.3 0.0 copy-start.17
  17.3 4.5 %shard_map.233 = (bf16[24,384]{1,0:T(8,128)(2,1)}, bf16[24,384]{1,0:T(8,128)(2,1)S(1)}, bf16[24,128]{1,0:T(8,128)(2,1)S(1)}, bf16[24,128]{1,0:T(8,128)(2,1)S(1)}) custom-call(bf16[8,24,384]{2,1,0:T(8,128)(2,1)S(1)} %pad_maximum_fusion.held_ref, bf16[8,24,384]{2,1,0:T(8,128)(2,1)S(1)} %collective-permute-done.4.other_ref, bf16[132,16,384]{2,1,0:T(8,128)(2,1)S(1)} %bitcast.16, ...), custom_call_target="tpu_custom_call" | custom-call | flops 2000000000 | bytes 10000000 | tf_op jit(solution)/shard_map/pallas_call | solution.py:663
  21.8 1.6 %collective-permute-start.5 = (bf16[1,24,128]{2,1,0:T(8,128)(2,1)S(1)}, bf16[1,24,128]{2,1,0:T(8,128)(2,1)S(1)}, u32[]{:S(2)}, u32[]{:S(2)}) collective-permute-start(bf16[1,24,128]{2,1,0:T(8,128)(2,1)S(1)} %bitcast.21), channel_id=1, source_target_pairs={{0,2},{1,3},{2,0},{3,1},{4,6},{5,7},{6,4},{7,5},{8,10},{9,11},{10,... | collective-permute-start | bytes 18440 | tf_op jit(solution)/shard_map/ppermute | solution.py:145
  23.5 2.0 %collective-permute-done.5 = bf16[1,24,128]{2,1,0:T(8,128)(2,1)S(1)} collective-permute-done((bf16[1,24,128]{2,1,0:T(8,128)(2,1)S(1)}, bf16[1,24,128]{2,1,0:T(8,128)(2,1)S(1)}, u32[]{:S(2)}, u32[]{:S(2)}) %collective-permute-start.5) | collective-permute-done | bytes 6176 | tf_op jit(solution)/shard_map/ppermute | solution.py:145
  25.5 3.7 %collective-permute-start.6 = (bf16[2,24,128]{2,1,0:T(8,128)(2,1)S(1)}, bf16[2,24,128]{2,1,0:T(8,128)(2,1)S(1)}, u32[]{:S(2)}, u32[]{:S(2)}) collective-permute-start(bf16[2,24,128]{2,1,0:T(8,128)(2,1)S(1)} %pad_maximum_fusion.3), channel_id=1, source_target_pairs={{0,12},{1,13},{2,14},{3,15},{4,8},{5,9},{6,10},{7,11},{8,4},{9,5},... | collective-permute-start | bytes 36872 | tf_op jit(solution)/shard_map/ppermute | solution.py:145
  29.2 0.6 %collective-permute-start.8 = (bf16[2,24,128]{2,1,0:T(8,128)(2,1)S(1)}, bf16[2,24,128]{2,1,0:T(8,128)(2,1)S(1)}, u32[]{:S(2)}, u32[]{:S(2)}) collective-permute-start(bf16[2,24,128]{2,1,0:T(8,128)(2,1)S(1)} %pad_maximum_fusion.3), channel_id=1, source_target_pairs={{0,4},{1,5},{2,6},{3,7},{4,0},{5,1},{6,2},{7,3},{8,12},{9,13},{10,... | collective-permute-start | bytes 36872 | tf_op jit(solution)/shard_map/ppermute | solution.py:145
  29.8 1.1 %collective-permute-done.6 = bf16[2,24,128]{2,1,0:T(8,128)(2,1)S(1)} collective-permute-done((bf16[2,24,128]{2,1,0:T(8,128)(2,1)S(1)}, bf16[2,24,128]{2,1,0:T(8,128)(2,1)S(1)}, u32[]{:S(2)}, u32[]{:S(2)}) %collective-permute-start.6) | collective-permute-done | bytes 12320 | tf_op jit(solution)/shard_map/ppermute | solution.py:145
  31.0 2.8 %collective-permute-done.7 = bf16[2,24,128]{2,1,0:T(8,128)(2,1)S(1)} collective-permute-done((bf16[2,24,128]{2,1,0:T(8,128)(2,1)S(1)}, bf16[2,24,128]{2,1,0:T(8,128)(2,1)S(1)}, u32[]{:S(2)}, u32[]{:S(2)}) %collective-permute-start.7) | collective-permute-done | bytes 12320 | tf_op jit(solution)/shard_map/ppermute | solution.py:145
  33.8 0.1 collective-permute-start.9
  33.9 0.8 %shard_map.234 = (f32[3,3,24]{2,1,0:T(4,128)}, f32[3,24]{1,0:T(4,128)}) custom-call(s32[3,384]{1,0:T(4,128)S(1)} %select_select_fusion.rows_ref.live_row_ref, bf16[24,384]{1,0:T(8,128)(2,1)S(1)} %get-tuple-element.33.single_ref, bf16[6,384]{1,0:T(8,128)(2,1)S(1)} %bitcast.20, f32[3,3,384]{2,1,0:T(4,128)S(1)} %copy-done.4, f32[3,384]{1,0:T(4,128)S(1)} %copy-done.6), custom_call_target="tpu_custom_call" | custom-call | flops 1000000 | bytes 100000 | tf_op jit(solution)/shard_map/pallas_call | solution.py:699
  34.7 0.4 collective-permute-done.9.rest_1_
  35.1 7.2 %shard_map.235 = bf16[24,384,128]{2,1,0:T(8,128)(2,1)} custom-call(s32[384]{0:T(512)S(1)} %copy-done.9, bf16[24,384,128]{2,1,0:T(8,128)(2,1)S(1)} %get-tuple-element.30.pair_ref, bf16[2,12,128]{2,1,0:T(8,128)(2,1)S(1)} %reshape.20.left_ref, s32[3,384]{1,0:T(4,128)S(1)} %select_select_fusion.rows_ref.live_row_ref, f32[1,128]{1,0:T(1,128)S(1)} %bitcast.27, ...), custom_call_target="tpu_custom_call" | custom-call | flops 3019898880 | bytes 4718592 | tf_op jit(solution)/shard_map/pallas_call | solution.py:269
  (39 shorter events, 0.1 us)
Async XLA Ops:
  0.6 5.0 %collective-permute-start = (bf16[1,24,384]{2,1,0:T(8,128)(2,1)}, bf16[1,24,384]{2,1,0:T(8,128)(2,1)S(1)}, u32[]{:S(2)}, u32[]{:S(2)}) collective-permute-start(bf16[1,24,384]{2,1,0:T(8,128)(2,1)} %bitcast.18), channel_id=1, source_target_pairs={{0,2},{1,3},{2,0},{3,1},{4,6},{5,7},{6,4},{7,5},{8,10},{9,11},{10,... | collective-permute-start | bytes 55304 | tf_op jit(solution)/shard_map/ppermute | solution.py:145
  6.3 9.3 %collective-permute-start.1 = (bf16[2,24,384]{2,1,0:T(8,128)(2,1)S(1)}, bf16[2,24,384]{2,1,0:T(8,128)(2,1)S(1)}, u32[]{:S(2)}, u32[]{:S(2)}) collective-permute-start(bf16[2,24,384]{2,1,0:T(8,128)(2,1)S(1)} %pad_maximum_fusion.2), channel_id=1, source_target_pairs={{0,12},{1,13},{2,14},{3,15},{4,8},{5,9},{6,10},{7,11},{8,4},{9,5},... | collective-permute-start | bytes 110600 | tf_op jit(solution)/shard_map/ppermute | solution.py:145
  10.4 5.2 %collective-permute-start.2 = (bf16[2,24,384]{2,1,0:T(8,128)(2,1)S(1)}, bf16[2,24,384]{2,1,0:T(8,128)(2,1)S(1)}, u32[]{:S(2)}, u32[]{:S(2)}) collective-permute-start(bf16[2,24,384]{2,1,0:T(8,128)(2,1)S(1)} %pad_maximum_fusion.2), channel_id=1, source_target_pairs={{0,8},{1,9},{2,10},{3,11},{4,12},{5,13},{6,14},{7,15},{8,0},{9,1},... | collective-permute-start | bytes 110600 | tf_op jit(solution)/shard_map/ppermute | solution.py:145
  10.4 5.2 %collective-permute-start.3 = (bf16[2,24,384]{2,1,0:T(8,128)(2,1)S(1)}, bf16[2,24,384]{2,1,0:T(8,128)(2,1)S(1)}, u32[]{:S(2)}, u32[]{:S(2)}) collective-permute-start(bf16[2,24,384]{2,1,0:T(8,128)(2,1)S(1)} %pad_maximum_fusion.2), channel_id=1, source_target_pairs={{0,4},{1,5},{2,6},{3,7},{4,0},{5,1},{6,2},{7,3},{8,12},{9,13},{10,... | collective-permute-start | bytes 110600 | tf_op jit(solution)/shard_map/ppermute | solution.py:145
  11.1 0.7 %copy-start.15 = (bf16[128,16]{0,1:T(8,128)(2,1)S(1)}, bf16[128,16]{0,1:T(8,128)(2,1)}, u32[]{:S(2)}) copy-start(bf16[128,16]{0,1:T(8,128)(2,1)} %param.29) | copy-start | bytes 12292
  11.8 3.4 %copy-start.18 = (bf16[16,64,384]{2,1,0:T(8,128)(2,1)S(1)}, bf16[16,64,384]{2,1,0:T(8,128)(2,1)}, u32[]{:S(2)}) copy-start(bf16[16,64,384]{2,1,0:T(8,128)(2,1)} %param.32) | copy-start | bytes 2359300
  11.8 4.0 %copy-start = (bf16[384,16,132]{0,1,2:T(8,128)(2,1)S(1)}, bf16[384,16,132]{0,1,2:T(8,128)(2,1)}, u32[]{:S(2)}) copy-start(bf16[384,16,132]{0,1,2:T(8,128)(2,1)} %param.28) | copy-start | bytes 4866052
  11.8 4.0 %copy-start.4 = (f32[3,3,384]{2,1,0:T(4,128)S(1)}, f32[3,3,384]{2,1,0:T(4,128)}, u32[]{:S(2)}) copy-start(f32[3,3,384]{2,1,0:T(4,128)} %rot_ref.5) | copy-start | bytes 41476
  11.8 4.0 %copy-start.5 = (bf16[24,384]{1,0:T(8,128)(2,1)S(1)}, bf16[24,384]{1,0:T(8,128)(2,1)}, u32[]{:S(2)}) copy-start(bf16[24,384]{1,0:T(8,128)(2,1)} %single_ref.3) | copy-start | bytes 55300
  11.8 4.1 %copy-start.6 = (f32[3,384]{1,0:T(4,128)S(1)}, f32[3,384]{1,0:T(4,128)}, u32[]{:S(2)}) copy-start(f32[3,384]{1,0:T(4,128)} %trans_ref.5) | copy-start | bytes 13828
  11.8 4.0 %copy-start.8 = (s32[384]{0:T(512)S(1)}, s32[384]{0:T(512)}, u32[]{:S(2)}) copy-start(s32[384]{0:T(512)} %chain_ref.1) | copy-start | bytes 4612
  11.8 4.0 %copy-start.11 = (f32[16]{0:T(128)S(1)}, f32[16]{0:T(128)}, u32[]{:S(2)}) copy-start(f32[16]{0:T(128)} %param.30) | copy-start | bytes 196
  11.8 4.0 %copy-start.16 = (f32[16]{0:T(128)S(1)}, f32[16]{0:T(128)}, u32[]{:S(2)}) copy-start(f32[16]{0:T(128)} %param.31) | copy-start | bytes 196
  15.6 1.6 %copy-start.1 = (bf16[16,128,384]{2,1,0:T(8,128)(2,1)S(1)}, bf16[16,128,384]{2,1,0:T(8,128)(2,1)}, u32[]{:S(2)}) copy-start(bf16[16,128,384]{2,1,0:T(8,128)(2,1)} %param.33) | copy-start | bytes 4718596
  15.6 1.6 %copy-start.2 = (bf16[384,128]{1,0:T(8,128)(2,1)S(1)}, bf16[384,128]{1,0:T(8,128)(2,1)}, u32[]{:S(2)}) copy-start(bf16[384,128]{1,0:T(8,128)(2,1)} %left_ref.1) | copy-start | bytes 294916
  15.6 1.6 %copy-start.3 = (bf16[384,128]{1,0:T(8,128)(2,1)S(1)}, bf16[384,128]{1,0:T(8,128)(2,1)}, u32[]{:S(2)}) copy-start(bf16[384,128]{1,0:T(8,128)(2,1)} %right_ref.1) | copy-start | bytes 294916
  15.6 1.6 %copy-start.10 = (f32[384]{0:T(512)S(1)}, f32[384]{0:T(512)}, u32[]{:S(2)}) copy-start(f32[384]{0:T(512)} %gain_ref.1) | copy-start | bytes 4612
  15.7 1.4 %collective-permute-start.4 = (bf16[8,24,384]{2,1,0:T(8,128)(2,1)S(1)}, bf16[8,24,384]{2,1,0:T(8,128)(2,1)S(1)}, u32[]{:S(2)}, u32[]{:S(2)}) collective-permute-start(bf16[8,24,384]{2,1,0:T(8,128)(2,1)S(1)} %pad_maximum_fusion.held_ref), channel_id=1, source_target_pairs={{0,1},{1,0},{2,3},{3,2},{4,5},{5,4},{6,7},{7,6},{8,9},{9,8},{10,11... | collective-permute-start | bytes 442376 | tf_op jit(solution)/shard_map/ppermute | solution.py:145
  17.2 16.7 %copy-start.7 = (bf16[384,6]{0,1:T(8,128)(2,1)S(1)}, bf16[384,6]{0,1:T(8,128)(2,1)}, u32[]{:S(2)}) copy-start(bf16[384,6]{0,1:T(8,128)(2,1)} %param.35) | copy-start | bytes 13828
  17.2 17.9 %copy-start.9 = (s32[384]{0:T(512)S(1)}, s32[384]{0:T(512)}, u32[]{:S(2)}) copy-start(s32[384]{0:T(512)} %live_ref.1) | copy-start | bytes 4612
  17.2 17.9 %copy-start.12 = (bf16[256,256]{1,0:T(8,128)(2,1)S(1)}, bf16[256,256]{1,0:T(8,128)(2,1)}, u32[]{:S(2)}) copy-start(bf16[256,256]{1,0:T(8,128)(2,1)} %middle_ref.1) | copy-start | bytes 393220
  17.2 17.9 %copy-start.13 = (bf16[128,256]{1,0:T(8,128)(2,1)S(1)}, bf16[128,256]{1,0:T(8,128)(2,1)}, u32[]{:S(2)}) copy-start(bf16[128,256]{1,0:T(8,128)(2,1)} %hidden_ref.1) | copy-start | bytes 196612
  17.3 17.9 %copy-start.14 = (bf16[256,128]{1,0:T(8,128)(2,1)S(1)}, bf16[256,128]{1,0:T(8,128)(2,1)}, u32[]{:S(2)}) copy-start(bf16[256,128]{1,0:T(8,128)(2,1)} %back_ref.1) | copy-start | bytes 196612
  17.3 17.9 %copy-start.17 = (f32[128]{0:T(128)S(1)}, f32[128]{0:T(128)}, u32[]{:S(2)}) copy-start(f32[128]{0:T(128)} %param.38) | copy-start | bytes 1540
  21.8 3.6 %collective-permute-start.5 = (bf16[1,24,128]{2,1,0:T(8,128)(2,1)S(1)}, bf16[1,24,128]{2,1,0:T(8,128)(2,1)S(1)}, u32[]{:S(2)}, u32[]{:S(2)}) collective-permute-start(bf16[1,24,128]{2,1,0:T(8,128)(2,1)S(1)} %bitcast.21), channel_id=1, source_target_pairs={{0,2},{1,3},{2,0},{3,1},{4,6},{5,7},{6,4},{7,5},{8,10},{9,11},{10,... | collective-permute-start | bytes 18440 | tf_op jit(solution)/shard_map/ppermute | solution.py:145
  25.5 5.5 %collective-permute-start.6 = (bf16[2,24,128]{2,1,0:T(8,128)(2,1)S(1)}, bf16[2,24,128]{2,1,0:T(8,128)(2,1)S(1)}, u32[]{:S(2)}, u32[]{:S(2)}) collective-permute-start(bf16[2,24,128]{2,1,0:T(8,128)(2,1)S(1)} %pad_maximum_fusion.3), channel_id=1, source_target_pairs={{0,12},{1,13},{2,14},{3,15},{4,8},{5,9},{6,10},{7,11},{8,4},{9,5},... | collective-permute-start | bytes 36872 | tf_op jit(solution)/shard_map/ppermute | solution.py:145
  29.2 4.6 %collective-permute-start.7 = (bf16[2,24,128]{2,1,0:T(8,128)(2,1)S(1)}, bf16[2,24,128]{2,1,0:T(8,128)(2,1)S(1)}, u32[]{:S(2)}, u32[]{:S(2)}) collective-permute-start(bf16[2,24,128]{2,1,0:T(8,128)(2,1)S(1)} %pad_maximum_fusion.3), channel_id=1, source_target_pairs={{0,8},{1,9},{2,10},{3,11},{4,12},{5,13},{6,14},{7,15},{8,0},{9,1},... | collective-permute-start | bytes 36872 | tf_op jit(solution)/shard_map/ppermute | solution.py:145
  29.2 4.6 %collective-permute-start.8 = (bf16[2,24,128]{2,1,0:T(8,128)(2,1)S(1)}, bf16[2,24,128]{2,1,0:T(8,128)(2,1)S(1)}, u32[]{:S(2)}, u32[]{:S(2)}) collective-permute-start(bf16[2,24,128]{2,1,0:T(8,128)(2,1)S(1)} %pad_maximum_fusion.3), channel_id=1, source_target_pairs={{0,4},{1,5},{2,6},{3,7},{4,0},{5,1},{6,2},{7,3},{8,12},{9,13},{10,... | collective-permute-start | bytes 36872 | tf_op jit(solution)/shard_map/ppermute | solution.py:145
  33.8 1.3 %collective-permute-start.9 = (bf16[8,24,128]{2,1,0:T(8,128)(2,1)S(1)}, bf16[8,24,128]{2,1,0:T(8,128)(2,1)S(1)}, u32[]{:S(2)}, u32[]{:S(2)}) collective-permute-start(bf16[8,24,128]{2,1,0:T(8,128)(2,1)S(1)} %pad_maximum_fusion.1.rest_0_), channel_id=1, source_target_pairs={{0,1},{1,0},{2,3},{3,2},{4,5},{5,4},{6,7},{7,6},{8,9},{9,8},{10,11... | collective-permute-start | bytes 147464 | tf_op jit(solution)/shard_map/ppermute | solution.py:145

commit v6 on v5

--- a/solution.py
+++ b/solution.py
@@ -145,12 +145,15 @@
     return lax.ppermute(block, "res", [(k, k ^ step) for k in range(count)])
 
 
-def gather_most(block, count, tied=()):
+def gather_most(block, count, tied=(), own=None):
     held, offsets = block[None], [0]
     quarter = count // 4
     step = quarter // 2
     while step > 1:
-        held = jnp.concatenate([held, exchange(held, count, step)], 0)
+        other = exchange(held, count, step)
+        if own is not None and len(held) == 1:
+            held = own[None]
+        held = jnp.concatenate([held, other], 0)
         offsets = offsets + [o ^ step for o in offsets]
         step //= 2
     held, tied = lax.optimization_barrier((held, tied))
@@ -326,8 +329,8 @@
 
 
 def halves(values):
-    high = values.astype(jnp.bfloat16)
-    return high, (values - high.astype(jnp.float32)).astype(jnp.bfloat16)
+    high = values.astype(jnp.bfloat16).astype(jnp.float32)
+    return jnp.concatenate([high, values - high], 0).astype(jnp.bfloat16)
 
 
 def point_rows(weight_ref, offset, npoints, coord):
@@ -341,13 +344,29 @@
     ]
 
 
-def bias_kernel(weight_ref, pair_ref, out_ref, copy_ref):
-    count = pair_ref.shape[0]
-    first = pl.program_id(0) * count
-    for r in range(count):
-        bias = dot_rows(weight_ref[...], pair_ref[r])
-        out_ref[first + r] = bias.astype(jnp.bfloat16).astype(jnp.float32)
-    copy_ref[pl.ds(first, count)] = pair_ref[...]
+def copy_kernel(source_ref, out_ref):
+    out_ref[...] = source_ref[...]
+
+
+def bias_kernel(source_ref, pair_ref, out_ref, copy_ref, weight_ref, weight_sem, sems):
+    pieces = sems.shape[0]
+    count = pair_ref.shape[0] // pieces
+    copies = [
+        pltpu.make_async_copy(
+            pair_ref.at[pl.ds(k * count, count)], copy_ref.at[pl.ds(k * count, count)], sems.at[k]
+        )
+        for k in range(pieces)
+    ]
+    weight_copy = pltpu.make_async_copy(source_ref, weight_ref, weight_sem)
+    weight_copy.start()
+    for copy in copies:
+        copy.start()
+    weight_copy.wait()
+    for k, copy in enumerate(copies):
+        copy.wait()
+        for r in range(k * count, (k + 1) * count):
+            bias = dot_rows(weight_ref[...], copy_ref[r])
+            out_ref[r] = bias.astype(jnp.bfloat16).astype(jnp.float32)
 
 
 def query_kernel(
@@ -493,7 +512,7 @@
     norm = jnp.sqrt(sum(jnp.square(v) for v in local) + 1.0)
 
     def product(values, rows_of_weight):
-        return dot(jnp.concatenate(halves(values), 0), rows_of_weight)
+        return dot(halves(values), rows_of_weight)
 
     first = HEAD_FEATURES * heads
     update = product(scalar_out, local_ref[pl.ds(0, HEAD_FEATURES)].reshape(first, -1))
@@ -614,24 +633,36 @@
     heads = single_projection_weight.shape[1]
     width = single.shape[1]
     table = stacked_rows(residue_chain_index, residue_move_mask, timestep)
-    offsets, held, table = gather_most(single, total // rows, table)
+    own_rows = pl.pallas_call(
+        copy_kernel,
+        grid=(1,),
+        in_specs=[pl.BlockSpec((rows, width), lambda i: (0, 0))],
+        out_specs=pl.BlockSpec(memory_space=pltpu.VMEM),
+        out_shape=jax.ShapeDtypeStruct(single.shape, single.dtype),
+        compiler_params=pltpu.CompilerParams(vmem_limit_bytes=2 * 1024 * 1024),
+        cost_estimate=pl.CostEstimate(flops=0, bytes_accessed=10**5, transcendentals=0),
+    )(single)
+    offsets, held, table = gather_most(single, total // rows, table, own_rows)
     weight = jnp.transpose(single_projection_weight, (2, 1, 0))
     local_weight = jnp.transpose(local_output_weight, (1, 0, 2))
     distance = head_distance_weight[None]
     depth = heads * (HEAD_FEATURES + 9 * PQ)
-    part = math.gcd(rows, 8)
     bias, pair = pl.pallas_call(
         bias_kernel,
-        grid=(rows // part,),
         in_specs=[
-            pl.BlockSpec((heads, feats), lambda i: (0, 0)),
-            pl.BlockSpec((part, total, feats), lambda i: (i, 0, 0)),
+            pl.BlockSpec(memory_space=pl.ANY),
+            pl.BlockSpec(memory_space=pl.ANY),
         ],
         out_specs=tuple(in_vmem(2)),
         out_shape=(
             jax.ShapeDtypeStruct((rows, heads, total), jnp.float32),
             jax.ShapeDtypeStruct(pair.shape, pair.dtype),
         ),
+        scratch_shapes=[
+            pltpu.VMEM((heads, feats), head_bias_weight.dtype),
+            pltpu.SemaphoreType.DMA,
+            pltpu.SemaphoreType.DMA((math.gcd(rows, 3),)),
+        ],
         compiler_params=pltpu.CompilerParams(vmem_limit_bytes=51200 * 1024),
         cost_estimate=pl.CostEstimate(flops=10**9, bytes_accessed=6 * 10**6, transcendentals=0),
     )(jnp.transpose(head_bias_weight), pair)

time: 42.6 us -> 41.1 us (0.965)
  Pallas kernels: 17.1 us -> 16.3 us
  other arithmetic: 1.55 us -> 0.83 us
  local copies, waits for them, and re-layouts: 1.26 us -> 1.98 us
    pallas_call x1 -> x2, Pallas kernels: 3.29 us -> 2.5 us  [the longest x1 2.49 us: attend(): pl.pallas_call(bias_kernel, in_specs=[pl.BlockSpec(memory_space=pl.ANY),...]
    unnamed x39 -> x41, local copies, waits for them, and re-layouts: 1.25 us -> 1.97 us
    concatenate x2, other arithmetic: 0.74 us -> 0.01 us  [gather_most(): held = jnp.concatenate([held, other], 0)]
  transfers between devices with their start and end apart: 10 -> 10, of which waited for: 5 -> 5; matrix products, arithmetic and copies ran while one was open for 3% -> 3% of each run, Pallas kernels for 13% -> 11%
where the time goes in v6:
time: 41.1 us; the launch traced here: 40.9 us
  Pallas kernels  16.3 us (40%)
  starting transfers between devices  13.7 us (33%)
  waiting for transfers between devices  6.5 us (16%)
  local copies, waits for them, and re-layouts  1.98 us (5%)
  between operations  1.6 us (4%)
  other arithmetic  0.83 us (2%)
    ppermute x10, starting transfers between devices, exchange(): return lax.ppermute(block, 'res', [(k, k ^ step) for k in range(count)])  13.7 us
    pallas_call x1, Pallas kernels, pair_transition(): pl.pallas_call(kernel, grid=(rows_dev // rows_block,), in_specs=[pl.Block...  7.19 us
    ppermute x10, waiting for transfers between devices, exchange(): return lax.ppermute(block, 'res', [(k, k ^ step) for k in range(count)])  6.5 us
    pallas_call x1, Pallas kernels, attend(): pl.pallas_call(functools.partial(attention_kernel, offsets), in_specs=in_...  4.54 us
    pallas_call x1, Pallas kernels, attend(): pl.pallas_call(bias_kernel, in_specs=[pl.BlockSpec(memory_space=pl.ANY),...  2.49 us
    unnamed x41, local copies, waits for them, and re-layouts  1.97 us
    pallas_call x1, Pallas kernels, attend(): pl.pallas_call(query_kernel, in_specs=[pl.BlockSpec(memory_space=pltpu.SM...  1.28 us
  transfers between devices with their start and end apart: 10, of which 5 were waited for; matrix products, arithmetic and copies ran while one was open for 3% of the time, Pallas kernels for 11%

profile of v6, /device:TPU:0, one launch (start us, length us, event | category | flops | bytes accessed | tf_op | source)
XLA Modules:
  0.0 40.9 jit_solution(15525831872271008434)
XLA Ops:
  0.6 3.0 %collective-permute-start = (bf16[1,24,384]{2,1,0:T(8,128)(2,1)}, bf16[1,24,384]{2,1,0:T(8,128)(2,1)S(1)}, u32[]{:S(2)}, u32[]{:S(2)}) collective-permute-start(bf16[1,24,384]{2,1,0:T(8,128)(2,1)} %bitcast.20), channel_id=1, source_target_pairs={{0,2},{1,3},{2,0},{3,1},{4,6},{5,7},{6,4},{7,5},{8,10},{9,11},{10,... | collective-permute-start | bytes 55304 | tf_op jit(solution)/shard_map/ppermute | solution.py:145
  4.3 0.8 %select_select_fusion.rows_ref.live_row_ref = s32[3,384]{1,0:T(4,128)S(1)} fusion(s32[384]{0:T(512)} %chain_ref.1, s32[384]{0:T(512)} %live_ref.1, s32[]{:T(128)} %bitcast.14, pred[3]{0:T(512)(128)(4,1)S(1)} %get-tuple-element.38, pred[3]{0:T(512)(128)(4,1)S(1)} %get-tuple-element.39), kind=kLoop, calls=%fused_computation.5 | loop fusion | flops 2304 | bytes 7690 | tf_op jit(solution)/shard_map/jit(_where)/select_n | solution.py:605
  5.1 0.7 %copy-done.5 = bf16[24,384]{1,0:T(8,128)(2,1)S(1)} copy-done((bf16[24,384]{1,0:T(8,128)(2,1)S(1)}, bf16[24,384]{1,0:T(8,128)(2,1)}, u32[]{:S(2)}) %copy-start.5) | copy-done | bytes 18456
  5.8 4.0 %collective-permute-start.1 = (bf16[2,24,384]{2,1,0:T(8,128)(2,1)S(1)}, bf16[2,24,384]{2,1,0:T(8,128)(2,1)S(1)}, u32[]{:S(2)}, u32[]{:S(2)}) collective-permute-start(bf16[2,24,384]{2,1,0:T(8,128)(2,1)S(1)} %pad_maximum_fusion.2), channel_id=1, source_target_pairs={{0,12},{1,13},{2,14},{3,15},{4,8},{5,9},{6,10},{7,11},{8,4},{9,5},... | collective-permute-start | bytes 110600 | tf_op jit(solution)/shard_map/ppermute | solution.py:145
  9.8 0.6 %collective-permute-start.3 = (bf16[2,24,384]{2,1,0:T(8,128)(2,1)S(1)}, bf16[2,24,384]{2,1,0:T(8,128)(2,1)S(1)}, u32[]{:S(2)}, u32[]{:S(2)}) collective-permute-start(bf16[2,24,384]{2,1,0:T(8,128)(2,1)S(1)} %pad_maximum_fusion.2), channel_id=1, source_target_pairs={{0,4},{1,5},{2,6},{3,7},{4,0},{5,1},{6,2},{7,3},{8,12},{9,13},{10,... | collective-permute-start | bytes 110600 | tf_op jit(solution)/shard_map/ppermute | solution.py:145
  10.4 0.7 %copy-done.16 = bf16[128,16]{0,1:T(8,128)(2,1)S(1)} copy-done((bf16[128,16]{0,1:T(8,128)(2,1)S(1)}, bf16[128,16]{0,1:T(8,128)(2,1)}, u32[]{:S(2)}) %copy-start.16) | copy-done | bytes 4120
  11.1 0.0 copy-start.7
  11.1 0.0 copy-start.9
  11.2 0.0 copy-start.12
  11.2 0.0 copy-start.17
  11.2 2.5 %shard_map.232 = (f32[24,16,384]{2,1,0:T(8,128)S(1)}, bf16[24,384,128]{2,1,0:T(8,128)(2,1)S(1)}) custom-call(bf16[16,128]{1,0:T(8,128)(2,1)S(1)} %bitcast.26, bf16[24,384,128]{2,1,0:T(8,128)(2,1)} %pair_ref.1), custom_call_target="tpu_custom_call" | custom-call | flops 1000000000 | bytes 6000000 | tf_op jit(solution)/shard_map/pallas_call | solution.py:650
  13.7 0.5 %copy.28 = bf16[16,64,384]{2,0,1:T(8,128)(2,1)S(1)} copy(bf16[16,64,384]{2,1,0:T(8,128)(2,1)S(1)} %copy-done.19) | data formatting | bytes 1572864 | tf_op args[11]
  14.2 0.0 copy-start.2
  14.2 0.0 copy-start.3
  14.2 0.4 %collective-permute-done.2 = bf16[2,24,384]{2,1,0:T(8,128)(2,1)S(1)} collective-permute-done((bf16[2,24,384]{2,1,0:T(8,128)(2,1)S(1)}, bf16[2,24,384]{2,1,0:T(8,128)(2,1)S(1)}, u32[]{:S(2)}, u32[]{:S(2)}) %collective-permute-start.2) | collective-permute-done | bytes 36896 | tf_op jit(solution)/shard_map/ppermute | solution.py:145
  14.7 0.1 collective-permute-start.4
  14.8 1.3 %shard_map.233 = (bf16[384,1408]{1,0:T(8,128)(2,1)S(1)}, f32[24,16,384]{2,1,0:T(8,128)S(1)}, f32[24,16]{1,0:T(8,128)S(1)}) custom-call(s32[384]{0:T(512)S(1)} %copy-done.9, f32[24,16,384]{2,1,0:T(8,128)S(1)} %get-tuple-element.25.bias_ref, bf16[24,384]{1,0:T(8,128)(2,1)S(1)} %copy-done.6, bf16[132,16,384]{2,1,0:T(8,128)(2,1)S(1)} %bitcast.16, ...), custom_call_target="tpu_custom_call" | custom-call | flops 1000000000 | bytes 6000000 | tf_op jit(solution)/shard_map/pallas_call | solution.py:671
  16.1 0.0 collective-permute-done.4.other_ref
  16.2 0.0 copy-start.8
  16.2 0.0 copy-start.14
  16.2 0.0 copy-start.15
  16.2 4.5 %shard_map.234 = (bf16[24,384]{1,0:T(8,128)(2,1)}, bf16[24,384]{1,0:T(8,128)(2,1)S(1)}, bf16[24,128]{1,0:T(8,128)(2,1)S(1)}, bf16[24,128]{1,0:T(8,128)(2,1)S(1)}) custom-call(bf16[8,24,384]{2,1,0:T(8,128)(2,1)S(1)} %pad_maximum_fusion.held_ref, bf16[8,24,384]{2,1,0:T(8,128)(2,1)S(1)} %collective-permute-done.4.other_ref, bf16[132,16,384]{2,1,0:T(8,128)(2,1)S(1)} %bitcast.17, ...), custom_call_target="tpu_custom_call" | custom-call | flops 2000000000 | bytes 10000000 | tf_op jit(solution)/shard_map/pallas_call | solution.py:694
  20.8 1.5 %collective-permute-start.5 = (bf16[1,24,128]{2,1,0:T(8,128)(2,1)S(1)}, bf16[1,24,128]{2,1,0:T(8,128)(2,1)S(1)}, u32[]{:S(2)}, u32[]{:S(2)}) collective-permute-start(bf16[1,24,128]{2,1,0:T(8,128)(2,1)S(1)} %bitcast.22), channel_id=1, source_target_pairs={{0,2},{1,3},{2,0},{3,1},{4,6},{5,7},{6,4},{7,5},{8,10},{9,11},{10,... | collective-permute-start | bytes 18440 | tf_op jit(solution)/shard_map/ppermute | solution.py:145
  22.3 2.1 %collective-permute-done.5 = bf16[1,24,128]{2,1,0:T(8,128)(2,1)S(1)} collective-permute-done((bf16[1,24,128]{2,1,0:T(8,128)(2,1)S(1)}, bf16[1,24,128]{2,1,0:T(8,128)(2,1)S(1)}, u32[]{:S(2)}, u32[]{:S(2)}) %collective-permute-start.5) | collective-permute-done | bytes 6176 | tf_op jit(solution)/shard_map/ppermute | solution.py:145
  24.4 3.3 %collective-permute-start.6 = (bf16[2,24,128]{2,1,0:T(8,128)(2,1)S(1)}, bf16[2,24,128]{2,1,0:T(8,128)(2,1)S(1)}, u32[]{:S(2)}, u32[]{:S(2)}) collective-permute-start(bf16[2,24,128]{2,1,0:T(8,128)(2,1)S(1)} %pad_maximum_fusion.3), channel_id=1, source_target_pairs={{0,12},{1,13},{2,14},{3,15},{4,8},{5,9},{6,10},{7,11},{8,4},{9,5},... | collective-permute-start | bytes 36872 | tf_op jit(solution)/shard_map/ppermute | solution.py:145
  27.8 1.1 %collective-permute-start.8 = (bf16[2,24,128]{2,1,0:T(8,128)(2,1)S(1)}, bf16[2,24,128]{2,1,0:T(8,128)(2,1)S(1)}, u32[]{:S(2)}, u32[]{:S(2)}) collective-permute-start(bf16[2,24,128]{2,1,0:T(8,128)(2,1)S(1)} %pad_maximum_fusion.3), channel_id=1, source_target_pairs={{0,4},{1,5},{2,6},{3,7},{4,0},{5,1},{6,2},{7,3},{8,12},{9,13},{10,... | collective-permute-start | bytes 36872 | tf_op jit(solution)/shard_map/ppermute | solution.py:145
  28.8 1.1 %collective-permute-done.6 = bf16[2,24,128]{2,1,0:T(8,128)(2,1)S(1)} collective-permute-done((bf16[2,24,128]{2,1,0:T(8,128)(2,1)S(1)}, bf16[2,24,128]{2,1,0:T(8,128)(2,1)S(1)}, u32[]{:S(2)}, u32[]{:S(2)}) %collective-permute-start.6) | collective-permute-done | bytes 12320 | tf_op jit(solution)/shard_map/ppermute | solution.py:145
  29.9 2.4 %collective-permute-done.7 = bf16[2,24,128]{2,1,0:T(8,128)(2,1)S(1)} collective-permute-done((bf16[2,24,128]{2,1,0:T(8,128)(2,1)S(1)}, bf16[2,24,128]{2,1,0:T(8,128)(2,1)S(1)}, u32[]{:S(2)}, u32[]{:S(2)}) %collective-permute-start.7) | collective-permute-done | bytes 12320 | tf_op jit(solution)/shard_map/ppermute | solution.py:145
  32.4 0.1 collective-permute-start.9
  32.5 0.8 %shard_map.235 = (f32[3,3,24]{2,1,0:T(4,128)}, f32[3,24]{1,0:T(4,128)}) custom-call(s32[3,384]{1,0:T(4,128)S(1)} %select_select_fusion.rows_ref.live_row_ref, bf16[24,384]{1,0:T(8,128)(2,1)S(1)} %get-tuple-element.33.single_ref, bf16[6,384]{1,0:T(8,128)(2,1)S(1)} %bitcast.21, f32[3,3,384]{2,1,0:T(4,128)S(1)} %copy-done.4, f32[3,384]{1,0:T(4,128)S(1)} %copy-done.7), custom_call_target="tpu_custom_call" | custom-call | flops 1000000 | bytes 100000 | tf_op jit(solution)/shard_map/pallas_call | solution.py:730
  33.3 0.4 collective-permute-done.9.rest_1_
  33.7 7.2 %shard_map.236 = bf16[24,384,128]{2,1,0:T(8,128)(2,1)} custom-call(s32[384]{0:T(512)S(1)} %copy-done.10, bf16[24,384,128]{2,1,0:T(8,128)(2,1)S(1)} %get-tuple-element.30.pair_ref, bf16[2,12,128]{2,1,0:T(8,128)(2,1)S(1)} %reshape.20.left_ref, s32[3,384]{1,0:T(4,128)S(1)} %select_select_fusion.rows_ref.live_row_ref, f32[1,128]{1,0:T(1,128)S(1)} %bitcast.28, ...), custom_call_target="tpu_custom_call" | custom-call | flops 3019898880 | bytes 4718592 | tf_op jit(solution)/shard_map/pallas_call | solution.py:272
  (42 shorter events, 0.2 us)
Async XLA Ops:
  0.6 5.2 %collective-permute-start = (bf16[1,24,384]{2,1,0:T(8,128)(2,1)}, bf16[1,24,384]{2,1,0:T(8,128)(2,1)S(1)}, u32[]{:S(2)}, u32[]{:S(2)}) collective-permute-start(bf16[1,24,384]{2,1,0:T(8,128)(2,1)} %bitcast.20), channel_id=1, source_target_pairs={{0,2},{1,3},{2,0},{3,1},{4,6},{5,7},{6,4},{7,5},{8,10},{9,11},{10,... | collective-permute-start | bytes 55304 | tf_op jit(solution)/shard_map/ppermute | solution.py:145
  5.1 0.7 %copy-start.5 = (bf16[24,384]{1,0:T(8,128)(2,1)S(1)}, bf16[24,384]{1,0:T(8,128)(2,1)}, u32[]{:S(2)}) copy-start(bf16[24,384]{1,0:T(8,128)(2,1)} %single_ref.3) | copy-start | bytes 55300
  5.8 8.4 %collective-permute-start.1 = (bf16[2,24,384]{2,1,0:T(8,128)(2,1)S(1)}, bf16[2,24,384]{2,1,0:T(8,128)(2,1)S(1)}, u32[]{:S(2)}, u32[]{:S(2)}) collective-permute-start(bf16[2,24,384]{2,1,0:T(8,128)(2,1)S(1)} %pad_maximum_fusion.2), channel_id=1, source_target_pairs={{0,12},{1,13},{2,14},{3,15},{4,8},{5,9},{6,10},{7,11},{8,4},{9,5},... | collective-permute-start | bytes 110600 | tf_op jit(solution)/shard_map/ppermute | solution.py:145
  9.8 4.9 %collective-permute-start.2 = (bf16[2,24,384]{2,1,0:T(8,128)(2,1)S(1)}, bf16[2,24,384]{2,1,0:T(8,128)(2,1)S(1)}, u32[]{:S(2)}, u32[]{:S(2)}) collective-permute-start(bf16[2,24,384]{2,1,0:T(8,128)(2,1)S(1)} %pad_maximum_fusion.2), channel_id=1, source_target_pairs={{0,8},{1,9},{2,10},{3,11},{4,12},{5,13},{6,14},{7,15},{8,0},{9,1},... | collective-permute-start | bytes 110600 | tf_op jit(solution)/shard_map/ppermute | solution.py:145
  9.8 4.9 %collective-permute-start.3 = (bf16[2,24,384]{2,1,0:T(8,128)(2,1)S(1)}, bf16[2,24,384]{2,1,0:T(8,128)(2,1)S(1)}, u32[]{:S(2)}, u32[]{:S(2)}) collective-permute-start(bf16[2,24,384]{2,1,0:T(8,128)(2,1)S(1)} %pad_maximum_fusion.2), channel_id=1, source_target_pairs={{0,4},{1,5},{2,6},{3,7},{4,0},{5,1},{6,2},{7,3},{8,12},{9,13},{10,... | collective-permute-start | bytes 110600 | tf_op jit(solution)/shard_map/ppermute | solution.py:145
  10.4 0.7 %copy-start.16 = (bf16[128,16]{0,1:T(8,128)(2,1)S(1)}, bf16[128,16]{0,1:T(8,128)(2,1)}, u32[]{:S(2)}) copy-start(bf16[128,16]{0,1:T(8,128)(2,1)} %param.29) | copy-start | bytes 12292
  11.1 2.6 %copy-start.19 = (bf16[16,64,384]{2,1,0:T(8,128)(2,1)S(1)}, bf16[16,64,384]{2,1,0:T(8,128)(2,1)}, u32[]{:S(2)}) copy-start(bf16[16,64,384]{2,1,0:T(8,128)(2,1)} %param.32) | copy-start | bytes 2359300
  11.1 3.6 %copy-start = (bf16[384,16,132]{0,1,2:T(8,128)(2,1)S(1)}, bf16[384,16,132]{0,1,2:T(8,128)(2,1)}, u32[]{:S(2)}) copy-start(bf16[384,16,132]{0,1,2:T(8,128)(2,1)} %param.28) | copy-start | bytes 4866052
  11.1 3.6 %copy-start.4 = (f32[3,3,384]{2,1,0:T(4,128)S(1)}, f32[3,3,384]{2,1,0:T(4,128)}, u32[]{:S(2)}) copy-start(f32[3,3,384]{2,1,0:T(4,128)} %rot_ref.5) | copy-start | bytes 41476
  11.1 3.7 %copy-start.6 = (bf16[24,384]{1,0:T(8,128)(2,1)S(1)}, bf16[24,384]{1,0:T(8,128)(2,1)}, u32[]{:S(2)}) copy-start(bf16[24,384]{1,0:T(8,128)(2,1)} %single_ref.3) | copy-start | bytes 55300
  11.1 3.7 %copy-start.7 = (f32[3,384]{1,0:T(4,128)S(1)}, f32[3,384]{1,0:T(4,128)}, u32[]{:S(2)}) copy-start(f32[3,384]{1,0:T(4,128)} %trans_ref.5) | copy-start | bytes 13828
  11.1 3.7 %copy-start.9 = (s32[384]{0:T(512)S(1)}, s32[384]{0:T(512)}, u32[]{:S(2)}) copy-start(s32[384]{0:T(512)} %chain_ref.1) | copy-start | bytes 4612
  11.2 3.7 %copy-start.12 = (f32[16]{0:T(128)S(1)}, f32[16]{0:T(128)}, u32[]{:S(2)}) copy-start(f32[16]{0:T(128)} %param.30) | copy-start | bytes 196
  11.2 3.7 %copy-start.17 = (f32[16]{0:T(128)S(1)}, f32[16]{0:T(128)}, u32[]{:S(2)}) copy-start(f32[16]{0:T(128)} %param.31) | copy-start | bytes 196
  14.2 2.0 %copy-start.1 = (bf16[16,128,384]{2,1,0:T(8,128)(2,1)S(1)}, bf16[16,128,384]{2,1,0:T(8,128)(2,1)}, u32[]{:S(2)}) copy-start(bf16[16,128,384]{2,1,0:T(8,128)(2,1)} %param.33) | copy-start | bytes 4718596
  14.2 2.0 %copy-start.2 = (bf16[384,128]{1,0:T(8,128)(2,1)S(1)}, bf16[384,128]{1,0:T(8,128)(2,1)}, u32[]{:S(2)}) copy-start(bf16[384,128]{1,0:T(8,128)(2,1)} %left_ref.1) | copy-start | bytes 294916
  14.2 2.0 %copy-start.3 = (bf16[384,128]{1,0:T(8,128)(2,1)S(1)}, bf16[384,128]{1,0:T(8,128)(2,1)}, u32[]{:S(2)}) copy-start(bf16[384,128]{1,0:T(8,128)(2,1)} %right_ref.1) | copy-start | bytes 294916
  14.2 2.0 %copy-start.11 = (f32[384]{0:T(512)S(1)}, f32[384]{0:T(512)}, u32[]{:S(2)}) copy-start(f32[384]{0:T(512)} %gain_ref.1) | copy-start | bytes 4612
  14.7 1.4 %collective-permute-start.4 = (bf16[8,24,384]{2,1,0:T(8,128)(2,1)S(1)}, bf16[8,24,384]{2,1,0:T(8,128)(2,1)S(1)}, u32[]{:S(2)}, u32[]{:S(2)}) collective-permute-start(bf16[8,24,384]{2,1,0:T(8,128)(2,1)S(1)} %pad_maximum_fusion.held_ref), channel_id=1, source_target_pairs={{0,1},{1,0},{2,3},{3,2},{4,5},{5,4},{6,7},{7,6},{8,9},{9,8},{10,11... | collective-permute-start | bytes 442376 | tf_op jit(solution)/shard_map/ppermute | solution.py:145
  16.2 16.3 %copy-start.8 = (bf16[384,6]{0,1:T(8,128)(2,1)S(1)}, bf16[384,6]{0,1:T(8,128)(2,1)}, u32[]{:S(2)}) copy-start(bf16[384,6]{0,1:T(8,128)(2,1)} %param.35) | copy-start | bytes 13828
  16.2 17.5 %copy-start.10 = (s32[384]{0:T(512)S(1)}, s32[384]{0:T(512)}, u32[]{:S(2)}) copy-start(s32[384]{0:T(512)} %live_ref.1) | copy-start | bytes 4612
  16.2 17.5 %copy-start.13 = (bf16[256,256]{1,0:T(8,128)(2,1)S(1)}, bf16[256,256]{1,0:T(8,128)(2,1)}, u32[]{:S(2)}) copy-start(bf16[256,256]{1,0:T(8,128)(2,1)} %middle_ref.1) | copy-start | bytes 393220
  16.2 17.5 %copy-start.14 = (bf16[128,256]{1,0:T(8,128)(2,1)S(1)}, bf16[128,256]{1,0:T(8,128)(2,1)}, u32[]{:S(2)}) copy-start(bf16[128,256]{1,0:T(8,128)(2,1)} %hidden_ref.1) | copy-start | bytes 196612
  16.2 17.5 %copy-start.15 = (bf16[256,128]{1,0:T(8,128)(2,1)S(1)}, bf16[256,128]{1,0:T(8,128)(2,1)}, u32[]{:S(2)}) copy-start(bf16[256,128]{1,0:T(8,128)(2,1)} %back_ref.1) | copy-start | bytes 196612
  16.2 17.5 %copy-start.18 = (f32[128]{0:T(128)S(1)}, f32[128]{0:T(128)}, u32[]{:S(2)}) copy-start(f32[128]{0:T(128)} %param.38) | copy-start | bytes 1540
  20.8 3.6 %collective-permute-start.5 = (bf16[1,24,128]{2,1,0:T(8,128)(2,1)S(1)}, bf16[1,24,128]{2,1,0:T(8,128)(2,1)S(1)}, u32[]{:S(2)}, u32[]{:S(2)}) collective-permute-start(bf16[1,24,128]{2,1,0:T(8,128)(2,1)S(1)} %bitcast.22), channel_id=1, source_target_pairs={{0,2},{1,3},{2,0},{3,1},{4,6},{5,7},{6,4},{7,5},{8,10},{9,11},{10,... | collective-permute-start | bytes 18440 | tf_op jit(solution)/shard_map/ppermute | solution.py:145
  24.4 5.5 %collective-permute-start.6 = (bf16[2,24,128]{2,1,0:T(8,128)(2,1)S(1)}, bf16[2,24,128]{2,1,0:T(8,128)(2,1)S(1)}, u32[]{:S(2)}, u32[]{:S(2)}) collective-permute-start(bf16[2,24,128]{2,1,0:T(8,128)(2,1)S(1)} %pad_maximum_fusion.3), channel_id=1, source_target_pairs={{0,12},{1,13},{2,14},{3,15},{4,8},{5,9},{6,10},{7,11},{8,4},{9,5},... | collective-permute-start | bytes 36872 | tf_op jit(solution)/shard_map/ppermute | solution.py:145
  27.8 4.6 %collective-permute-start.7 = (bf16[2,24,128]{2,1,0:T(8,128)(2,1)S(1)}, bf16[2,24,128]{2,1,0:T(8,128)(2,1)S(1)}, u32[]{:S(2)}, u32[]{:S(2)}) collective-permute-start(bf16[2,24,128]{2,1,0:T(8,128)(2,1)S(1)} %pad_maximum_fusion.3), channel_id=1, source_target_pairs={{0,8},{1,9},{2,10},{3,11},{4,12},{5,13},{6,14},{7,15},{8,0},{9,1},... | collective-permute-start | bytes 36872 | tf_op jit(solution)/shard_map/ppermute | solution.py:145
  27.8 4.6 %collective-permute-start.8 = (bf16[2,24,128]{2,1,0:T(8,128)(2,1)S(1)}, bf16[2,24,128]{2,1,0:T(8,128)(2,1)S(1)}, u32[]{:S(2)}, u32[]{:S(2)}) collective-permute-start(bf16[2,24,128]{2,1,0:T(8,128)(2,1)S(1)} %pad_maximum_fusion.3), channel_id=1, source_target_pairs={{0,4},{1,5},{2,6},{3,7},{4,0},{5,1},{6,2},{7,3},{8,12},{9,13},{10,... | collective-permute-start | bytes 36872 | tf_op jit(solution)/shard_map/ppermute | solution.py:145
  32.4 1.3 %collective-permute-start.9 = (bf16[8,24,128]{2,1,0:T(8,128)(2,1)S(1)}, bf16[8,24,128]{2,1,0:T(8,128)(2,1)S(1)}, u32[]{:S(2)}, u32[]{:S(2)}) collective-permute-start(bf16[8,24,128]{2,1,0:T(8,128)(2,1)S(1)} %pad_maximum_fusion.1.rest_0_), channel_id=1, source_target_pairs={{0,1},{1,0},{2,3},{3,2},{4,5},{5,4},{6,7},{7,6},{8,9},{9,8},{10,11... | collective-permute-start | bytes 147464 | tf_op jit(solution)/shard_map/ppermute | solution.py:145

commit v7 on v6

--- a/solution.py
+++ b/solution.py
@@ -344,11 +344,12 @@
     ]
 
 
-def copy_kernel(source_ref, out_ref):
+def copy_kernel(source_ref, weight_ref, out_ref, weight_out_ref):
     out_ref[...] = source_ref[...]
-
-
-def bias_kernel(source_ref, pair_ref, out_ref, copy_ref, weight_ref, weight_sem, sems):
+    weight_out_ref[...] = weight_ref[...]
+
+
+def bias_kernel(weight_ref, pair_ref, out_ref, copy_ref, sems):
     pieces = sems.shape[0]
     count = pair_ref.shape[0] // pieces
     copies = [
@@ -357,11 +358,8 @@
         )
         for k in range(pieces)
     ]
-    weight_copy = pltpu.make_async_copy(source_ref, weight_ref, weight_sem)
-    weight_copy.start()
     for copy in copies:
         copy.start()
-    weight_copy.wait()
     for k, copy in enumerate(copies):
         copy.wait()
         for r in range(k * count, (k + 1) * count):
@@ -633,24 +631,33 @@
     heads = single_projection_weight.shape[1]
     width = single.shape[1]
     table = stacked_rows(residue_chain_index, residue_move_mask, timestep)
-    own_rows = pl.pallas_call(
+    bias_weight = jnp.transpose(head_bias_weight)
+    own_rows, bias_weight = pl.pallas_call(
         copy_kernel,
         grid=(1,),
-        in_specs=[pl.BlockSpec((rows, width), lambda i: (0, 0))],
-        out_specs=pl.BlockSpec(memory_space=pltpu.VMEM),
-        out_shape=jax.ShapeDtypeStruct(single.shape, single.dtype),
+        in_specs=[
+            pl.BlockSpec((rows, width), lambda i: (0, 0)),
+            pl.BlockSpec((heads, feats), lambda i: (0, 0)),
+        ],
+        out_specs=tuple(in_vmem(2)),
+        out_shape=(
+            jax.ShapeDtypeStruct(single.shape, single.dtype),
+            jax.ShapeDtypeStruct(bias_weight.shape, bias_weight.dtype),
+        ),
         compiler_params=pltpu.CompilerParams(vmem_limit_bytes=2 * 1024 * 1024),
         cost_estimate=pl.CostEstimate(flops=0, bytes_accessed=10**5, transcendentals=0),
-    )(single)
-    offsets, held, table = gather_most(single, total // rows, table, own_rows)
+    )(single, bias_weight)
+    offsets, held, (table, bias_weight, local_output_weight) = gather_most(
+        single, total // rows, (table, bias_weight, local_output_weight), own_rows
+    )
     weight = jnp.transpose(single_projection_weight, (2, 1, 0))
-    local_weight = jnp.transpose(local_output_weight, (1, 0, 2))
     distance = head_distance_weight[None]
     depth = heads * (HEAD_FEATURES + 9 * PQ)
+    local_weight = jnp.transpose(local_output_weight, (1, 0, 2))
     bias, pair = pl.pallas_call(
         bias_kernel,
         in_specs=[
-            pl.BlockSpec(memory_space=pl.ANY),
+            pl.BlockSpec(memory_space=pltpu.VMEM),
             pl.BlockSpec(memory_space=pl.ANY),
         ],
         out_specs=tuple(in_vmem(2)),
@@ -658,14 +665,10 @@
             jax.ShapeDtypeStruct((rows, heads, total), jnp.float32),
             jax.ShapeDtypeStruct(pair.shape, pair.dtype),
         ),
-        scratch_shapes=[
-            pltpu.VMEM((heads, feats), head_bias_weight.dtype),
-            pltpu.SemaphoreType.DMA,
-            pltpu.SemaphoreType.DMA((math.gcd(rows, 3),)),
-        ],
+        scratch_shapes=[pltpu.SemaphoreType.DMA((math.gcd(rows, 3),))],
         compiler_params=pltpu.CompilerParams(vmem_limit_bytes=51200 * 1024),
         cost_estimate=pl.CostEstimate(flops=10**9, bytes_accessed=6 * 10**6, transcendentals=0),
-    )(jnp.transpose(head_bias_weight), pair)
+    )(bias_weight, pair)
     held, bias, pair, local_weight = lax.optimization_barrier((held, bias, pair, local_weight))
     other = exchange(held, total // rows, 1)
     query, base, frame = pl.pallas_call(

time: 41.1 us -> 40.7 us (level)
  starting transfers between devices: 13.7 us -> 13.1 us
    ppermute x10, starting transfers between devices: 13.7 us -> 13.1 us  [exchange(): return lax.ppermute(block, 'res', [(k, k ^ step) for k in range(count)])]
    optimization_barrier x0 -> x1, local copies, waits for them, and re-layouts: none -> 0.46 us  [gather_most(): held, tied = lax.optimization_barrier((held, tied))]
    unnamed x41 -> x40, local copies, waits for them, and re-layouts: 1.97 us -> 1.52 us
where the time goes in v7:
time: 40.7 us; the launch traced here: 40.4 us
  Pallas kernels  16.2 us (40%)
  starting transfers between devices  13.1 us (32%)
  waiting for transfers between devices  6.73 us (17%)
  local copies, waits for them, and re-layouts  1.99 us (5%)
  between operations  1.63 us (4%)
  other arithmetic  0.83 us (2%)
    ppermute x10, starting transfers between devices, exchange(): return lax.ppermute(block, 'res', [(k, k ^ step) for k in range(count)])  13.1 us
    pallas_call x1, Pallas kernels, pair_transition(): pl.pallas_call(kernel, grid=(rows_dev // rows_block,), in_specs=[pl.Block...  7.19 us
    ppermute x10, waiting for transfers between devices, exchange(): return lax.ppermute(block, 'res', [(k, k ^ step) for k in range(count)])  6.73 us
    pallas_call x1, Pallas kernels, attend(): pl.pallas_call(functools.partial(attention_kernel, offsets), in_specs=in_...  4.54 us
    pallas_call x1, Pallas kernels, attend(): pl.pallas_call(bias_kernel, in_specs=[pl.BlockSpec(memory_space=pltpu.VME...  2.33 us
    unnamed x40, local copies, waits for them, and re-layouts  1.52 us
    pallas_call x1, Pallas kernels, attend(): pl.pallas_call(query_kernel, in_specs=[pl.BlockSpec(memory_space=pltpu.SM...  1.28 us
    pallas_call x1, Pallas kernels, attend(): pl.pallas_call(frame_kernel, in_specs=in_vmem(5), out_specs=tuple(in_vmem...  0.82 us
  transfers between devices with their start and end apart: 10, of which 5 were waited for; matrix products, arithmetic and copies ran while one was open for 3% of the time, Pallas kernels for 11%

profile of v7, /device:TPU:0, one launch (start us, length us, event | category | flops | bytes accessed | tf_op | source)
XLA Modules:
  0.0 40.4 jit_solution(7503785638297317386)
XLA Ops:
  0.6 3.0 %collective-permute-start = (bf16[1,24,384]{2,1,0:T(8,128)(2,1)}, bf16[1,24,384]{2,1,0:T(8,128)(2,1)S(1)}, u32[]{:S(2)}, u32[]{:S(2)}) collective-permute-start(bf16[1,24,384]{2,1,0:T(8,128)(2,1)} %bitcast.19), channel_id=1, source_target_pairs={{0,2},{1,3},{2,0},{3,1},{4,6},{5,7},{6,4},{7,5},{8,10},{9,11},{10,... | collective-permute-start | bytes 55304 | tf_op jit(solution)/shard_map/ppermute | solution.py:145
  4.3 0.8 %select_select_fusion.rows_ref.live_row_ref = s32[3,384]{1,0:T(4,128)S(1)} fusion(s32[384]{0:T(512)} %chain_ref.1, s32[384]{0:T(512)} %live_ref.1, s32[]{:T(128)} %bitcast.14, pred[3]{0:T(512)(128)(4,1)S(1)} %get-tuple-element.46, pred[3]{0:T(512)(128)(4,1)S(1)} %get-tuple-element.47), kind=kLoop, calls=%fused_computation.5 | loop fusion | flops 2304 | bytes 7690 | tf_op jit(solution)/shard_map/jit(_where)/select_n | solution.py:603
  5.1 0.7 %copy-done.5 = bf16[24,384]{1,0:T(8,128)(2,1)S(1)} copy-done((bf16[24,384]{1,0:T(8,128)(2,1)S(1)}, bf16[24,384]{1,0:T(8,128)(2,1)}, u32[]{:S(2)}) %copy-start.5) | copy-done | bytes 18456
  5.8 0.7 %copy-done.9 = bf16[128,16]{0,1:T(8,128)(2,1)S(1)} copy-done((bf16[128,16]{0,1:T(8,128)(2,1)S(1)}, bf16[128,16]{0,1:T(8,128)(2,1)}, u32[]{:S(2)}) %copy-start.9) | copy-done | bytes 4120
  6.5 0.0 copy-start
  6.5 0.0 copy-start.4
  6.5 0.0 copy-start.7
  6.6 0.0 copy-start.10
  6.6 3.7 %collective-permute-start.1 = (bf16[2,24,384]{2,1,0:T(8,128)(2,1)S(1)}, bf16[2,24,384]{2,1,0:T(8,128)(2,1)S(1)}, u32[]{:S(2)}, u32[]{:S(2)}) collective-permute-start(bf16[2,24,384]{2,1,0:T(8,128)(2,1)S(1)} %pad_maximum_fusion.2), channel_id=1, source_target_pairs={{0,12},{1,13},{2,14},{3,15},{4,8},{5,9},{6,10},{7,11},{8,4},{9,5},... | collective-permute-start | bytes 110600 | tf_op jit(solution)/shard_map/ppermute | solution.py:145
  10.3 0.8 %collective-permute-start.3 = (bf16[2,24,384]{2,1,0:T(8,128)(2,1)S(1)}, bf16[2,24,384]{2,1,0:T(8,128)(2,1)S(1)}, u32[]{:S(2)}, u32[]{:S(2)}) collective-permute-start(bf16[2,24,384]{2,1,0:T(8,128)(2,1)S(1)} %pad_maximum_fusion.2), channel_id=1, source_target_pairs={{0,4},{1,5},{2,6},{3,7},{4,0},{5,1},{6,2},{7,3},{8,12},{9,13},{10,... | collective-permute-start | bytes 110600 | tf_op jit(solution)/shard_map/ppermute | solution.py:145
  11.0 2.3 %shard_map.232 = (f32[24,16,384]{2,1,0:T(8,128)S(1)}, bf16[24,384,128]{2,1,0:T(8,128)(2,1)S(1)}) custom-call(bf16[16,128]{1,0:T(8,128)(2,1)S(1)} %get-tuple-element.28.weight_ref, bf16[24,384,128]{2,1,0:T(8,128)(2,1)} %pair_ref.1), custom_call_target="tpu_custom_call" | custom-call | flops 1000000000 | bytes 6000000 | tf_op jit(solution)/shard_map/pallas_call | solution.py:657
  13.4 0.5 %copy.28 = bf16[16,64,384]{2,0,1:T(8,128)(2,1)S(1)} copy(bf16[16,64,384]{2,1,0:T(8,128)(2,1)S(1)} %copy-done.19) | data formatting | bytes 1572864 | tf_op jit(solution)/shard_map/optimization_barrier | solution.py:159
  13.9 0.0 copy-start.3
  13.9 0.0 copy-start.12
  13.9 1.2 %collective-permute-done.2 = bf16[2,24,384]{2,1,0:T(8,128)(2,1)S(1)} collective-permute-done((bf16[2,24,384]{2,1,0:T(8,128)(2,1)S(1)}, bf16[2,24,384]{2,1,0:T(8,128)(2,1)S(1)}, u32[]{:S(2)}, u32[]{:S(2)}) %collective-permute-start.2) | collective-permute-done | bytes 36896 | tf_op jit(solution)/shard_map/ppermute | solution.py:145
  15.1 0.1 collective-permute-start.4
  15.3 1.3 %shard_map.233 = (bf16[384,1408]{1,0:T(8,128)(2,1)S(1)}, f32[24,16,384]{2,1,0:T(8,128)S(1)}, f32[24,16]{1,0:T(8,128)S(1)}) custom-call(s32[384]{0:T(512)S(1)} %copy-done.10, f32[24,16,384]{2,1,0:T(8,128)S(1)} %get-tuple-element.33.bias_ref, bf16[24,384]{1,0:T(8,128)(2,1)S(1)} %copy-done.6, bf16[132,16,384]{2,1,0:T(8,128)(2,1)S(1)} %bitcast.16, ...), custom_call_target="tpu_custom_call" | custom-call | flops 1000000000 | bytes 6000000 | tf_op jit(solution)/shard_map/pallas_call | solution.py:674
  16.6 0.0 collective-permute-done.4.other_ref
  16.6 0.0 copy-start.11
  16.7 0.0 copy-start.14
  16.7 0.0 copy-start.18
  16.7 4.5 %shard_map.234 = (bf16[24,384]{1,0:T(8,128)(2,1)}, bf16[24,384]{1,0:T(8,128)(2,1)S(1)}, bf16[24,128]{1,0:T(8,128)(2,1)S(1)}, bf16[24,128]{1,0:T(8,128)(2,1)S(1)}) custom-call(bf16[8,24,384]{2,1,0:T(8,128)(2,1)S(1)} %pad_maximum_fusion.held_ref, bf16[8,24,384]{2,1,0:T(8,128)(2,1)S(1)} %collective-permute-done.4.other_ref, bf16[132,16,384]{2,1,0:T(8,128)(2,1)S(1)} %bitcast.17, ...), custom_call_target="tpu_custom_call" | custom-call | flops 2000000000 | bytes 10000000 | tf_op jit(solution)/shard_map/pallas_call | solution.py:697
  21.2 1.1 %collective-permute-start.5 = (bf16[1,24,128]{2,1,0:T(8,128)(2,1)S(1)}, bf16[1,24,128]{2,1,0:T(8,128)(2,1)S(1)}, u32[]{:S(2)}, u32[]{:S(2)}) collective-permute-start(bf16[1,24,128]{2,1,0:T(8,128)(2,1)S(1)} %bitcast.22), channel_id=1, source_target_pairs={{0,2},{1,3},{2,0},{3,1},{4,6},{5,7},{6,4},{7,5},{8,10},{9,11},{10,... | collective-permute-start | bytes 18440 | tf_op jit(solution)/shard_map/ppermute | solution.py:145
  22.4 2.5 %collective-permute-done.5 = bf16[1,24,128]{2,1,0:T(8,128)(2,1)S(1)} collective-permute-done((bf16[1,24,128]{2,1,0:T(8,128)(2,1)S(1)}, bf16[1,24,128]{2,1,0:T(8,128)(2,1)S(1)}, u32[]{:S(2)}, u32[]{:S(2)}) %collective-permute-start.5) | collective-permute-done | bytes 6176 | tf_op jit(solution)/shard_map/ppermute | solution.py:145
  24.9 2.4 %collective-permute-start.6 = (bf16[2,24,128]{2,1,0:T(8,128)(2,1)S(1)}, bf16[2,24,128]{2,1,0:T(8,128)(2,1)S(1)}, u32[]{:S(2)}, u32[]{:S(2)}) collective-permute-start(bf16[2,24,128]{2,1,0:T(8,128)(2,1)S(1)} %pad_maximum_fusion.3), channel_id=1, source_target_pairs={{0,12},{1,13},{2,14},{3,15},{4,8},{5,9},{6,10},{7,11},{8,4},{9,5},... | collective-permute-start | bytes 36872 | tf_op jit(solution)/shard_map/ppermute | solution.py:145
  27.3 2.0 %collective-permute-start.8 = (bf16[2,24,128]{2,1,0:T(8,128)(2,1)S(1)}, bf16[2,24,128]{2,1,0:T(8,128)(2,1)S(1)}, u32[]{:S(2)}, u32[]{:S(2)}) collective-permute-start(bf16[2,24,128]{2,1,0:T(8,128)(2,1)S(1)} %pad_maximum_fusion.3), channel_id=1, source_target_pairs={{0,4},{1,5},{2,6},{3,7},{4,0},{5,1},{6,2},{7,3},{8,12},{9,13},{10,... | collective-permute-start | bytes 36872 | tf_op jit(solution)/shard_map/ppermute | solution.py:145
  29.3 1.1 %collective-permute-done.6 = bf16[2,24,128]{2,1,0:T(8,128)(2,1)S(1)} collective-permute-done((bf16[2,24,128]{2,1,0:T(8,128)(2,1)S(1)}, bf16[2,24,128]{2,1,0:T(8,128)(2,1)S(1)}, u32[]{:S(2)}, u32[]{:S(2)}) %collective-permute-start.6) | collective-permute-done | bytes 12320 | tf_op jit(solution)/shard_map/ppermute | solution.py:145
  30.4 1.5 %collective-permute-done.7 = bf16[2,24,128]{2,1,0:T(8,128)(2,1)S(1)} collective-permute-done((bf16[2,24,128]{2,1,0:T(8,128)(2,1)S(1)}, bf16[2,24,128]{2,1,0:T(8,128)(2,1)S(1)}, u32[]{:S(2)}, u32[]{:S(2)}) %collective-permute-start.7) | collective-permute-done | bytes 12320 | tf_op jit(solution)/shard_map/ppermute | solution.py:145
  31.9 0.1 collective-permute-start.9
  32.0 0.8 %shard_map.235 = (f32[3,3,24]{2,1,0:T(4,128)}, f32[3,24]{1,0:T(4,128)}) custom-call(s32[3,384]{1,0:T(4,128)S(1)} %select_select_fusion.rows_ref.live_row_ref, bf16[24,384]{1,0:T(8,128)(2,1)S(1)} %get-tuple-element.41.single_ref, bf16[6,384]{1,0:T(8,128)(2,1)S(1)} %bitcast.21, f32[3,3,384]{2,1,0:T(4,128)S(1)} %copy-done.4, f32[3,384]{1,0:T(4,128)S(1)} %copy-done.7), custom_call_target="tpu_custom_call" | custom-call | flops 1000000 | bytes 100000 | tf_op jit(solution)/shard_map/pallas_call | solution.py:733
  32.8 0.4 collective-permute-done.9.rest_1_
  33.2 7.2 %shard_map.236 = bf16[24,384,128]{2,1,0:T(8,128)(2,1)} custom-call(s32[384]{0:T(512)S(1)} %copy-done.11, bf16[24,384,128]{2,1,0:T(8,128)(2,1)S(1)} %get-tuple-element.38.pair_ref, bf16[2,12,128]{2,1,0:T(8,128)(2,1)S(1)} %reshape.20.left_ref, s32[3,384]{1,0:T(4,128)S(1)} %select_select_fusion.rows_ref.live_row_ref, f32[1,128]{1,0:T(1,128)S(1)} %bitcast.28, ...), custom_call_target="tpu_custom_call" | custom-call | flops 3019898880 | bytes 4718592 | tf_op jit(solution)/shard_map/pallas_call | solution.py:272
  (42 shorter events, 0.2 us)
Async XLA Ops:
  0.6 5.9 %collective-permute-start = (bf16[1,24,384]{2,1,0:T(8,128)(2,1)}, bf16[1,24,384]{2,1,0:T(8,128)(2,1)S(1)}, u32[]{:S(2)}, u32[]{:S(2)}) collective-permute-start(bf16[1,24,384]{2,1,0:T(8,128)(2,1)} %bitcast.19), channel_id=1, source_target_pairs={{0,2},{1,3},{2,0},{3,1},{4,6},{5,7},{6,4},{7,5},{8,10},{9,11},{10,... | collective-permute-start | bytes 55304 | tf_op jit(solution)/shard_map/ppermute | solution.py:145
  5.1 0.7 %copy-start.5 = (bf16[24,384]{1,0:T(8,128)(2,1)S(1)}, bf16[24,384]{1,0:T(8,128)(2,1)}, u32[]{:S(2)}) copy-start(bf16[24,384]{1,0:T(8,128)(2,1)} %single_ref.3) | copy-start | bytes 55300
  5.8 0.7 %copy-start.9 = (bf16[128,16]{0,1:T(8,128)(2,1)S(1)}, bf16[128,16]{0,1:T(8,128)(2,1)}, u32[]{:S(2)}) copy-start(bf16[128,16]{0,1:T(8,128)(2,1)} %param.29) | copy-start | bytes 12292
  6.5 6.9 %copy-start.19 = (bf16[16,64,384]{2,1,0:T(8,128)(2,1)S(1)}, bf16[16,64,384]{2,1,0:T(8,128)(2,1)}, u32[]{:S(2)}) copy-start(bf16[16,64,384]{2,1,0:T(8,128)(2,1)} %param.32) | copy-start | bytes 2359300
  6.5 8.7 %copy-start = (bf16[384,16,132]{0,1,2:T(8,128)(2,1)S(1)}, bf16[384,16,132]{0,1,2:T(8,128)(2,1)}, u32[]{:S(2)}) copy-start(bf16[384,16,132]{0,1,2:T(8,128)(2,1)} %param.28) | copy-start | bytes 4866052
  6.5 8.7 %copy-start.4 = (f32[3,3,384]{2,1,0:T(4,128)S(1)}, f32[3,3,384]{2,1,0:T(4,128)}, u32[]{:S(2)}) copy-start(f32[3,3,384]{2,1,0:T(4,128)} %rot_ref.5) | copy-start | bytes 41476
  6.5 8.7 %copy-start.6 = (bf16[24,384]{1,0:T(8,128)(2,1)S(1)}, bf16[24,384]{1,0:T(8,128)(2,1)}, u32[]{:S(2)}) copy-start(bf16[24,384]{1,0:T(8,128)(2,1)} %single_ref.3) | copy-start | bytes 55300
  6.5 8.7 %copy-start.7 = (f32[3,384]{1,0:T(4,128)S(1)}, f32[3,384]{1,0:T(4,128)}, u32[]{:S(2)}) copy-start(f32[3,384]{1,0:T(4,128)} %trans_ref.5) | copy-start | bytes 13828
  6.6 8.7 %copy-start.10 = (s32[384]{0:T(512)S(1)}, s32[384]{0:T(512)}, u32[]{:S(2)}) copy-start(s32[384]{0:T(512)} %chain_ref.1) | copy-start | bytes 4612
  6.6 8.7 %copy-start.13 = (f32[16]{0:T(128)S(1)}, f32[16]{0:T(128)}, u32[]{:S(2)}) copy-start(f32[16]{0:T(128)} %param.30) | copy-start | bytes 196
  6.6 8.7 %copy-start.17 = (f32[16]{0:T(128)S(1)}, f32[16]{0:T(128)}, u32[]{:S(2)}) copy-start(f32[16]{0:T(128)} %param.31) | copy-start | bytes 196
  6.6 7.3 %collective-permute-start.1 = (bf16[2,24,384]{2,1,0:T(8,128)(2,1)S(1)}, bf16[2,24,384]{2,1,0:T(8,128)(2,1)S(1)}, u32[]{:S(2)}, u32[]{:S(2)}) collective-permute-start(bf16[2,24,384]{2,1,0:T(8,128)(2,1)S(1)} %pad_maximum_fusion.2), channel_id=1, source_target_pairs={{0,12},{1,13},{2,14},{3,15},{4,8},{5,9},{6,10},{7,11},{8,4},{9,5},... | collective-permute-start | bytes 110600 | tf_op jit(solution)/shard_map/ppermute | solution.py:145
  10.3 4.9 %collective-permute-start.2 = (bf16[2,24,384]{2,1,0:T(8,128)(2,1)S(1)}, bf16[2,24,384]{2,1,0:T(8,128)(2,1)S(1)}, u32[]{:S(2)}, u32[]{:S(2)}) collective-permute-start(bf16[2,24,384]{2,1,0:T(8,128)(2,1)S(1)} %pad_maximum_fusion.2), channel_id=1, source_target_pairs={{0,8},{1,9},{2,10},{3,11},{4,12},{5,13},{6,14},{7,15},{8,0},{9,1},... | collective-permute-start | bytes 110600 | tf_op jit(solution)/shard_map/ppermute | solution.py:145
  10.3 4.9 %collective-permute-start.3 = (bf16[2,24,384]{2,1,0:T(8,128)(2,1)S(1)}, bf16[2,24,384]{2,1,0:T(8,128)(2,1)S(1)}, u32[]{:S(2)}, u32[]{:S(2)}) collective-permute-start(bf16[2,24,384]{2,1,0:T(8,128)(2,1)S(1)} %pad_maximum_fusion.2), channel_id=1, source_target_pairs={{0,4},{1,5},{2,6},{3,7},{4,0},{5,1},{6,2},{7,3},{8,12},{9,13},{10,... | collective-permute-start | bytes 110600 | tf_op jit(solution)/shard_map/ppermute | solution.py:145
  13.9 2.7 %copy-start.1 = (bf16[16,128,384]{2,1,0:T(8,128)(2,1)S(1)}, bf16[16,128,384]{2,1,0:T(8,128)(2,1)}, u32[]{:S(2)}) copy-start(bf16[16,128,384]{2,1,0:T(8,128)(2,1)} %param.33) | copy-start | bytes 4718596
  13.9 2.7 %copy-start.2 = (bf16[384,128]{1,0:T(8,128)(2,1)S(1)}, bf16[384,128]{1,0:T(8,128)(2,1)}, u32[]{:S(2)}) copy-start(bf16[384,128]{1,0:T(8,128)(2,1)} %left_ref.1) | copy-start | bytes 294916
  13.9 2.7 %copy-start.3 = (bf16[384,128]{1,0:T(8,128)(2,1)S(1)}, bf16[384,128]{1,0:T(8,128)(2,1)}, u32[]{:S(2)}) copy-start(bf16[384,128]{1,0:T(8,128)(2,1)} %right_ref.1) | copy-start | bytes 294916
  13.9 2.7 %copy-start.12 = (f32[384]{0:T(512)S(1)}, f32[384]{0:T(512)}, u32[]{:S(2)}) copy-start(f32[384]{0:T(512)} %gain_ref.1) | copy-start | bytes 4612
  15.1 1.4 %collective-permute-start.4 = (bf16[8,24,384]{2,1,0:T(8,128)(2,1)S(1)}, bf16[8,24,384]{2,1,0:T(8,128)(2,1)S(1)}, u32[]{:S(2)}, u32[]{:S(2)}) collective-permute-start(bf16[8,24,384]{2,1,0:T(8,128)(2,1)S(1)} %pad_maximum_fusion.held_ref), channel_id=1, source_target_pairs={{0,1},{1,0},{2,3},{3,2},{4,5},{5,4},{6,7},{7,6},{8,9},{9,8},{10,11... | collective-permute-start | bytes 442376 | tf_op jit(solution)/shard_map/ppermute | solution.py:145
  16.6 15.4 %copy-start.8 = (bf16[384,6]{0,1:T(8,128)(2,1)S(1)}, bf16[384,6]{0,1:T(8,128)(2,1)}, u32[]{:S(2)}) copy-start(bf16[384,6]{0,1:T(8,128)(2,1)} %param.35) | copy-start | bytes 13828
  16.6 16.6 %copy-start.11 = (s32[384]{0:T(512)S(1)}, s32[384]{0:T(512)}, u32[]{:S(2)}) copy-start(s32[384]{0:T(512)} %live_ref.1) | copy-start | bytes 4612
  16.7 16.6 %copy-start.14 = (bf16[256,256]{1,0:T(8,128)(2,1)S(1)}, bf16[256,256]{1,0:T(8,128)(2,1)}, u32[]{:S(2)}) copy-start(bf16[256,256]{1,0:T(8,128)(2,1)} %middle_ref.1) | copy-start | bytes 393220
  16.7 16.5 %copy-start.15 = (bf16[128,256]{1,0:T(8,128)(2,1)S(1)}, bf16[128,256]{1,0:T(8,128)(2,1)}, u32[]{:S(2)}) copy-start(bf16[128,256]{1,0:T(8,128)(2,1)} %hidden_ref.1) | copy-start | bytes 196612
  16.7 16.5 %copy-start.16 = (bf16[256,128]{1,0:T(8,128)(2,1)S(1)}, bf16[256,128]{1,0:T(8,128)(2,1)}, u32[]{:S(2)}) copy-start(bf16[256,128]{1,0:T(8,128)(2,1)} %back_ref.1) | copy-start | bytes 196612
  16.7 16.5 %copy-start.18 = (f32[128]{0:T(128)S(1)}, f32[128]{0:T(128)}, u32[]{:S(2)}) copy-start(f32[128]{0:T(128)} %param.38) | copy-start | bytes 1540
  21.2 3.6 %collective-permute-start.5 = (bf16[1,24,128]{2,1,0:T(8,128)(2,1)S(1)}, bf16[1,24,128]{2,1,0:T(8,128)(2,1)S(1)}, u32[]{:S(2)}, u32[]{:S(2)}) collective-permute-start(bf16[1,24,128]{2,1,0:T(8,128)(2,1)S(1)} %bitcast.22), channel_id=1, source_target_pairs={{0,2},{1,3},{2,0},{3,1},{4,6},{5,7},{6,4},{7,5},{8,10},{9,11},{10,... | collective-permute-start | bytes 18440 | tf_op jit(solution)/shard_map/ppermute | solution.py:145
  24.9 5.5 %collective-permute-start.6 = (bf16[2,24,128]{2,1,0:T(8,128)(2,1)S(1)}, bf16[2,24,128]{2,1,0:T(8,128)(2,1)S(1)}, u32[]{:S(2)}, u32[]{:S(2)}) collective-permute-start(bf16[2,24,128]{2,1,0:T(8,128)(2,1)S(1)} %pad_maximum_fusion.3), channel_id=1, source_target_pairs={{0,12},{1,13},{2,14},{3,15},{4,8},{5,9},{6,10},{7,11},{8,4},{9,5},... | collective-permute-start | bytes 36872 | tf_op jit(solution)/shard_map/ppermute | solution.py:145
  27.3 4.6 %collective-permute-start.7 = (bf16[2,24,128]{2,1,0:T(8,128)(2,1)S(1)}, bf16[2,24,128]{2,1,0:T(8,128)(2,1)S(1)}, u32[]{:S(2)}, u32[]{:S(2)}) collective-permute-start(bf16[2,24,128]{2,1,0:T(8,128)(2,1)S(1)} %pad_maximum_fusion.3), channel_id=1, source_target_pairs={{0,8},{1,9},{2,10},{3,11},{4,12},{5,13},{6,14},{7,15},{8,0},{9,1},... | collective-permute-start | bytes 36872 | tf_op jit(solution)/shard_map/ppermute | solution.py:145
  27.3 4.6 %collective-permute-start.8 = (bf16[2,24,128]{2,1,0:T(8,128)(2,1)S(1)}, bf16[2,24,128]{2,1,0:T(8,128)(2,1)S(1)}, u32[]{:S(2)}, u32[]{:S(2)}) collective-permute-start(bf16[2,24,128]{2,1,0:T(8,128)(2,1)S(1)} %pad_maximum_fusion.3), channel_id=1, source_target_pairs={{0,4},{1,5},{2,6},{3,7},{4,0},{5,1},{6,2},{7,3},{8,12},{9,13},{10,... | collective-permute-start | bytes 36872 | tf_op jit(solution)/shard_map/ppermute | solution.py:145
  31.9 1.3 %collective-permute-start.9 = (bf16[8,24,128]{2,1,0:T(8,128)(2,1)S(1)}, bf16[8,24,128]{2,1,0:T(8,128)(2,1)S(1)}, u32[]{:S(2)}, u32[]{:S(2)}) collective-permute-start(bf16[8,24,128]{2,1,0:T(8,128)(2,1)S(1)} %pad_maximum_fusion.1.rest_0_), channel_id=1, source_target_pairs={{0,1},{1,0},{2,3},{3,2},{4,5},{5,4},{6,7},{7,6},{8,9},{9,8},{10,11... | collective-permute-start | bytes 147464 | tf_op jit(solution)/shard_map/ppermute | solution.py:145
